TPU v7x, 256 devices: a whole 4x4x8 slice. The times are simulated.
256 devices in a mesh: tok: 4 (over x), feat: 64 (over y, z, core).
Axes of the slice: x: 4, y: 4, z: 8, core: 2. Of those that a mesh axis runs over, the one named last changes fastest.
Arguments:
- activations: bfloat16 [32768, 28672], P('tok', 'feat'), may hold values from -6 to 6
- labels: int32 [8, 32768], P(None, 'tok'), may hold values 0 or 1
- probe_weights: bfloat16 [8, 28672], P(None, 'feat'), may hold values from -0.25 to 0.25
- direction: bfloat16 [8, 28672], P(None, 'feat'), may hold values from -0.25 to 0.25
- group_ids: int32 [28672], P('feat'), may hold values from 0 to 63, never falling along the last dimension, each value on 1 to 896 neighbouring positions
Outputs:
- gradient: float32 [8, 28672], P(None, 'feat')
- hess_vec: float32 [8, 28672], P(None, 'feat')
Inputs may be any that keep to these rules, and one draw needn't show every extreme that they name: `group_ids`: group numbers never fall along the neurons; every group holds 1 to 896 neurons in a row, some group exactly that many.
All inputs are finite; a program needn't handle non-finite values. No bound on the sum of `labels` on one device may be relied on, other than what follows from the above.
Results may differ from a plain program's by a relative error of at most 0.0022.
Values may be sent and summed in bfloat16 or wider, within the bound.
No kernel may reach another device: no remote copies, remote signals or barrier semaphores. Data moves between devices by JAX's collectives and lax.ppermute only.
A program may use at most 64 MiB of HBM per device.

v0:
```python
import math

import jax
import jax.numpy as jnp
from jax import lax
from jax.sharding import PartitionSpec as P

GROUPS = 64


DELTA = 0.05
LAMBDA_WEIGHT = 8.0


def residuals(margins, targets, probes):
    logits = margins[:probes]
    slopes = margins[probes:]
    likely = jax.nn.sigmoid(logits)
    return jnp.concatenate(
        [likely - targets.astype(jnp.float32), likely * (1.0 - likely) * slopes], 0
    ).astype(jnp.bfloat16)


def local(activations, labels, probe_weights, direction, group_ids):
    probes = probe_weights.shape[0]
    stacked = jnp.concatenate([probe_weights, direction], 0)
    partial_value = lax.dot_general(
        stacked, activations, (((1,), (1,)), ((), ())), preferred_element_type=jnp.float32
    )
    wide_weights = probe_weights.astype(jnp.float32)
    wide_direction = direction.astype(jnp.float32)
    member = (group_ids[None, :] == jnp.arange(GROUPS, dtype=jnp.int32)[:, None]).astype(
        jnp.float32
    )
    products = jnp.concatenate([wide_weights * wide_weights, wide_weights * wide_direction], 0)
    local_stats = lax.dot_general(
        products,
        member,
        (((1,), (1,)), ((), ())),
        precision=lax.Precision.HIGHEST,
        preferred_element_type=jnp.float32,
    )
    totals = lax.psum(local_stats, "feat")
    margins = lax.psum(partial_value, "feat")
    weighted = residuals(margins, labels, probes)
    local_fit = jnp.dot(weighted, activations, preferred_element_type=jnp.float32)
    fitted = lax.psum(local_fit, "tok")
    tokens_all = activations.shape[0] * lax.axis_size("tok")
    fitted = fitted / math.sqrt(tokens_all)
    group_norm = jnp.sqrt(totals[:probes] + DELTA * DELTA)
    spread = jnp.dot(
        jnp.concatenate([group_norm, totals[probes:]], 0),
        member,
        precision=lax.Precision.HIGHEST,
        preferred_element_type=jnp.float32,
    )
    scale = spread[:probes]
    cross = spread[probes:]
    gradient = fitted[:probes] + LAMBDA_WEIGHT * wide_weights / scale
    hess_vec = fitted[probes:] + LAMBDA_WEIGHT * (
        wide_direction / scale - wide_weights * cross / (scale * scale * scale)
    )
    return (gradient, hess_vec)


def solution(mesh):
    return jax.shard_map(
        local,
        mesh=mesh,
        in_specs=(P("tok", "feat"), P(None, "tok"), P(None, "feat"), P(None, "feat"), P("feat")),
        out_specs=(P(None, "feat"), P(None, "feat")),
        check_vma=False,
    )
```

profile of v0, /device:TPU:6, one launch (start us, length us, event | category | flops | bytes accessed | tf_op | source)
XLA Modules:
  0.0 224.4 jit_solution(12276585543046059213)
XLA Ops:
  7.2 0.0 copy-start.1
  7.2 0.0 copy-start.2
  7.2 0.0 copy-start.3
  7.2 0.0 copy-start
  7.2 0.0 all-reduce.2.cloned.1.call-start
  7.3 5.0 %fusion.22 = f32[16,8192]{1,0:T(8,128)} fusion(bf16[8192,448]{0,1:T(8,128)(2,1)} %param.5, bf16[8,448]{1,0:T(8,128)(2,1)} %param.8, bf16[8,448]{1,0:T(8,128)(2,1)} %param.7), kind=kOutput, calls=%fused_computation.32 | convolution fusion | flops 117469184 | bytes 7878656 | tf_op jit(solution)/shard_map/dot_general | solution.py:27
  12.3 0.0 all-reduce.2.cloned.1.call-update
  12.3 0.0 copy-done.1
  12.3 0.0 copy-done.2
  12.3 0.0 copy-done.3
  12.3 0.1 fusion.10
  12.5 133.9 %psum.23 = f32[16,64]{1,0:T(8,128)S(1)} all-reduce(f32[16,64]{1,0:T(8,128)S(1)} %fusion.10), channel_id=1, replica_groups=mesh['tok'=4,'feat'=64] {'feat'}, use_global_device_ids=true, to_apply=%region_2.0 | all-reduce | flops 1024 | bytes 8192 | tf_op jit(solution)/shard_map/psum | solution.py:43
  146.4 0.2 fusion.9
  146.6 50.0 %all-reduce.2.cloned.1.call-done = f32[16,8192]{1,0:T(8,128)} async-done(((f32[16,8192]{1,0:T(8,128)}), f32[16,8192]{1,0:T(8,128)}) %all-reduce.2.cloned.1.call-update) | async-done | bytes 524304 | tf_op jit(solution)/shard_map/psum | solution.py:44
  196.6 0.0 copy-done
  196.6 1.1 subtract_convert_fusion
  197.7 5.1 %fusion.5 = f32[16,448]{1,0:T(8,128)S(1)} fusion(bf16[8192,448]{0,1:T(8,128)(2,1)} %param.5, bf16[8,8192]{1,0:T(8,128)(2,1)S(1)} %get-tuple-element.3, bf16[8,8192]{1,0:T(8,128)(2,1)S(1)} %get-tuple-element.2), kind=kOutput, calls=%fused_computation.7 | convolution fusion | flops 117964800 | bytes 7630848 | tf_op jit(solution)/shard_map/dot_general | solution.py:46
  202.8 14.1 %psum.22 = f32[16,448]{1,0:T(8,128)S(1)} all-reduce(f32[16,448]{1,0:T(8,128)S(1)} %fusion.5), channel_id=1, replica_groups=mesh['tok'=4,'feat'=64] {'tok'}, use_global_device_ids=true, to_apply=%region_1.0 | all-reduce | flops 7168 | bytes 57344 | tf_op jit(solution)/shard_map/psum | solution.py:47
  216.9 0.6 fusion.18
  (3 shorter events, 0.0 us)
Async XLA Ops:
  7.2 5.1 %copy-start.1 = (bf16[8,448]{1,0:T(8,128)(2,1)S(1)}, bf16[8,448]{1,0:T(8,128)(2,1)}, u32[]{:S(2)}) copy-start(bf16[8,448]{1,0:T(8,128)(2,1)} %param.8) | copy-start | bytes 21508
  7.2 5.1 %copy-start.2 = (bf16[8,448]{1,0:T(8,128)(2,1)S(1)}, bf16[8,448]{1,0:T(8,128)(2,1)}, u32[]{:S(2)}) copy-start(bf16[8,448]{1,0:T(8,128)(2,1)} %param.7) | copy-start | bytes 21508
  7.2 5.1 %copy-start.3 = (s32[448]{0:T(512)S(1)}, s32[448]{0:T(512)}, u32[]{:S(2)}) copy-start(s32[448]{0:T(512)} %param.9) | copy-start | bytes 5380
  7.2 189.4 %copy-start = (s32[8,8192]{1,0:T(8,128)S(1)}, s32[8,8192]{1,0:T(8,128)}, u32[]{:S(2)}) copy-start(s32[8,8192]{1,0:T(8,128)} %param.6) | copy-start | bytes 786436
  7.2 189.4 %all-reduce.2.cloned.1.call-start = ((), (), s32[]{:S(2)}) async-start(), calls=%async_computation | async-start | bytes 1048576 | tf_op jit(solution)/shard_map/psum | solution.py:44
Sparse Core Ops, SparseCore 0:
  12.4 184.1 all-reduce.1
where the time goes:
time: 227 us; the launch traced here: 224 us
  blocking collectives  148 us (65%)
  waiting for transfers between devices  50 us (22%)
  between operations  14.1 us (6%)
  matrix products  10.4 us (5%)
    psum x1, blocking collectives, local(): totals = lax.psum(local_stats, 'feat')  134 us
    psum x1, waiting for transfers between devices, local(): margins = lax.psum(partial_value, 'feat')  50 us
    psum x1, blocking collectives, local(): fitted = lax.psum(local_fit, 'tok')  14.1 us
    dot_general x1, matrix products, local(): jnp.dot(weighted, activations, preferred_element_type=jnp.float32)  5.08 us
    dot_general x1, matrix products, local(): lax.dot_general(stacked, activations, (((1,), (1,)), ((), ())), preferred...  5.02 us
  transfers between devices with their start and end apart: 1, of which 1 were waited for; matrix products, arithmetic and copies ran while one was open for 0% of the time, Pallas kernels for 0%

commit v1 on v0

--- a/solution.py
+++ b/solution.py
@@ -12,17 +12,18 @@
 LAMBDA_WEIGHT = 8.0
 
 
-def residuals(margins, targets, probes):
-    logits = margins[:probes]
-    slopes = margins[probes:]
-    likely = jax.nn.sigmoid(logits)
-    return jnp.concatenate(
-        [likely - targets.astype(jnp.float32), likely * (1.0 - likely) * slopes], 0
-    ).astype(jnp.bfloat16)
-
-
 def local(activations, labels, probe_weights, direction, group_ids):
     probes = probe_weights.shape[0]
+    rows = 2 * probes
+    tokens = activations.shape[0]
+    planes = lax.axis_size("tok")
+    devices = lax.axis_size("feat")
+    chips = devices // 2
+    share = tokens // chips
+    chip = lax.axis_index("feat") // 2
+    by_core = [[2 * i + core for i in range(chips)] for core in range(2)]
+    swap = [(i, i ^ 1) for i in range(devices)]
+
     stacked = jnp.concatenate([probe_weights, direction], 0)
     partial_value = lax.dot_general(
         stacked, activations, (((1,), (1,)), ((), ())), preferred_element_type=jnp.float32
@@ -40,13 +41,39 @@
         precision=lax.Precision.HIGHEST,
         preferred_element_type=jnp.float32,
     )
-    totals = lax.psum(local_stats, "feat")
-    margins = lax.psum(partial_value, "feat")
-    weighted = residuals(margins, labels, probes)
-    local_fit = jnp.dot(weighted, activations, preferred_element_type=jnp.float32)
-    fitted = lax.psum(local_fit, "tok")
-    tokens_all = activations.shape[0] * lax.axis_size("tok")
-    fitted = fitted / math.sqrt(tokens_all)
+    high = lax.reduce_precision(local_stats, 8, 7)
+    split_stats = jnp.concatenate([high, local_stats - high], 1).astype(jnp.bfloat16)
+
+    outgoing = jnp.concatenate(
+        [
+            partial_value.reshape(rows, chips, share).transpose(1, 0, 2).astype(jnp.bfloat16),
+            jnp.broadcast_to(split_stats[None], (chips, rows, 2 * GROUPS)),
+        ],
+        2,
+    )
+    arrived = lax.all_to_all(outgoing, "feat", 0, 0, axis_index_groups=by_core)
+    summed = arrived.astype(jnp.float32).sum(0)
+    summed = summed + lax.ppermute(summed, "feat", swap)
+    margins = summed[:, :share]
+    totals = summed[:, share : share + GROUPS] + summed[:, share + GROUPS :]
+
+    targets = lax.dynamic_slice_in_dim(labels, chip * share, share, 1)
+    likely = jax.nn.sigmoid(margins[:probes])
+    weighted = jnp.concatenate(
+        [likely - targets.astype(jnp.float32), likely * (1.0 - likely) * margins[probes:]], 0
+    ).astype(jnp.bfloat16)
+    copies = jnp.broadcast_to(weighted[None], (chips, rows, share))
+    gathered = lax.all_to_all(copies, "feat", 0, 0, axis_index_groups=by_core)
+    weighted_all = gathered.transpose(1, 0, 2).reshape(rows, tokens)
+
+    local_fit = jnp.dot(weighted_all, activations, preferred_element_type=jnp.float32)
+    one, two, three = (
+        lax.ppermute(local_fit, "tok", [(i, (i + hop) % planes) for i in range(planes)])
+        for hop in (1, 2, 3)
+    )
+    fitted = (local_fit + two) + (one + three)
+    fitted = fitted / math.sqrt(tokens * planes)
+
     group_norm = jnp.sqrt(totals[:probes] + DELTA * DELTA)
     spread = jnp.dot(
         jnp.concatenate([group_norm, totals[probes:]], 0),

time: 227 us -> 67 us (0.30)
  blocking collectives: 148 us -> 25.8 us
  waiting for transfers between devices: 50 us -> 17.7 us
  between operations: 14.1 us -> 0.76 us
  starting transfers between devices: 0.04 us -> 8.66 us
    psum x2 -> x0, blocking collectives: 148 us -> none  [the longest x1 134 us: local(): totals = lax.psum(local_stats, 'feat')]
    psum x1 -> x0, waiting for transfers between devices: 50 us -> none  [local(): margins = lax.psum(partial_value, 'feat')]
    all_to_all x0 -> x1, blocking collectives: none -> 25.8 us  [local(): arrived = lax.all_to_all(outgoing, 'feat', 0, 0, axis_index_groups=by_core)]
    all_to_all x0 -> x1, waiting for transfers between devices: none -> 12.7 us  [local(): gathered = lax.all_to_all(copies, 'feat', 0, 0, axis_index_groups=by_core)]
    all_to_all x0 -> x1, starting transfers between devices: none -> 5.13 us  [local(): gathered = lax.all_to_all(copies, 'feat', 0, 0, axis_index_groups=by_core)]
    ppermute x0 -> x4, waiting for transfers between devices: none -> 5.02 us  [the longest x3 3.86 us: local(): lax.ppermute(local_fit, 'tok', [(i, (i + hop) % planes) for i in range(pl...]
    ppermute x0 -> x4, starting transfers between devices: none -> 3.53 us  [the longest x3 3.45 us: local(): lax.ppermute(local_fit, 'tok', [(i, (i + hop) % planes) for i in range(pl...]
  transfers between devices with their start and end apart: 1 -> 5, of which waited for: 1 -> 5; matrix products, arithmetic and copies ran while one was open for 0% -> 0% of each run, Pallas kernels for 0% -> 0%
where the time goes in v1:
time: 67 us; the launch traced here: 65.7 us
  blocking collectives  25.8 us (39%)
  waiting for transfers between devices  17.7 us (26%)
  matrix products  9.56 us (14%)
  starting transfers between devices  8.66 us (13%)
  other arithmetic  2.38 us (4%)
  local copies, waits for them, and re-layouts  0.8 us (1%)
  between operations  0.76 us (1%)
    all_to_all x1, blocking collectives, local(): arrived = lax.all_to_all(outgoing, 'feat', 0, 0, axis_index_groups=by_core)  25.8 us
    all_to_all x1, waiting for transfers between devices, local(): gathered = lax.all_to_all(copies, 'feat', 0, 0, axis_index_groups=by_core)  12.7 us
    all_to_all x1, starting transfers between devices, local(): gathered = lax.all_to_all(copies, 'feat', 0, 0, axis_index_groups=by_core)  5.13 us
    dot_general x1, matrix products, local(): jnp.dot(weighted_all, activations, preferred_element_type=jnp.float32)  5.08 us
    dot_general x1, matrix products, local(): lax.dot_general(stacked, activations, (((1,), (1,)), ((), ())), preferred...  4.18 us
    ppermute x3, waiting for transfers between devices, local(): lax.ppermute(local_fit, 'tok', [(i, (i + hop) % planes) for i in range(pl...  3.86 us
    ppermute x3, starting transfers between devices, local(): lax.ppermute(local_fit, 'tok', [(i, (i + hop) % planes) for i in range(pl...  3.45 us
  transfers between devices with their start and end apart: 5, of which 5 were waited for; matrix products, arithmetic and copies ran while one was open for 0% of the time, Pallas kernels for 0%

profile of v1, /device:TPU:6, one launch (start us, length us, event | category | flops | bytes accessed | tf_op | source)
XLA Modules:
  0.0 65.7 jit_solution(7947644379079709568)
XLA Ops:
  0.6 0.0 copy-start.2
  0.6 0.7 %convert_multiply_fusion.3 = (f32[8,448]{1,0:T(8,128)S(1)}, f32[8,448]{1,0:T(8,128)S(1)}) fusion(bf16[8,448]{1,0:T(8,128)(2,1)} %param.7, bf16[8,448]{1,0:T(8,128)(2,1)} %param.8), kind=kLoop, calls=%fused_computation.16 | loop fusion | flops 14336 | bytes 43008 | tf_op jit(solution)/shard_map/mul | solution.py:36
  1.4 4.2 %convolution_convert_fusion = bf16[16,8192]{1,0:T(8,128)(2,1)S(1)} fusion(bf16[8192,448]{0,1:T(8,128)(2,1)} %param.5, bf16[8,448]{1,0:T(8,128)(2,1)} %param.8, bf16[8,448]{1,0:T(8,128)(2,1)} %param.7), kind=kOutput, calls=%fused_computation | convolution fusion | flops 117600256 | bytes 7616512 | tf_op jit(solution)/shard_map/dot_general | solution.py:28
  5.5 0.0 copy-start
  5.5 0.0 copy-start.1
  5.6 0.0 copy-done.2
  5.6 0.1 reduce-precision_convert_fusion
  5.7 0.1 pad_maximum_fusion.2
  5.9 25.8 %all_to_all.10 = bf16[32,16,384]{2,1,0:T(8,128)(2,1)S(1)} all-to-all(bf16[32,16,384]{2,1,0:T(8,128)(2,1)S(1)} %pad_maximum_fusion), channel_id=1, replica_groups={{0,2,4,6,8,10,12,14,16,18,20,22,24,26,28,30,32,34,36,38,40,42,44,46,48,..., dimensions={0} | all-to-all | bytes 786432 | tf_op jit(solution)/shard_map/all_to_all | solution.py:54
  31.7 0.1 convert_reduce_fusion
  31.8 0.1 collective-permute-start
  31.9 1.2 %collective-permute-done = f32[16,384]{1,0:T(8,128)S(1)} collective-permute-done((f32[16,384]{1,0:T(8,128)S(1)}, f32[16,384]{1,0:T(8,128)S(1)}, u32[]{:S(2)}, u32[]{:S(2)}) %collective-permute-start) | collective-permute-done | bytes 24608 | tf_op jit(solution)/shard_map/ppermute | solution.py:56
  33.1 0.7 %subtract_convert_fusion = (bf16[8,256]{1,0:T(8,128)(2,1)S(1)}, bf16[8,256]{1,0:T(8,128)(2,1)S(1)}) fusion(s32[8,8192]{1,0:T(8,128)} %param.6, s32[]{:T(128)S(6)} %select_n.9, f32[16,384]{1,0:T(8,128)S(1)} %add.34), kind=kLoop, calls=%fused_computation.43 | loop fusion | flops 20480 | bytes 32772 | tf_op jit(solution)/shard_map/convert
  33.8 0.7 %broadcast_in_dim.5 = bf16[32,16,256]{2,1,0:T(8,128)(2,1)} broadcast(bf16[16,256]{1,0:T(8,128)(2,1)S(1)} %pad_maximum_fusion.1), dimensions={1,2} | broadcast | bytes 270336 | tf_op jit(solution)/shard_map/broadcast_in_dim | solution.py:65
  34.5 5.1 %all-to-all-start.1 = ((bf16[32,16,256]{2,1,0:T(8,128)(2,1)}), bf16[32,16,256]{2,1,0:T(8,128)(2,1)S(1)}, u32[]{:S(2)}, u32[]{:S(2)}) async-start(bf16[32,16,256]{2,1,0:T(8,128)(2,1)} %broadcast_in_dim.5), calls=%async_computation.1 | async-start | bytes 524288 | tf_op jit(solution)/shard_map/all_to_all | solution.py:66
  39.7 0.1 slice_add_fusion
  39.8 12.7 %all-to-all-done.1 = bf16[32,16,256]{2,1,0:T(8,128)(2,1)S(1)} async-done(((bf16[32,16,256]{2,1,0:T(8,128)(2,1)}), bf16[32,16,256]{2,1,0:T(8,128)(2,1)S(1)}, u32[]{:S(2)}, u32[]{:S(2)}) %all-to-all-start.1) | async-done | bytes 262176 | tf_op jit(solution)/shard_map/all_to_all | solution.py:66
  52.5 5.1 %fusion.29 = f32[16,448]{1,0:T(8,128)S(1)} fusion(bf16[16,8192]{1,0:T(8,128)(2,1)S(1)} %bitcast.16, bf16[8192,448]{0,1:T(8,128)(2,1)} %param.5), kind=kOutput, calls=%fused_computation.50 | convolution fusion | flops 117440512 | bytes 7630848 | tf_op jit(solution)/shard_map/dot_general | solution.py:69
  57.5 0.5 collective-permute-start.2
  58.0 1.5 %collective-permute-start.3 = (f32[16,448]{1,0:T(8,128)S(1)}, f32[16,448]{1,0:T(8,128)S(1)}, u32[]{:S(2)}, u32[]{:S(2)}) collective-permute-start(f32[16,448]{1,0:T(8,128)S(1)} %fusion.29), channel_id=1, source_target_pairs={{0,192},{64,0},{128,64},{192,128},{1,193},{65,1},{129,65},{193,129... | collective-permute-start | bytes 86024 | tf_op jit(solution)/shard_map/ppermute | solution.py:71
  59.6 1.4 %collective-permute-start.1 = (f32[16,448]{1,0:T(8,128)S(1)}, f32[16,448]{1,0:T(8,128)S(1)}, u32[]{:S(2)}, u32[]{:S(2)}) collective-permute-start(f32[16,448]{1,0:T(8,128)S(1)} %fusion.29), channel_id=1, source_target_pairs={{0,128},{64,192},{128,0},{192,64},{1,129},{65,193},{129,1},{193,65... | collective-permute-start | bytes 86024 | tf_op jit(solution)/shard_map/ppermute | solution.py:71
  61.0 0.2 fusion
  61.1 0.3 collective-permute-done.2
  61.5 1.7 %collective-permute-done.3 = f32[16,448]{1,0:T(8,128)S(1)} collective-permute-done((f32[16,448]{1,0:T(8,128)S(1)}, f32[16,448]{1,0:T(8,128)S(1)}, u32[]{:S(2)}, u32[]{:S(2)}) %collective-permute-start.3) | collective-permute-done | bytes 28704 | tf_op jit(solution)/shard_map/ppermute | solution.py:71
  63.2 1.8 %collective-permute-done.1 = f32[16,448]{1,0:T(8,128)S(1)} collective-permute-done((f32[16,448]{1,0:T(8,128)S(1)}, f32[16,448]{1,0:T(8,128)S(1)}, u32[]{:S(2)}, u32[]{:S(2)}) %collective-permute-start.1) | collective-permute-done | bytes 28704 | tf_op jit(solution)/shard_map/ppermute | solution.py:71
  65.0 0.0 copy-done
  65.0 0.0 copy-done.1
  65.0 0.6 fusion.9
  (8 shorter events, 0.1 us)
Async XLA Ops:
  0.6 5.0 %copy-start.2 = (s32[448]{0:T(512)S(1)}, s32[448]{0:T(512)}, u32[]{:S(2)}) copy-start(s32[448]{0:T(512)} %param.9) | copy-start | bytes 5380
  5.5 59.5 %copy-start = (bf16[8,448]{1,0:T(8,128)(2,1)S(1)}, bf16[8,448]{1,0:T(8,128)(2,1)}, u32[]{:S(2)}) copy-start(bf16[8,448]{1,0:T(8,128)(2,1)} %param.8) | copy-start | bytes 21508
  5.5 59.5 %copy-start.1 = (bf16[8,448]{1,0:T(8,128)(2,1)S(1)}, bf16[8,448]{1,0:T(8,128)(2,1)}, u32[]{:S(2)}) copy-start(bf16[8,448]{1,0:T(8,128)(2,1)} %param.7) | copy-start | bytes 21508
  31.8 1.3 %collective-permute-start = (f32[16,384]{1,0:T(8,128)S(1)}, f32[16,384]{1,0:T(8,128)S(1)}, u32[]{:S(2)}, u32[]{:S(2)}) collective-permute-start(f32[16,384]{1,0:T(8,128)S(1)} %convert_reduce_fusion), channel_id=1, source_target_pairs={{0,1},{1,0},{2,3},{3,2},{4,5},{5,4},{6,7},{7,6},{8,9},{9,8},{10,11... | collective-permute-start | bytes 73736 | tf_op jit(solution)/shard_map/ppermute | solution.py:56
  34.5 17.9 %all-to-all-start.1 = ((bf16[32,16,256]{2,1,0:T(8,128)(2,1)}), bf16[32,16,256]{2,1,0:T(8,128)(2,1)S(1)}, u32[]{:S(2)}, u32[]{:S(2)}) async-start(bf16[32,16,256]{2,1,0:T(8,128)(2,1)} %broadcast_in_dim.5), calls=%async_computation.1 | async-start | bytes 524288 | tf_op jit(solution)/shard_map/all_to_all | solution.py:66
  57.5 3.9 %collective-permute-start.2 = (f32[16,448]{1,0:T(8,128)S(1)}, f32[16,448]{1,0:T(8,128)S(1)}, u32[]{:S(2)}, u32[]{:S(2)}) collective-permute-start(f32[16,448]{1,0:T(8,128)S(1)} %fusion.29), channel_id=1, source_target_pairs={{0,64},{64,128},{128,192},{192,0},{1,65},{65,129},{129,193},{193,1... | collective-permute-start | bytes 86024 | tf_op jit(solution)/shard_map/ppermute | solution.py:71
  58.0 5.1 %collective-permute-start.3 = (f32[16,448]{1,0:T(8,128)S(1)}, f32[16,448]{1,0:T(8,128)S(1)}, u32[]{:S(2)}, u32[]{:S(2)}) collective-permute-start(f32[16,448]{1,0:T(8,128)S(1)} %fusion.29), channel_id=1, source_target_pairs={{0,192},{64,0},{128,64},{192,128},{1,193},{65,1},{129,65},{193,129... | collective-permute-start | bytes 86024 | tf_op jit(solution)/shard_map/ppermute | solution.py:71
  59.6 5.4 %collective-permute-start.1 = (f32[16,448]{1,0:T(8,128)S(1)}, f32[16,448]{1,0:T(8,128)S(1)}, u32[]{:S(2)}, u32[]{:S(2)}) collective-permute-start(f32[16,448]{1,0:T(8,128)S(1)} %fusion.29), channel_id=1, source_target_pairs={{0,128},{64,192},{128,0},{192,64},{1,129},{65,193},{129,1},{193,65... | collective-permute-start | bytes 86024 | tf_op jit(solution)/shard_map/ppermute | solution.py:71

commit v2 on v0

v2 whole, which is shorter than its diff:
```python
import math

import jax
import jax.numpy as jnp
from jax import lax
from jax.experimental import pallas as pl
from jax.experimental.pallas import tpu as pltpu
from jax.sharding import PartitionSpec as P

GROUPS = 64


DELTA = 0.05
LAMBDA_WEIGHT = 8.0

LANES = 128
PIECES = 4


def transposed_dot(left, right, precision=None):
    return lax.dot_general(
        left,
        right,
        (((1,), (1,)), ((), ())),
        precision=precision,
        preferred_element_type=jnp.float32,
    )


def margins_kernel(
    w_ref, d_ref, g_ref, labels_ref, a_ref,
    mine, theirs, stats_mine, stats_theirs, targets,
    a_mine, a_theirs, labels_sem, a_sems,
):
    me = lax.axis_index("feat")
    core, chip = lax.rem(me, 2), lax.div(me, 2)
    half = a_mine.shape[1]
    piece = half // PIECES
    copies = []
    for side, held in ((1 - core, a_theirs), (core, a_mine)):
        for i in range(PIECES):
            start = pl.multiple_of(side * half + i * piece, LANES)
            copy = pltpu.make_async_copy(
                a_ref.at[:, pl.ds(start, piece)],
                held.at[:, pl.ds(i * piece, piece)],
                a_sems.at[len(copies)],
            )
            copy.start()
            copies.append(copy)
    share = targets.shape[1]
    spot = pl.multiple_of(core * half + chip * share, LANES)
    labels_copy = pltpu.make_async_copy(labels_ref.at[:, pl.ds(spot, share)], targets, labels_sem)
    labels_copy.start()

    wide_weights = w_ref[...].astype(jnp.float32)
    wide_direction = d_ref[...].astype(jnp.float32)
    number = lax.broadcasted_iota(jnp.int32, (GROUPS, g_ref.shape[1]), 0)
    member = (number == g_ref[...]).astype(jnp.float32)
    squares = transposed_dot(wide_weights * wide_weights, member, lax.Precision.HIGHEST)
    crosses = transposed_dot(wide_weights * wide_direction, member, lax.Precision.HIGHEST)
    stats_mine[...] = jnp.where(core == 0, squares, crosses)
    stats_theirs[...] = jnp.where(core == 0, crosses, squares)

    stacked = jnp.concatenate([w_ref[...], d_ref[...]], 0)
    per_piece = piece // LANES
    for n, copy in enumerate(copies):
        copy.wait()
        held, out = (a_theirs, theirs) if n < PIECES else (a_mine, mine)
        i = n % PIECES
        product = jnp.dot(
            stacked, held[:, i * piece : (i + 1) * piece], preferred_element_type=jnp.float32
        )
        for k in range(per_piece):
            out[i * per_piece + k] = product[:, k * LANES : (k + 1) * LANES]
    labels_copy.wait()


def weighted_kernel(arrived, targets, copies, totals):
    rows = copies.shape[1]
    probes = rows // 2
    summed = jnp.sum(arrived[...].astype(jnp.float32), 0)
    logits, slopes, split_stats = summed[:probes], summed[probes:rows], summed[rows:]
    likely = 1.0 / (1.0 + jnp.exp(-logits))
    weighted = jnp.concatenate(
        [likely - targets[...].astype(jnp.float32), likely * (1.0 - likely) * slopes], 0
    ).astype(jnp.bfloat16)
    copies[...] = jnp.broadcast_to(weighted[None], copies.shape)
    totals[...] = split_stats[:, :GROUPS] + split_stats[:, GROUPS:]


def flatten(weighted, flat):
    for k in range(weighted.shape[0]):
        flat[:, k * LANES : (k + 1) * LANES] = weighted[k]


def fit_mine_kernel(weighted, a_ref, out, a_theirs, flat, a_mine, sems):
    core = lax.rem(lax.axis_index("feat"), 2)
    half = a_mine.shape[1]
    piece = half // PIECES
    copies = []
    for side, held in ((core, a_mine), (1 - core, a_theirs)):
        for i in range(PIECES):
            start = pl.multiple_of(side * half + i * piece, LANES)
            copy = pltpu.make_async_copy(
                a_ref.at[:, pl.ds(start, piece)],
                held.at[:, pl.ds(i * piece, piece)],
                sems.at[len(copies)],
            )
            copy.start()
            copies.append(copy)
    flatten(weighted, flat)
    total = jnp.zeros(out.shape, jnp.float32)
    for i in range(PIECES):
        copies[i].wait()
        at = slice(i * piece, (i + 1) * piece)
        total = total + transposed_dot(flat[:, at], a_mine[:, at])
    out[...] = total
    for copy in copies[PIECES:]:
        copy.wait()


def fit_theirs_kernel(weighted, a_theirs, base, out, flat):
    flatten(weighted, flat)
    out[...] = base[...] + transposed_dot(flat[...], a_theirs[...])


def local(activations, labels, probe_weights, direction, group_ids):
    probes, width = probe_weights.shape
    rows = 2 * probes
    tokens = activations.shape[0]
    half = tokens // 2
    planes = lax.axis_size("tok")
    devices = lax.axis_size("feat")
    chips = devices // 2
    share = half // chips
    core = lax.rem(lax.axis_index("feat"), 2)
    by_core = [[2 * i + side for i in range(chips)] for side in range(2)]
    swap = [(i, i ^ 1) for i in range(devices)]
    f32, bf16 = jnp.float32, jnp.bfloat16
    vmem, hbm = pl.BlockSpec(memory_space=pltpu.VMEM), pl.BlockSpec(memory_space=pltpu.HBM)

    by_neuron = pltpu.with_memory_space_constraint(activations.T, pltpu.HBM)
    mine, theirs, stats_mine, stats_theirs, targets = pl.pallas_call(
        margins_kernel,
        out_shape=[
            jax.ShapeDtypeStruct((chips, rows, share), f32),
            jax.ShapeDtypeStruct((chips, rows, share), f32),
            jax.ShapeDtypeStruct((probes, GROUPS), f32),
            jax.ShapeDtypeStruct((probes, GROUPS), f32),
            jax.ShapeDtypeStruct((probes, share), jnp.int32),
        ],
        in_specs=[vmem, vmem, vmem, hbm, hbm],
        out_specs=[vmem] * 5,
        scratch_shapes=[
            pltpu.VMEM((width, half), bf16),
            pltpu.VMEM((width, half), bf16),
            pltpu.SemaphoreType.DMA,
            pltpu.SemaphoreType.DMA((2 * PIECES,)),
        ],
        compiler_params=pltpu.CompilerParams(vmem_limit_bytes=24 << 20),
        name="margins",
    )(probe_weights, direction, group_ids[None, :], pltpu.with_memory_space_constraint(labels, pltpu.HBM), by_neuron)

    stats = stats_mine + lax.ppermute(stats_theirs, "feat", swap)
    high = lax.reduce_precision(stats, 8, 7)
    split_stats = jnp.concatenate([high, stats - high], 1).astype(bf16)
    pair_sum = (mine + lax.ppermute(theirs, "feat", swap)).astype(bf16)
    outgoing = jnp.concatenate(
        [pair_sum, jnp.broadcast_to(split_stats[None], (chips, probes, 2 * GROUPS))], 1
    )
    arrived = lax.all_to_all(outgoing, "feat", 0, 0, axis_index_groups=by_core)
    copies, totals_mine = pl.pallas_call(
        weighted_kernel,
        out_shape=[
            jax.ShapeDtypeStruct((chips, rows, share), bf16),
            jax.ShapeDtypeStruct((probes, GROUPS), f32),
        ],
        in_specs=[vmem] * 2,
        out_specs=[vmem] * 2,
        compiler_params=pltpu.CompilerParams(vmem_limit_bytes=4 << 20),
        name="weighted",
    )(arrived, targets)
    weighted_mine = lax.all_to_all(copies, "feat", 0, 0, axis_index_groups=by_core)
    weighted_theirs = lax.ppermute(weighted_mine, "feat", swap)

    half_cost = pl.CostEstimate(
        flops=2 * rows * width * half, bytes_accessed=4 * width * half, transcendentals=0
    )
    fit_mine, a_theirs = pl.pallas_call(
        fit_mine_kernel,
        out_shape=[jax.ShapeDtypeStruct((rows, width), f32), pltpu.VMEM((width, half), bf16)],
        in_specs=[vmem, hbm],
        out_specs=[vmem] * 2,
        scratch_shapes=[
            pltpu.VMEM((rows, half), bf16),
            pltpu.VMEM((width, half), bf16),
            pltpu.SemaphoreType.DMA((2 * PIECES,)),
        ],
        compiler_params=pltpu.CompilerParams(vmem_limit_bytes=24 << 20),
        cost_estimate=half_cost,
        name="fit_mine",
    )(weighted_mine, by_neuron)
    fit_mine, totals_mine = lax.optimization_barrier((fit_mine, totals_mine))
    local_fit = pl.pallas_call(
        fit_theirs_kernel,
        out_shape=jax.ShapeDtypeStruct((rows, width), f32),
        in_specs=[vmem] * 3,
        out_specs=vmem,
        scratch_shapes=[pltpu.VMEM((rows, half), bf16)],
        compiler_params=pltpu.CompilerParams(vmem_limit_bytes=8 << 20),
        cost_estimate=half_cost,
        name="fit_theirs",
    )(weighted_theirs, pltpu.with_memory_space_constraint(a_theirs, pltpu.VMEM), fit_mine)
    one, two, three = (
        lax.ppermute(local_fit, "tok", [(i, (i + hop) % planes) for i in range(planes)])
        for hop in (1, 2, 3)
    )
    fitted = (local_fit + two) + (one + three)
    fitted = fitted / math.sqrt(tokens * planes)

    totals_theirs = lax.ppermute(totals_mine, "feat", swap)
    squares = jnp.where(core == 0, totals_mine, totals_theirs)
    crosses = jnp.where(core == 0, totals_theirs, totals_mine)
    wide_weights = probe_weights.astype(f32)
    wide_direction = direction.astype(f32)
    member = (group_ids[None, :] == jnp.arange(GROUPS, dtype=jnp.int32)[:, None]).astype(f32)
    group_norm = jnp.sqrt(squares + DELTA * DELTA)
    spread = jnp.dot(
        jnp.concatenate([group_norm, crosses], 0),
        member,
        precision=lax.Precision.HIGHEST,
        preferred_element_type=f32,
    )
    scale = spread[:probes]
    cross = spread[probes:]
    gradient = fitted[:probes] + LAMBDA_WEIGHT * wide_weights / scale
    hess_vec = fitted[probes:] + LAMBDA_WEIGHT * (
        wide_direction / scale - wide_weights * cross / (scale * scale * scale)
    )
    return (gradient, hess_vec)


def solution(mesh):
    return jax.shard_map(
        local,
        mesh=mesh,
        in_specs=(P("tok", "feat"), P(None, "tok"), P(None, "feat"), P(None, "feat"), P("feat")),
        out_specs=(P(None, "feat"), P(None, "feat")),
        check_vma=False,
    )
```

time: 227 us -> 64.9 us (0.29); the launches traced: 224 us -> 64.6 us
  blocking collectives: 148 us -> 37.4 us
  waiting for transfers between devices: 50 us -> 7.12 us
  between operations: 14.1 us -> 0.75 us
  matrix products: 10.4 us -> 0.16 us
  Pallas kernels: 0 us -> 7.91 us
  local copies, waits for them, and re-layouts: 0.02 us -> 5.9 us
  starting transfers between devices: 0.04 us -> 4.56 us
    psum x2 -> x0, blocking collectives: 148 us -> none  [the longest x1 134 us: local(): totals = lax.psum(local_stats, 'feat')]
    psum x1 -> x0, waiting for transfers between devices: 50 us -> none  [local(): margins = lax.psum(partial_value, 'feat')]
    all_to_all x0 -> x2, blocking collectives: none -> 37.4 us  [the longest x1 23.3 us: local(): arrived = lax.all_to_all(outgoing, 'feat', 0, 0, axis_index_groups=by_core)]
    dot_general x4 -> x1, matrix products: 10.4 us -> 0.16 us  [local(): jnp.dot(jnp.concatenate([group_norm, crosses], 0), member, precision=lax....]
    pallas_call x0 -> x4, Pallas kernels: none -> 7.91 us  [the longest x1 3.54 us: local(): pl.pallas_call(margins_kernel, out_shape=[jax.ShapeDtypeStruct((chips, ro...]
    ppermute x0 -> x7, waiting for transfers between devices: none -> 7.12 us  [the longest x3 5.06 us: local(): lax.ppermute(local_fit, 'tok', [(i, (i + hop) % planes) for i in range(pl...]
    unnamed x8 -> x16, local copies, waits for them, and re-layouts: 0.02 us -> 5.89 us
    ppermute x0 -> x7, starting transfers between devices: none -> 4.56 us  [the longest x3 3.47 us: local(): lax.ppermute(local_fit, 'tok', [(i, (i + hop) % planes) for i in range(pl...]
  transfers between devices with their start and end apart: 1 -> 7, of which waited for: 1 -> 6; matrix products, arithmetic and copies ran while one was open for 0% -> 0% of each run, Pallas kernels for 0% -> 0%
where the time goes in v2:
time: 64.9 us; the launch traced here: 64.6 us
  blocking collectives  37.4 us (58%)
  Pallas kernels  7.91 us (12%)
  waiting for transfers between devices  7.12 us (11%)
  local copies, waits for them, and re-layouts  5.9 us (9%)
  starting transfers between devices  4.56 us (7%)
  other arithmetic  0.79 us (1%)
  between operations  0.75 us (1%)
    all_to_all x1, blocking collectives, local(): arrived = lax.all_to_all(outgoing, 'feat', 0, 0, axis_index_groups=by_core)  23.3 us
    all_to_all x1, blocking collectives, local(): lax.all_to_all(copies, 'feat', 0, 0, axis_index_groups=by_core)  14.1 us
    unnamed x16, local copies, waits for them, and re-layouts  5.89 us
    ppermute x3, waiting for transfers between devices, local(): lax.ppermute(local_fit, 'tok', [(i, (i + hop) % planes) for i in range(pl...  5.06 us
    pallas_call x1, Pallas kernels, local(): pl.pallas_call(margins_kernel, out_shape=[jax.ShapeDtypeStruct((chips, ro...  3.54 us
    ppermute x3, starting transfers between devices, local(): lax.ppermute(local_fit, 'tok', [(i, (i + hop) % planes) for i in range(pl...  3.47 us
    pallas_call x1, Pallas kernels, local(): pl.pallas_call(fit_mine_kernel, out_shape=[jax.ShapeDtypeStruct((rows, wi...  3.21 us
  transfers between devices with their start and end apart: 7, of which 6 were waited for; matrix products, arithmetic and copies ran while one was open for 0% of the time, Pallas kernels for 0%

profile of v2, /device:TPU:6, one launch (start us, length us, event | category | flops | bytes accessed | tf_op | source)
XLA Modules:
  0.0 64.6 jit_solution(1372051838626075520)
XLA Ops:
  0.6 0.0 copy-start.2
  0.6 0.7 %copy-done.2 = bf16[8,448]{1,0:T(8,128)(2,1)S(1)} copy-done((bf16[8,448]{1,0:T(8,128)(2,1)S(1)}, bf16[8,448]{1,0:T(8,128)(2,1)}, u32[]{:S(2)}) %copy-start.2) | copy-done | bytes 7192
  1.3 0.0 copy-start.4
  1.3 0.7 %copy-done.4 = bf16[8,448]{1,0:T(8,128)(2,1)S(1)} copy-done((bf16[8,448]{1,0:T(8,128)(2,1)S(1)}, bf16[8,448]{1,0:T(8,128)(2,1)}, u32[]{:S(2)}) %copy-start.4) | copy-done | bytes 7192
  2.0 0.0 copy-start.6
  2.0 0.7 %copy-done.6 = s32[448]{0:T(512)S(1)} copy-done((s32[448]{0:T(512)S(1)}, s32[448]{0:T(512)}, u32[]{:S(2)}) %copy-start.6) | copy-done | bytes 1816
  2.7 3.5 %margins.1 = (f32[32,16,128]{2,1,0:T(8,128)S(1)}, f32[32,16,128]{2,1,0:T(8,128)S(1)}, f32[8,64]{1,0:T(8,128)S(1)}, f32[8,64]{1,0:T(8,128)S(1)}, s32[8,128]{1,0:T(8,128)S(1)}) custom-call(bf16[8,448]{1,0:T(8,128)(2,1)S(1)} %copy-done.2, bf16[8,448]{1,0:T(8,128)(2,1)S(1)} %copy-done.4, s32[1,448]{1,0:T(1,128)S(1)} %bitcast.2, s32[8,8192]{1,0:T(8,128)} %labels_ref.1, ...), custom_call_target="tpu_custom_call" | custom-call | tf_op jit(solution)/shard_map/margins/pallas_call | solution.py:143
  6.3 0.0 copy-start.7
  6.3 0.0 copy-start.3
  6.3 0.0 copy-start.5
  6.3 0.1 collective-permute-start.1
  6.4 0.5 collective-permute-start
  6.9 0.7 %collective-permute-done.1 = f32[8,64]{1,0:T(8,128)S(1)} collective-permute-done((f32[8,64]{1,0:T(8,128)S(1)}, f32[8,64]{1,0:T(8,128)S(1)}, u32[]{:S(2)}, u32[]{:S(2)}) %collective-permute-start.1) | collective-permute-done | bytes 2080 | tf_op jit(solution)/shard_map/ppermute | solution.py:164
  7.6 0.1 pad_maximum_fusion.1
  7.6 0.4 collective-permute-done
  8.1 23.3 %all_to_all.10.arrived = bf16[32,24,128]{2,1,0:T(8,128)(2,1)S(1)} all-to-all(bf16[32,24,128]{2,1,0:T(8,128)(2,1)S(1)} %pad_maximum_fusion), channel_id=1, replica_groups={{0,2,4,6,8,10,12,14,16,18,20,22,24,26,28,30,32,34,36,38,40,42,44,46,48,..., dimensions={0} | all-to-all | bytes 393216 | tf_op jit(solution)/shard_map/all_to_all | solution.py:171
  31.4 0.1 weighted.1
  31.5 14.1 %all_to_all.11.weighted = bf16[32,16,128]{2,1,0:T(8,128)(2,1)S(1)} all-to-all(bf16[32,16,128]{2,1,0:T(8,128)(2,1)S(1)} %get-tuple-element.18), channel_id=1, replica_groups={{0,2,4,6,8,10,12,14,16,18,20,22,24,26,28,30,32,34,36,38,40,42,44,46,48,..., dimensions={0} | all-to-all | bytes 262144 | tf_op jit(solution)/shard_map/all_to_all | solution.py:183
  45.7 3.2 %fit_mine.1 = (f32[16,448]{1,0:T(8,128)S(1)}, bf16[448,4096]{1,0:T(8,128)(2,1)S(1)}) custom-call(bf16[32,16,128]{2,1,0:T(8,128)(2,1)S(1)} %all_to_all.11.weighted, bf16[448,8192]{1,0:T(8,128)(2,1)} %bitcast.4), custom_call_target="tpu_custom_call" | custom-call | flops 58720256 | bytes 7340032 | tf_op jit(solution)/shard_map/fit_mine/pallas_call | solution.py:189
  48.9 0.0 copy-start
  48.9 1.8 %copy-done = bf16[448,4096]{1,0:T(8,128)(2,1)} copy-done((bf16[448,4096]{1,0:T(8,128)(2,1)}, bf16[448,4096]{1,0:T(8,128)(2,1)S(1)}, u32[]{:S(2)}) %copy-start) | copy-done | bytes 3670040
  50.7 0.0 collective-permute-start.6
  50.7 0.5 collective-permute-start.2
  51.2 0.7 %collective-permute-done.6 = f32[8,64]{1,0:T(8,128)S(1)} collective-permute-done((f32[8,64]{1,0:T(8,128)S(1)}, f32[8,64]{1,0:T(8,128)S(1)}, u32[]{:S(2)}, u32[]{:S(2)}) %collective-permute-start.6) | collective-permute-done | bytes 2080 | tf_op jit(solution)/shard_map/ppermute | solution.py:221
  51.8 0.3 collective-permute-done.2.weighted
  52.2 0.0 copy-start.1
  52.2 2.0 %copy-done.1 = bf16[448,4096]{1,0:T(8,128)(2,1)S(1)} copy-done((bf16[448,4096]{1,0:T(8,128)(2,1)S(1)}, bf16[448,4096]{1,0:T(8,128)(2,1)}, u32[]{:S(2)}) %copy-start.1) | copy-done | bytes 3670040
  54.2 1.1 %fit_theirs.1 = f32[16,448]{1,0:T(8,128)S(1)} custom-call(bf16[32,16,128]{2,1,0:T(8,128)(2,1)S(1)} %collective-permute-done.2.weighted, bf16[448,4096]{1,0:T(8,128)(2,1)S(1)} %copy-done.1, f32[16,448]{1,0:T(8,128)S(1)} %get-tuple-element.22.base), custom_call_target="tpu_custom_call" | custom-call | flops 58720256 | bytes 7340032 | tf_op jit(solution)/shard_map/fit_theirs/pallas_call | solution.py:204
  55.3 0.9 %collective-permute-start.5 = (f32[16,448]{1,0:T(8,128)S(1)}, f32[16,448]{1,0:T(8,128)S(1)}, u32[]{:S(2)}, u32[]{:S(2)}) collective-permute-start(f32[16,448]{1,0:T(8,128)S(1)} %fit_theirs.1), channel_id=1, source_target_pairs={{0,192},{64,0},{128,64},{192,128},{1,193},{65,1},{129,65},{193,129... | collective-permute-start | bytes 86024 | tf_op jit(solution)/shard_map/ppermute | solution.py:215
  56.1 2.4 %collective-permute-start.4 = (f32[16,448]{1,0:T(8,128)S(1)}, f32[16,448]{1,0:T(8,128)S(1)}, u32[]{:S(2)}, u32[]{:S(2)}) collective-permute-start(f32[16,448]{1,0:T(8,128)S(1)} %fit_theirs.1), channel_id=1, source_target_pairs={{0,64},{64,128},{128,192},{192,0},{1,65},{65,129},{129,193},{193,1... | collective-permute-start | bytes 86024 | tf_op jit(solution)/shard_map/ppermute | solution.py:215
  58.5 0.2 collective-permute-start.3
  58.7 0.0 copy-done.7
  58.7 0.2 fusion
  58.9 1.5 %collective-permute-done.5 = f32[16,448]{1,0:T(8,128)S(1)} collective-permute-done((f32[16,448]{1,0:T(8,128)S(1)}, f32[16,448]{1,0:T(8,128)S(1)}, u32[]{:S(2)}, u32[]{:S(2)}) %collective-permute-start.5) | collective-permute-done | bytes 28704 | tf_op jit(solution)/shard_map/ppermute | solution.py:215
  60.4 0.0 collective-permute-done.4
  60.4 3.5 %collective-permute-done.3 = f32[16,448]{1,0:T(8,128)S(1)} collective-permute-done((f32[16,448]{1,0:T(8,128)S(1)}, f32[16,448]{1,0:T(8,128)S(1)}, u32[]{:S(2)}, u32[]{:S(2)}) %collective-permute-start.3) | collective-permute-done | bytes 28704 | tf_op jit(solution)/shard_map/ppermute | solution.py:215
  64.0 0.0 copy-done.3
  64.0 0.0 copy-done.5
  64.0 0.6 fusion.7
  (6 shorter events, 0.1 us)
Async XLA Ops:
  0.6 0.7 %copy-start.2 = (bf16[8,448]{1,0:T(8,128)(2,1)S(1)}, bf16[8,448]{1,0:T(8,128)(2,1)}, u32[]{:S(2)}) copy-start(bf16[8,448]{1,0:T(8,128)(2,1)} %w_ref.1) | copy-start | bytes 21508
  1.3 0.7 %copy-start.4 = (bf16[8,448]{1,0:T(8,128)(2,1)S(1)}, bf16[8,448]{1,0:T(8,128)(2,1)}, u32[]{:S(2)}) copy-start(bf16[8,448]{1,0:T(8,128)(2,1)} %d_ref.1) | copy-start | bytes 21508
  2.0 0.7 %copy-start.6 = (s32[448]{0:T(512)S(1)}, s32[448]{0:T(512)}, u32[]{:S(2)}) copy-start(s32[448]{0:T(512)} %param.9) | copy-start | bytes 5380
  6.3 52.5 %copy-start.7 = (s32[448]{0:T(512)S(1)}, s32[448]{0:T(512)}, u32[]{:S(2)}) copy-start(s32[448]{0:T(512)} %param.9) | copy-start | bytes 5380
  6.3 57.7 %copy-start.3 = (bf16[8,448]{1,0:T(8,128)(2,1)S(1)}, bf16[8,448]{1,0:T(8,128)(2,1)}, u32[]{:S(2)}) copy-start(bf16[8,448]{1,0:T(8,128)(2,1)} %w_ref.1) | copy-start | bytes 21508
  6.3 57.7 %copy-start.5 = (bf16[8,448]{1,0:T(8,128)(2,1)S(1)}, bf16[8,448]{1,0:T(8,128)(2,1)}, u32[]{:S(2)}) copy-start(bf16[8,448]{1,0:T(8,128)(2,1)} %d_ref.1) | copy-start | bytes 21508
  6.3 1.3 %collective-permute-start.1 = (f32[8,64]{1,0:T(8,128)S(1)}, f32[8,64]{1,0:T(8,128)S(1)}, u32[]{:S(2)}, u32[]{:S(2)}) collective-permute-start(f32[8,64]{1,0:T(8,128)S(1)} %get-tuple-element.16), channel_id=1, source_target_pairs={{0,1},{1,0},{2,3},{3,2},{4,5},{5,4},{6,7},{7,6},{8,9},{9,8},{10,11... | collective-permute-start | bytes 6152 | tf_op jit(solution)/shard_map/ppermute | solution.py:164
  6.4 1.7 %collective-permute-start = (f32[32,16,128]{2,1,0:T(8,128)S(1)}, f32[32,16,128]{2,1,0:T(8,128)S(1)}, u32[]{:S(2)}, u32[]{:S(2)}) collective-permute-start(f32[32,16,128]{2,1,0:T(8,128)S(1)} %get-tuple-element.14), channel_id=1, source_target_pairs={{0,1},{1,0},{2,3},{3,2},{4,5},{5,4},{6,7},{7,6},{8,9},{9,8},{10,11... | collective-permute-start | bytes 786440 | tf_op jit(solution)/shard_map/ppermute | solution.py:167
  48.9 1.8 %copy-start = (bf16[448,4096]{1,0:T(8,128)(2,1)}, bf16[448,4096]{1,0:T(8,128)(2,1)S(1)}, u32[]{:S(2)}) copy-start(bf16[448,4096]{1,0:T(8,128)(2,1)S(1)} %get-tuple-element.19.a_theirs) | copy-start | bytes 11010052
  50.7 1.2 %collective-permute-start.6 = (f32[8,64]{1,0:T(8,128)S(1)}, f32[8,64]{1,0:T(8,128)S(1)}, u32[]{:S(2)}, u32[]{:S(2)}) collective-permute-start(f32[8,64]{1,0:T(8,128)S(1)} %get-tuple-element.23), channel_id=1, source_target_pairs={{0,1},{1,0},{2,3},{3,2},{4,5},{5,4},{6,7},{7,6},{8,9},{9,8},{10,11... | collective-permute-start | bytes 6152 | tf_op jit(solution)/shard_map/ppermute | solution.py:221
  50.7 1.5 %collective-permute-start.2 = (bf16[32,16,128]{2,1,0:T(8,128)(2,1)S(1)}, bf16[32,16,128]{2,1,0:T(8,128)(2,1)S(1)}, u32[]{:S(2)}, u32[]{:S(2)}) collective-permute-start(bf16[32,16,128]{2,1,0:T(8,128)(2,1)S(1)} %all_to_all.11.weighted), channel_id=1, source_target_pairs={{0,1},{1,0},{2,3},{3,2},{4,5},{5,4},{6,7},{7,6},{8,9},{9,8},{10,11... | collective-permute-start | bytes 393224 | tf_op jit(solution)/shard_map/ppermute | solution.py:184
  52.2 2.0 %copy-start.1 = (bf16[448,4096]{1,0:T(8,128)(2,1)S(1)}, bf16[448,4096]{1,0:T(8,128)(2,1)}, u32[]{:S(2)}) copy-start(bf16[448,4096]{1,0:T(8,128)(2,1)} %copy-done) | copy-start | bytes 11010052
  55.3 5.2 %collective-permute-start.5 = (f32[16,448]{1,0:T(8,128)S(1)}, f32[16,448]{1,0:T(8,128)S(1)}, u32[]{:S(2)}, u32[]{:S(2)}) collective-permute-start(f32[16,448]{1,0:T(8,128)S(1)} %fit_theirs.1), channel_id=1, source_target_pairs={{0,192},{64,0},{128,64},{192,128},{1,193},{65,1},{129,65},{193,129... | collective-permute-start | bytes 86024 | tf_op jit(solution)/shard_map/ppermute | solution.py:215
  56.1 4.3 %collective-permute-start.4 = (f32[16,448]{1,0:T(8,128)S(1)}, f32[16,448]{1,0:T(8,128)S(1)}, u32[]{:S(2)}, u32[]{:S(2)}) collective-permute-start(f32[16,448]{1,0:T(8,128)S(1)} %fit_theirs.1), channel_id=1, source_target_pairs={{0,64},{64,128},{128,192},{192,0},{1,65},{65,129},{129,193},{193,1... | collective-permute-start | bytes 86024 | tf_op jit(solution)/shard_map/ppermute | solution.py:215
  58.5 5.4 %collective-permute-start.3 = (f32[16,448]{1,0:T(8,128)S(1)}, f32[16,448]{1,0:T(8,128)S(1)}, u32[]{:S(2)}, u32[]{:S(2)}) collective-permute-start(f32[16,448]{1,0:T(8,128)S(1)} %fit_theirs.1), channel_id=1, source_target_pairs={{0,128},{64,192},{128,0},{192,64},{1,129},{65,193},{129,1},{193,65... | collective-permute-start | bytes 86024 | tf_op jit(solution)/shard_map/ppermute | solution.py:215

commit v3 on v0

v3 whole, which is shorter than its diff:
```python
import math

import jax
import jax.numpy as jnp
from jax import lax
from jax.experimental import pallas as pl
from jax.experimental.pallas import tpu as pltpu
from jax.sharding import PartitionSpec as P

GROUPS = 64


DELTA = 0.05
LAMBDA_WEIGHT = 8.0

LANES = 128
PIECES = 4


def transposed_dot(left, right, precision=None):
    return lax.dot_general(
        left,
        right,
        (((1,), (1,)), ((), ())),
        precision=precision,
        preferred_element_type=jnp.float32,
    )


def start_half(a_ref, side, held, sems):
    half = held.shape[1]
    piece = half // PIECES
    copies = []
    for i in range(PIECES):
        start = pl.multiple_of(side * half + i * piece, LANES)
        copy = pltpu.make_async_copy(
            a_ref.at[:, pl.ds(start, piece)], held.at[:, pl.ds(i * piece, piece)], sems.at[i]
        )
        copy.start()
        copies.append(copy)
    return copies


def multiply_half(stacked, copies, held, out):
    piece = held.shape[1] // PIECES
    per_piece = piece // LANES
    for i, copy in enumerate(copies):
        copy.wait()
        product = jnp.dot(
            stacked, held[:, i * piece : (i + 1) * piece], preferred_element_type=jnp.float32
        )
        for k in range(per_piece):
            out[i * per_piece + k] = product[:, k * LANES : (k + 1) * LANES]


def margins_theirs_kernel(
    w_ref, d_ref, g_ref, a_ref, theirs, stacked_out, ids_out, w, d, held, small_sems, a_sems
):
    core = lax.rem(lax.axis_index("feat"), 2)
    small = [
        pltpu.make_async_copy(source, target, small_sems.at[i])
        for i, (source, target) in enumerate(((w_ref, w), (d_ref, d), (g_ref, ids_out)))
    ]
    for copy in small:
        copy.start()
    copies = start_half(a_ref, 1 - core, held, a_sems)
    for copy in small:
        copy.wait()
    stacked = jnp.concatenate([w[...], d[...]], 0)
    stacked_out[...] = stacked
    wide_weights = w[...].astype(jnp.float32)
    products = jnp.concatenate(
        [wide_weights * wide_weights, wide_weights * d[...].astype(jnp.float32)], 0
    )
    number = lax.broadcasted_iota(jnp.int32, (LANES, ids_out.shape[1]), 0)
    member = (number == ids_out[...]).astype(jnp.float32)
    theirs[theirs.shape[0] - 1] = transposed_dot(products, member, lax.Precision.HIGHEST)
    multiply_half(stacked, copies, held, theirs)


def margins_mine_kernel(stacked, labels_ref, a_ref, mine, targets, held, labels_sem, a_sems):
    me = lax.axis_index("feat")
    core, chip = lax.rem(me, 2), lax.div(me, 2)
    copies = start_half(a_ref, core, held, a_sems)
    share = targets.shape[1]
    spot = pl.multiple_of(core * held.shape[1] + chip * share, LANES)
    labels_copy = pltpu.make_async_copy(labels_ref.at[:, pl.ds(spot, share)], targets, labels_sem)
    labels_copy.start()
    multiply_half(stacked[...], copies, held, mine)
    labels_copy.wait()


def weighted_kernel(arrived, targets, copies):
    rows = copies.shape[1]
    probes = rows // 2
    margins = jnp.sum(arrived[...].astype(jnp.float32), 0)
    likely = 1.0 / (1.0 + jnp.exp(-margins[:probes]))
    weighted = jnp.concatenate(
        [likely - targets[...].astype(jnp.float32), likely * (1.0 - likely) * margins[probes:]], 0
    ).astype(jnp.bfloat16)
    copies[...] = jnp.broadcast_to(weighted[None], copies.shape)


def fit_kernel(side, weighted, base, a_ref, out, flat, held, sems):
    core = lax.rem(lax.axis_index("feat"), 2)
    copies = start_half(a_ref, core if side == 0 else 1 - core, held, sems)
    for k in range(weighted.shape[0]):
        flat[:, k * LANES : (k + 1) * LANES] = weighted[k]
    total = base[...]
    piece = held.shape[1] // PIECES
    for i, copy in enumerate(copies):
        copy.wait()
        at = slice(i * piece, (i + 1) * piece)
        total = total + transposed_dot(flat[:, at], held[:, at])
    out[...] = total


def local(activations, labels, probe_weights, direction, group_ids):
    probes, width = probe_weights.shape
    rows = 2 * probes
    tokens = activations.shape[0]
    half = tokens // 2
    planes = lax.axis_size("tok")
    devices = lax.axis_size("feat")
    chips = devices // 2
    share = half // chips
    by_core = [[2 * i + side for i in range(chips)] for side in range(2)]
    swap = [(i, i ^ 1) for i in range(devices)]
    along = [(2 * i, 2 * i + 2) for i in range(chips - 1)]
    along += [(2 * i + 3, 2 * i + 1) for i in range(chips - 1)]
    f32, bf16 = jnp.float32, jnp.bfloat16
    vmem, hbm = pl.BlockSpec(memory_space=pltpu.VMEM), pl.BlockSpec(memory_space=pltpu.HBM)
    held = [pltpu.VMEM((width, half), bf16)]
    limit = pltpu.CompilerParams(vmem_limit_bytes=16 << 20)
    half_cost = pl.CostEstimate(
        flops=2 * rows * width * half, bytes_accessed=2 * width * half, transcendentals=0
    )

    def stay(value):
        return pltpu.with_memory_space_constraint(value, pltpu.HBM)

    by_neuron = stay(activations.T)
    theirs, stacked, ids = pl.pallas_call(
        margins_theirs_kernel,
        out_shape=[
            jax.ShapeDtypeStruct((chips + 1, rows, share), f32),
            jax.ShapeDtypeStruct((rows, width), bf16),
            jax.ShapeDtypeStruct((1, width), jnp.int32),
        ],
        in_specs=[hbm] * 4,
        out_specs=[vmem] * 3,
        scratch_shapes=[
            pltpu.VMEM((probes, width), bf16),
            pltpu.VMEM((probes, width), bf16),
            *held,
            pltpu.SemaphoreType.DMA((3,)),
            pltpu.SemaphoreType.DMA((PIECES,)),
        ],
        compiler_params=limit,
        cost_estimate=half_cost,
        name="margins_theirs",
    )(stay(probe_weights), stay(direction), stay(group_ids[None, :]), by_neuron)
    from_pair = lax.ppermute(theirs, "feat", swap)
    mine, targets = pl.pallas_call(
        margins_mine_kernel,
        out_shape=[
            jax.ShapeDtypeStruct((chips, rows, share), f32),
            jax.ShapeDtypeStruct((probes, share), jnp.int32),
        ],
        in_specs=[vmem, hbm, hbm],
        out_specs=[vmem] * 2,
        scratch_shapes=[*held, pltpu.SemaphoreType.DMA, pltpu.SemaphoreType.DMA((PIECES,))],
        compiler_params=limit,
        cost_estimate=half_cost,
        name="margins_mine",
    )(stacked, stay(labels), by_neuron)

    stats = theirs[chips, :, :GROUPS] + from_pair[chips, :, :GROUPS]
    outgoing = (mine + from_pair[:chips]).astype(bf16)
    beside = lax.ppermute(stats, "feat", along)
    arrived = lax.all_to_all(outgoing, "feat", 0, 0, axis_index_groups=by_core)
    copies = pl.pallas_call(
        weighted_kernel,
        out_shape=jax.ShapeDtypeStruct((chips, rows, share), bf16),
        in_specs=[vmem] * 2,
        out_specs=vmem,
        compiler_params=pltpu.CompilerParams(vmem_limit_bytes=4 << 20),
        name="weighted",
    )(arrived, targets)
    weighted_mine = lax.all_to_all(copies, "feat", 0, 0, axis_index_groups=by_core)
    weighted_theirs = lax.ppermute(weighted_mine, "feat", swap)

    def fit(side, weighted, base):
        def kernel(*refs):
            fit_kernel(side, *refs)

        return pl.pallas_call(
            kernel,
            out_shape=jax.ShapeDtypeStruct((rows, width), f32),
            in_specs=[vmem, vmem, hbm],
            out_specs=vmem,
            scratch_shapes=[
                pltpu.VMEM((rows, half), bf16),
                *held,
                pltpu.SemaphoreType.DMA((PIECES,)),
            ],
            compiler_params=limit,
            cost_estimate=half_cost,
            name=("fit_mine", "fit_theirs")[side],
        )(weighted, base, by_neuron)

    fit_mine = fit(0, weighted_mine, jnp.zeros((rows, width), f32))
    local_fit = fit(1, weighted_theirs, fit_mine)
    one, two, three = (
        lax.ppermute(local_fit, "tok", [(i, (i + hop) % planes) for i in range(planes)])
        for hop in (1, 2, 3)
    )
    fitted = (local_fit + two) + (one + three)
    fitted = fitted / math.sqrt(tokens * planes)

    weighted_theirs, beside = lax.optimization_barrier((weighted_theirs, beside))
    totals = stats + (beside + lax.ppermute(beside, "feat", swap))
    wide_weights = stacked[:probes].astype(f32)
    wide_direction = stacked[probes:].astype(f32)
    member = (ids == jnp.arange(GROUPS, dtype=jnp.int32)[:, None]).astype(f32)
    group_norm = jnp.sqrt(totals[:probes] + DELTA * DELTA)
    spread = jnp.dot(
        jnp.concatenate([group_norm, totals[probes:]], 0),
        member,
        precision=lax.Precision.HIGHEST,
        preferred_element_type=f32,
    )
    scale = spread[:probes]
    cross = spread[probes:]
    gradient = fitted[:probes] + LAMBDA_WEIGHT * wide_weights / scale
    hess_vec = fitted[probes:] + LAMBDA_WEIGHT * (
        wide_direction / scale - wide_weights * cross / (scale * scale * scale)
    )
    return (gradient, hess_vec)


def solution(mesh):
    return jax.shard_map(
        local,
        mesh=mesh,
        in_specs=(P("tok", "feat"), P(None, "tok"), P(None, "feat"), P(None, "feat"), P("feat")),
        out_specs=(P(None, "feat"), P(None, "feat")),
        check_vma=False,
    )
```

time: 227 us -> 61.5 us (0.27)
  the two profiles are of different devices: /device:TPU:6 before, /device:TPU:8 now
where the time goes in v3:
time: 61.5 us; the launch traced here: 61.2 us
  blocking collectives  35.2 us (57%)
  Pallas kernels  10.7 us (17%)
  starting transfers between devices  8.24 us (13%)
  waiting for transfers between devices  5.52 us (9%)
  between operations  0.73 us (1%)
  other arithmetic  0.69 us (1%)
    all_to_all x1, blocking collectives, local(): arrived = lax.all_to_all(outgoing, 'feat', 0, 0, axis_index_groups=by_core)  21.2 us
    all_to_all x1, blocking collectives, local(): lax.all_to_all(copies, 'feat', 0, 0, axis_index_groups=by_core)  13.9 us
    ppermute x3, starting transfers between devices, local(): lax.ppermute(local_fit, 'tok', [(i, (i + hop) % planes) for i in range(pl...  5.13 us
    pallas_call x2, Pallas kernels, fit(): pl.pallas_call(kernel, out_shape=jax.ShapeDtypeStruct((rows, width), f32)...  5.02 us
    ppermute x3, waiting for transfers between devices, local(): lax.ppermute(local_fit, 'tok', [(i, (i + hop) % planes) for i in range(pl...  3.42 us
    pallas_call x1, Pallas kernels, local(): pl.pallas_call(margins_theirs_kernel, out_shape=[jax.ShapeDtypeStruct((ch...  3.29 us
    ppermute x1, starting transfers between devices, local(): beside = lax.ppermute(stats, 'feat', along)  3.02 us
    pallas_call x1, Pallas kernels, local(): pl.pallas_call(margins_mine_kernel, out_shape=[jax.ShapeDtypeStruct((chip...  2.31 us
  transfers between devices with their start and end apart: 7, of which 3 were waited for; matrix products, arithmetic and copies ran while one was open for 0% of the time, Pallas kernels for 12%

profile of v3, /device:TPU:8, one launch (start us, length us, event | category | flops | bytes accessed | tf_op | source)
XLA Modules:
  0.0 61.2 jit_solution(18059182165047002315)
XLA Ops:
  0.6 3.3 %margins_theirs.1 = (f32[33,16,128]{2,1,0:T(8,128)S(1)}, bf16[16,448]{1,0:T(8,128)(2,1)S(1)}, s32[1,448]{1,0:T(1,128)S(1)}) custom-call(bf16[8,448]{1,0:T(8,128)(2,1)} %w_ref.1, bf16[8,448]{1,0:T(8,128)(2,1)} %d_ref.1, s32[1,448]{1,0:T(1,128)} %bitcast.10, bf16[448,8192]{1,0:T(8,128)(2,1)} %bitcast.6), custom_call_target="tpu_custom_call" | custom-call | flops 58720256 | bytes 3670016 | tf_op jit(solution)/shard_map/margins_theirs/pallas_call | solution.py:143
  3.9 0.1 collective-permute-start
  4.0 2.3 %margins_mine.1 = (f32[32,16,128]{2,1,0:T(8,128)S(1)}, s32[8,128]{1,0:T(8,128)S(1)}) custom-call(bf16[16,448]{1,0:T(8,128)(2,1)S(1)} %get-tuple-element.8.stacked, s32[8,8192]{1,0:T(8,128)} %labels_ref.1, bf16[448,8192]{1,0:T(8,128)(2,1)} %bitcast.7), custom_call_target="tpu_custom_call" | custom-call | flops 58720256 | bytes 3670016 | tf_op jit(solution)/shard_map/margins_mine/pallas_call | solution.py:164
  6.3 0.0 collective-permute-done
  6.4 21.2 %all_to_all.10.arrived = bf16[32,16,128]{2,1,0:T(8,128)(2,1)S(1)} all-to-all(bf16[32,16,128]{2,1,0:T(8,128)(2,1)S(1)} %fusion), channel_id=1, replica_groups={{0,2,4,6,8,10,12,14,16,18,20,22,24,26,28,30,32,34,36,38,40,42,44,46,48,..., dimensions={0} | all-to-all | bytes 262144 | tf_op jit(solution)/shard_map/all_to_all | solution.py:181
  27.7 0.1 weighted.1
  27.7 13.9 %all_to_all.11.refs_0_ = bf16[32,16,128]{2,1,0:T(8,128)(2,1)S(1)} all-to-all(bf16[32,16,128]{2,1,0:T(8,128)(2,1)S(1)} %weighted.1), channel_id=1, replica_groups={{0,2,4,6,8,10,12,14,16,18,20,22,24,26,28,30,32,34,36,38,40,42,44,46,48,..., dimensions={0} | all-to-all | bytes 262144 | tf_op jit(solution)/shard_map/all_to_all | solution.py:190
  41.6 0.0 collective-permute-start.1
  41.7 3.0 %collective-permute-start.5 = (f32[16,64]{1,0:T(8,128)S(1)}, f32[16,64]{1,0:T(8,128)S(1)}, u32[]{:S(2)}, u32[]{:S(2)}) collective-permute-start(f32[16,64]{1,0:T(8,128)S(1)} %fusion.9), channel_id=1, source_target_pairs={{0,2},{2,4},{4,6},{6,8},{8,10},{10,12},{12,14},{14,16},{16,18},{18... | collective-permute-start | bytes 12296 | tf_op jit(solution)/shard_map/ppermute | solution.py:180
  44.7 2.5 %fit_mine.1.refs_1_ = f32[16,448]{1,0:T(8,128)S(1)} custom-call(bf16[32,16,128]{2,1,0:T(8,128)(2,1)S(1)} %all_to_all.11.refs_0_, f32[16,448]{1,0:T(8,128)S(1)} %broadcast_in_dim.8.refs_1_, bf16[448,8192]{1,0:T(8,128)(2,1)} %bitcast.8), custom_call_target="tpu_custom_call" | custom-call | flops 58720256 | bytes 3670016 | tf_op jit(solution)/shard_map/fit_mine/pallas_call | solution.py:197
  47.2 2.1 %collective-permute-done.5 = f32[16,64]{1,0:T(8,128)S(1)} collective-permute-done((f32[16,64]{1,0:T(8,128)S(1)}, f32[16,64]{1,0:T(8,128)S(1)}, u32[]{:S(2)}, u32[]{:S(2)}) %collective-permute-start.5) | collective-permute-done | bytes 4128 | tf_op jit(solution)/shard_map/ppermute | solution.py:180
  49.3 0.0 collective-permute-done.1.refs_0_
  49.3 0.0 collective-permute-start.6
  49.3 2.5 %fit_theirs.1 = f32[16,448]{1,0:T(8,128)S(1)} custom-call(bf16[32,16,128]{2,1,0:T(8,128)(2,1)S(1)} %collective-permute-done.1.refs_0_, f32[16,448]{1,0:T(8,128)S(1)} %fit_mine.1.refs_1_, bf16[448,8192]{1,0:T(8,128)(2,1)} %bitcast.9), custom_call_target="tpu_custom_call" | custom-call | flops 58720256 | bytes 3670016 | tf_op jit(solution)/shard_map/fit_theirs/pallas_call | solution.py:197
  51.8 1.6 %collective-permute-start.3 = (f32[16,448]{1,0:T(8,128)S(1)}, f32[16,448]{1,0:T(8,128)S(1)}, u32[]{:S(2)}, u32[]{:S(2)}) collective-permute-start(f32[16,448]{1,0:T(8,128)S(1)} %fit_theirs.1), channel_id=1, source_target_pairs={{0,64},{64,128},{128,192},{192,0},{1,65},{65,129},{129,193},{193,1... | collective-permute-start | bytes 86024 | tf_op jit(solution)/shard_map/ppermute | solution.py:215
  53.4 1.7 %collective-permute-start.4 = (f32[16,448]{1,0:T(8,128)S(1)}, f32[16,448]{1,0:T(8,128)S(1)}, u32[]{:S(2)}, u32[]{:S(2)}) collective-permute-start(f32[16,448]{1,0:T(8,128)S(1)} %fit_theirs.1), channel_id=1, source_target_pairs={{0,192},{64,0},{128,64},{192,128},{1,193},{65,1},{129,65},{193,129... | collective-permute-start | bytes 86024 | tf_op jit(solution)/shard_map/ppermute | solution.py:215
  55.1 1.8 %collective-permute-start.2 = (f32[16,448]{1,0:T(8,128)S(1)}, f32[16,448]{1,0:T(8,128)S(1)}, u32[]{:S(2)}, u32[]{:S(2)}) collective-permute-start(f32[16,448]{1,0:T(8,128)S(1)} %fit_theirs.1), channel_id=1, source_target_pairs={{0,128},{64,192},{128,0},{192,64},{1,129},{65,193},{129,1},{193,65... | collective-permute-start | bytes 86024 | tf_op jit(solution)/shard_map/ppermute | solution.py:215
  57.0 0.0 collective-permute-done.6
  57.0 0.2 fusion.1
  57.1 0.0 collective-permute-done.3
  57.1 0.2 collective-permute-done.4
  57.3 3.2 %collective-permute-done.2 = f32[16,448]{1,0:T(8,128)S(1)} collective-permute-done((f32[16,448]{1,0:T(8,128)S(1)}, f32[16,448]{1,0:T(8,128)S(1)}, u32[]{:S(2)}, u32[]{:S(2)}) %collective-permute-start.2) | collective-permute-done | bytes 28704 | tf_op jit(solution)/shard_map/ppermute | solution.py:215
  60.6 0.6 %fusion.8 = (f32[8,448]{1,0:T(8,128)}, f32[8,448]{1,0:T(8,128)}) fusion(f32[16,448]{1,0:T(8,128)S(1)} %fusion.1, f32[16,448]{1,0:T(8,128)S(1)} %add_multiply_fusion, bf16[16,448]{1,0:T(8,128)(2,1)S(1)} %get-tuple-element.8.stacked), kind=kLoop, calls=%fused_computation.14 | loop fusion | flops 46592 | bytes 100352 | tf_op jit(solution)/shard_map/add | solution.py:236
  (6 shorter events, 0.1 us)
Async XLA Ops:
  3.9 2.4 %collective-permute-start = (f32[33,16,128]{2,1,0:T(8,128)S(1)}, f32[33,16,128]{2,1,0:T(8,128)S(1)}, u32[]{:S(2)}, u32[]{:S(2)}) collective-permute-start(f32[33,16,128]{2,1,0:T(8,128)S(1)} %get-tuple-element.10), channel_id=1, source_target_pairs={{0,1},{1,0},{2,3},{3,2},{4,5},{5,4},{6,7},{7,6},{8,9},{9,8},{10,11... | collective-permute-start | bytes 811016 | tf_op jit(solution)/shard_map/ppermute | solution.py:163
  41.6 7.7 %collective-permute-start.1 = (bf16[32,16,128]{2,1,0:T(8,128)(2,1)S(1)}, bf16[32,16,128]{2,1,0:T(8,128)(2,1)S(1)}, u32[]{:S(2)}, u32[]{:S(2)}) collective-permute-start(bf16[32,16,128]{2,1,0:T(8,128)(2,1)S(1)} %all_to_all.11.refs_0_), channel_id=1, source_target_pairs={{0,1},{1,0},{2,3},{3,2},{4,5},{5,4},{6,7},{7,6},{8,9},{9,8},{10,11... | collective-permute-start | bytes 393224 | tf_op jit(solution)/shard_map/ppermute | solution.py:191
  41.7 7.6 %collective-permute-start.5 = (f32[16,64]{1,0:T(8,128)S(1)}, f32[16,64]{1,0:T(8,128)S(1)}, u32[]{:S(2)}, u32[]{:S(2)}) collective-permute-start(f32[16,64]{1,0:T(8,128)S(1)} %fusion.9), channel_id=1, source_target_pairs={{0,2},{2,4},{4,6},{6,8},{8,10},{10,12},{12,14},{14,16},{16,18},{18... | collective-permute-start | bytes 12296 | tf_op jit(solution)/shard_map/ppermute | solution.py:180
  49.3 7.7 %collective-permute-start.6 = (f32[16,64]{1,0:T(8,128)S(1)}, f32[16,64]{1,0:T(8,128)S(1)}, u32[]{:S(2)}, u32[]{:S(2)}) collective-permute-start(f32[16,64]{1,0:T(8,128)S(1)} %collective-permute-done.5), channel_id=1, source_target_pairs={{0,1},{1,0},{2,3},{3,2},{4,5},{5,4},{6,7},{7,6},{8,9},{9,8},{10,11... | collective-permute-start | bytes 12296 | tf_op jit(solution)/shard_map/ppermute | solution.py:222
  51.8 5.3 %collective-permute-start.3 = (f32[16,448]{1,0:T(8,128)S(1)}, f32[16,448]{1,0:T(8,128)S(1)}, u32[]{:S(2)}, u32[]{:S(2)}) collective-permute-start(f32[16,448]{1,0:T(8,128)S(1)} %fit_theirs.1), channel_id=1, source_target_pairs={{0,64},{64,128},{128,192},{192,0},{1,65},{65,129},{129,193},{193,1... | collective-permute-start | bytes 86024 | tf_op jit(solution)/shard_map/ppermute | solution.py:215
  53.4 3.9 %collective-permute-start.4 = (f32[16,448]{1,0:T(8,128)S(1)}, f32[16,448]{1,0:T(8,128)S(1)}, u32[]{:S(2)}, u32[]{:S(2)}) collective-permute-start(f32[16,448]{1,0:T(8,128)S(1)} %fit_theirs.1), channel_id=1, source_target_pairs={{0,192},{64,0},{128,64},{192,128},{1,193},{65,1},{129,65},{193,129... | collective-permute-start | bytes 86024 | tf_op jit(solution)/shard_map/ppermute | solution.py:215
  55.1 5.4 %collective-permute-start.2 = (f32[16,448]{1,0:T(8,128)S(1)}, f32[16,448]{1,0:T(8,128)S(1)}, u32[]{:S(2)}, u32[]{:S(2)}) collective-permute-start(f32[16,448]{1,0:T(8,128)S(1)} %fit_theirs.1), channel_id=1, source_target_pairs={{0,128},{64,192},{128,0},{192,64},{1,129},{65,193},{129,1},{193,65... | collective-permute-start | bytes 86024 | tf_op jit(solution)/shard_map/ppermute | solution.py:215

commit v4 on v3

--- a/solution.py
+++ b/solution.py
@@ -41,10 +41,12 @@
     return copies
 
 
-def multiply_half(stacked, copies, held, out):
+def multiply_half(stacked, copies, held, out, meanwhile=None):
     piece = held.shape[1] // PIECES
     per_piece = piece // LANES
     for i, copy in enumerate(copies):
+        if i == 1 and meanwhile is not None:
+            meanwhile()
         copy.wait()
         product = jnp.dot(
             stacked, held[:, i * piece : (i + 1) * piece], preferred_element_type=jnp.float32
@@ -68,14 +70,21 @@
         copy.wait()
     stacked = jnp.concatenate([w[...], d[...]], 0)
     stacked_out[...] = stacked
-    wide_weights = w[...].astype(jnp.float32)
-    products = jnp.concatenate(
-        [wide_weights * wide_weights, wide_weights * d[...].astype(jnp.float32)], 0
-    )
-    number = lax.broadcasted_iota(jnp.int32, (LANES, ids_out.shape[1]), 0)
-    member = (number == ids_out[...]).astype(jnp.float32)
-    theirs[theirs.shape[0] - 1] = transposed_dot(products, member, lax.Precision.HIGHEST)
-    multiply_half(stacked, copies, held, theirs)
+
+    def sum_groups():
+        wide_weights = w[...].astype(jnp.float32)
+        products = jnp.concatenate(
+            [wide_weights * wide_weights, wide_weights * d[...].astype(jnp.float32)], 0
+        )
+        high = products.astype(jnp.bfloat16)
+        low = (products - high.astype(jnp.float32)).astype(jnp.bfloat16)
+        number = lax.broadcasted_iota(jnp.int32, (LANES, ids_out.shape[1]), 0)
+        member = (number == ids_out[...]).astype(jnp.float32).astype(jnp.bfloat16)
+        sums = transposed_dot(jnp.concatenate([high, low], 0), member)
+        rows = stacked.shape[0]
+        theirs[theirs.shape[0] - 1] = sums[:rows] + sums[rows:]
+
+    multiply_half(stacked, copies, held, theirs, sum_groups)
 
 
 def margins_mine_kernel(stacked, labels_ref, a_ref, mine, targets, held, labels_sem, a_sems):
@@ -101,18 +110,30 @@
     copies[...] = jnp.broadcast_to(weighted[None], copies.shape)
 
 
-def fit_kernel(side, weighted, base, a_ref, out, flat, held, sems):
-    core = lax.rem(lax.axis_index("feat"), 2)
-    copies = start_half(a_ref, core if side == 0 else 1 - core, held, sems)
+def flatten(weighted, flat):
     for k in range(weighted.shape[0]):
         flat[:, k * LANES : (k + 1) * LANES] = weighted[k]
-    total = base[...]
-    piece = held.shape[1] // PIECES
+
+
+def fit_mine_kernel(weighted, a_ref, out, theirs, flat, mine, mine_sems, theirs_sems):
+    core = lax.rem(lax.axis_index("feat"), 2)
+    copies = start_half(a_ref, core, mine, mine_sems)
+    others = start_half(a_ref, 1 - core, theirs, theirs_sems)
+    flatten(weighted, flat)
+    total = jnp.zeros(out.shape, jnp.float32)
+    piece = mine.shape[1] // PIECES
     for i, copy in enumerate(copies):
         copy.wait()
         at = slice(i * piece, (i + 1) * piece)
-        total = total + transposed_dot(flat[:, at], held[:, at])
+        total = total + transposed_dot(flat[:, at], mine[:, at])
     out[...] = total
+    for copy in others:
+        copy.wait()
+
+
+def fit_theirs_kernel(weighted, theirs, base, out, flat):
+    flatten(weighted, flat)
+    out[...] = base[...] + transposed_dot(flat[...], theirs[...])
 
 
 def local(activations, labels, probe_weights, direction, group_ids):
@@ -179,6 +200,7 @@
     outgoing = (mine + from_pair[:chips]).astype(bf16)
     beside = lax.ppermute(stats, "feat", along)
     arrived = lax.all_to_all(outgoing, "feat", 0, 0, axis_index_groups=by_core)
+    arrived, beside = lax.optimization_barrier((arrived, beside))
     copies = pl.pallas_call(
         weighted_kernel,
         out_shape=jax.ShapeDtypeStruct((chips, rows, share), bf16),
@@ -190,27 +212,32 @@
     weighted_mine = lax.all_to_all(copies, "feat", 0, 0, axis_index_groups=by_core)
     weighted_theirs = lax.ppermute(weighted_mine, "feat", swap)
 
-    def fit(side, weighted, base):
-        def kernel(*refs):
-            fit_kernel(side, *refs)
-
-        return pl.pallas_call(
-            kernel,
-            out_shape=jax.ShapeDtypeStruct((rows, width), f32),
-            in_specs=[vmem, vmem, hbm],
-            out_specs=vmem,
-            scratch_shapes=[
-                pltpu.VMEM((rows, half), bf16),
-                *held,
-                pltpu.SemaphoreType.DMA((PIECES,)),
-            ],
-            compiler_params=limit,
-            cost_estimate=half_cost,
-            name=("fit_mine", "fit_theirs")[side],
-        )(weighted, base, by_neuron)
-
-    fit_mine = fit(0, weighted_mine, jnp.zeros((rows, width), f32))
-    local_fit = fit(1, weighted_theirs, fit_mine)
+    flat = pltpu.VMEM((rows, half), bf16)
+    fit_mine, a_theirs = pl.pallas_call(
+        fit_mine_kernel,
+        out_shape=[jax.ShapeDtypeStruct((rows, width), f32), *held],
+        in_specs=[vmem, hbm],
+        out_specs=[vmem] * 2,
+        scratch_shapes=[
+            flat,
+            *held,
+            pltpu.SemaphoreType.DMA((PIECES,)),
+            pltpu.SemaphoreType.DMA((PIECES,)),
+        ],
+        compiler_params=limit,
+        cost_estimate=half_cost,
+        name="fit_mine",
+    )(weighted_mine, by_neuron)
+    local_fit = pl.pallas_call(
+        fit_theirs_kernel,
+        out_shape=jax.ShapeDtypeStruct((rows, width), f32),
+        in_specs=[vmem] * 3,
+        out_specs=vmem,
+        scratch_shapes=[flat],
+        compiler_params=limit,
+        cost_estimate=half_cost,
+        name="fit_theirs",
+    )(weighted_theirs, pltpu.with_memory_space_constraint(a_theirs, pltpu.VMEM), fit_mine)
     one, two, three = (
         lax.ppermute(local_fit, "tok", [(i, (i + hop) % planes) for i in range(planes)])
         for hop in (1, 2, 3)
@@ -218,7 +245,6 @@
     fitted = (local_fit + two) + (one + three)
     fitted = fitted / math.sqrt(tokens * planes)
 
-    weighted_theirs, beside = lax.optimization_barrier((weighted_theirs, beside))
     totals = stats + (beside + lax.ppermute(beside, "feat", swap))
     wide_weights = stacked[:probes].astype(f32)
     wide_direction = stacked[probes:].astype(f32)

time: 61.5 us -> 59.7 us (0.971)
  the two profiles are of different devices: /device:TPU:8 before, /device:TPU:6 now
where the time goes in v4:
time: 59.7 us; the launch traced here: 59.4 us
  starting transfers between devices  24.5 us (41%)
  waiting for transfers between devices  22.4 us (38%)
  Pallas kernels  10.2 us (17%)
  other arithmetic  1.35 us (2%)
  between operations  0.73 us (1%)
    all_to_all x1, starting transfers between devices, local(): arrived = lax.all_to_all(outgoing, 'feat', 0, 0, axis_index_groups=by_core)  11.5 us
    all_to_all x1, waiting for transfers between devices, local(): lax.all_to_all(copies, 'feat', 0, 0, axis_index_groups=by_core)  9.09 us
    all_to_all x1, waiting for transfers between devices, local(): arrived = lax.all_to_all(outgoing, 'feat', 0, 0, axis_index_groups=by_core)  5.86 us
    all_to_all x1, starting transfers between devices, local(): lax.all_to_all(copies, 'feat', 0, 0, axis_index_groups=by_core)  5.63 us
    ppermute x3, waiting for transfers between devices, local(): lax.ppermute(local_fit, 'tok', [(i, (i + hop) % planes) for i in range(pl...  4.97 us
    ppermute x1, starting transfers between devices, local(): beside = lax.ppermute(stats, 'feat', along)  3.69 us
    ppermute x3, starting transfers between devices, local(): lax.ppermute(local_fit, 'tok', [(i, (i + hop) % planes) for i in range(pl...  3.52 us
    pallas_call x1, Pallas kernels, local(): pl.pallas_call(fit_mine_kernel, out_shape=[jax.ShapeDtypeStruct((rows, wi...  3.34 us
  transfers between devices with their start and end apart: 9, of which 6 were waited for; matrix products, arithmetic and copies ran while one was open for 0% of the time, Pallas kernels for 10%

profile of v4, /device:TPU:6, one launch (start us, length us, event | category | flops | bytes accessed | tf_op | source)
XLA Modules:
  0.0 59.4 jit_solution(17650428608775462513)
XLA Ops:
  0.6 2.7 %margins_theirs.1 = (f32[33,16,128]{2,1,0:T(8,128)S(1)}, bf16[16,448]{1,0:T(8,128)(2,1)S(1)}, s32[1,448]{1,0:T(1,128)S(1)}) custom-call(bf16[8,448]{1,0:T(8,128)(2,1)} %w_ref.1, bf16[8,448]{1,0:T(8,128)(2,1)} %d_ref.1, s32[1,448]{1,0:T(1,128)} %bitcast.9, bf16[448,8192]{1,0:T(8,128)(2,1)} %bitcast.6), custom_call_target="tpu_custom_call" | custom-call | flops 58720256 | bytes 3670016 | tf_op jit(solution)/shard_map/margins_theirs/pallas_call | solution.py:164
  3.4 0.1 collective-permute-start
  3.5 2.3 %margins_mine.1 = (f32[32,16,128]{2,1,0:T(8,128)S(1)}, s32[8,128]{1,0:T(8,128)S(1)}) custom-call(bf16[16,448]{1,0:T(8,128)(2,1)S(1)} %get-tuple-element.11.stacked, s32[8,8192]{1,0:T(8,128)} %labels_ref.1, bf16[448,8192]{1,0:T(8,128)(2,1)} %bitcast.7), custom_call_target="tpu_custom_call" | custom-call | flops 58720256 | bytes 3670016 | tf_op jit(solution)/shard_map/margins_mine/pallas_call | solution.py:185
  5.8 0.0 collective-permute-done
  5.8 0.7 %fusion = bf16[32,16,128]{2,1,0:T(8,128)(2,1)} fusion(f32[32,16,128]{2,1,0:T(8,128)S(1)} %get-tuple-element.12, f32[33,16,128]{2,1,0:T(8,128)S(1)} %collective-permute-done), kind=kLoop, calls=%fused_computation.1 | loop fusion | flops 131072 | bytes 655360 | tf_op jit(solution)/shard_map/convert_element_type | solution.py:200
  6.5 11.5 %all-to-all-start = ((bf16[32,16,128]{2,1,0:T(8,128)(2,1)}), bf16[32,16,128]{2,1,0:T(8,128)(2,1)S(1)}, u32[]{:S(2)}, u32[]{:S(2)}) async-start(bf16[32,16,128]{2,1,0:T(8,128)(2,1)} %fusion), calls=%async_computation | async-start | bytes 262144 | tf_op jit(solution)/shard_map/all_to_all | solution.py:202
  18.0 3.7 %collective-permute-start.1 = (f32[16,64]{1,0:T(8,128)S(1)}, f32[16,64]{1,0:T(8,128)S(1)}, u32[]{:S(2)}, u32[]{:S(2)}) collective-permute-start(f32[16,64]{1,0:T(8,128)S(1)} %fusion.9), channel_id=1, source_target_pairs={{0,2},{2,4},{4,6},{6,8},{8,10},{10,12},{12,14},{14,16},{16,18},{18... | collective-permute-start | bytes 12296 | tf_op jit(solution)/shard_map/ppermute | solution.py:201
  21.7 1.3 %collective-permute-done.1 = f32[16,64]{1,0:T(8,128)S(1)} collective-permute-done((f32[16,64]{1,0:T(8,128)S(1)}, f32[16,64]{1,0:T(8,128)S(1)}, u32[]{:S(2)}, u32[]{:S(2)}) %collective-permute-start.1) | collective-permute-done | bytes 4128 | tf_op jit(solution)/shard_map/ppermute | solution.py:201
  23.1 5.9 %all-to-all-done.arrived = bf16[32,16,128]{2,1,0:T(8,128)(2,1)S(1)} async-done(((bf16[32,16,128]{2,1,0:T(8,128)(2,1)}), bf16[32,16,128]{2,1,0:T(8,128)(2,1)S(1)}, u32[]{:S(2)}, u32[]{:S(2)}) %all-to-all-start) | async-done | bytes 131104 | tf_op jit(solution)/shard_map/all_to_all | solution.py:202
  28.9 0.7 %weighted.1 = bf16[32,16,128]{2,1,0:T(8,128)(2,1)} custom-call(bf16[32,16,128]{2,1,0:T(8,128)(2,1)S(1)} %all-to-all-done.arrived, s32[8,128]{1,0:T(8,128)S(1)} %get-tuple-element.15.targets), custom_call_target="tpu_custom_call" | custom-call | tf_op jit(solution)/shard_map/weighted/pallas_call | solution.py:204
  29.6 5.6 %all-to-all-start.1 = ((bf16[32,16,128]{2,1,0:T(8,128)(2,1)}), bf16[32,16,128]{2,1,0:T(8,128)(2,1)S(1)}, u32[]{:S(2)}, u32[]{:S(2)}) async-start(bf16[32,16,128]{2,1,0:T(8,128)(2,1)} %weighted.1), calls=%async_computation.1 | async-start | bytes 262144 | tf_op jit(solution)/shard_map/all_to_all | solution.py:212
  35.3 0.1 collective-permute-start.6
  35.4 1.2 %collective-permute-done.6 = f32[16,64]{1,0:T(8,128)S(1)} collective-permute-done((f32[16,64]{1,0:T(8,128)S(1)}, f32[16,64]{1,0:T(8,128)S(1)}, u32[]{:S(2)}, u32[]{:S(2)}) %collective-permute-start.6) | collective-permute-done | bytes 4128 | tf_op jit(solution)/shard_map/ppermute | solution.py:248
  36.5 9.1 %all-to-all-done.1.weighted = bf16[32,16,128]{2,1,0:T(8,128)(2,1)S(1)} async-done(((bf16[32,16,128]{2,1,0:T(8,128)(2,1)}), bf16[32,16,128]{2,1,0:T(8,128)(2,1)S(1)}, u32[]{:S(2)}, u32[]{:S(2)}) %all-to-all-start.1) | async-done | bytes 131104 | tf_op jit(solution)/shard_map/all_to_all | solution.py:212
  45.6 0.0 collective-permute-start.2
  45.6 3.3 %fit_mine.1 = (f32[16,448]{1,0:T(8,128)S(1)}, bf16[448,4096]{1,0:T(8,128)(2,1)S(1)}) custom-call(bf16[32,16,128]{2,1,0:T(8,128)(2,1)S(1)} %all-to-all-done.1.weighted, bf16[448,8192]{1,0:T(8,128)(2,1)} %bitcast.8), custom_call_target="tpu_custom_call" | custom-call | flops 58720256 | bytes 3670016 | tf_op jit(solution)/shard_map/fit_mine/pallas_call | solution.py:216
  49.0 0.0 collective-permute-done.2.weighted
  49.0 1.1 %fit_theirs.1 = f32[16,448]{1,0:T(8,128)S(1)} custom-call(bf16[32,16,128]{2,1,0:T(8,128)(2,1)S(1)} %collective-permute-done.2.weighted, bf16[448,4096]{1,0:T(8,128)(2,1)S(1)} %get-tuple-element.16.theirs, f32[16,448]{1,0:T(8,128)S(1)} %get-tuple-element.17.base), custom_call_target="tpu_custom_call" | custom-call | flops 58720256 | bytes 3670016 | tf_op jit(solution)/shard_map/fit_theirs/pallas_call | solution.py:231
  50.1 1.4 %collective-permute-start.3 = (f32[16,448]{1,0:T(8,128)S(1)}, f32[16,448]{1,0:T(8,128)S(1)}, u32[]{:S(2)}, u32[]{:S(2)}) collective-permute-start(f32[16,448]{1,0:T(8,128)S(1)} %fit_theirs.1), channel_id=1, source_target_pairs={{0,128},{64,192},{128,0},{192,64},{1,129},{65,193},{129,1},{193,65... | collective-permute-start | bytes 86024 | tf_op jit(solution)/shard_map/ppermute | solution.py:242
  51.5 2.1 %collective-permute-start.4 = (f32[16,448]{1,0:T(8,128)S(1)}, f32[16,448]{1,0:T(8,128)S(1)}, u32[]{:S(2)}, u32[]{:S(2)}) collective-permute-start(f32[16,448]{1,0:T(8,128)S(1)} %fit_theirs.1), channel_id=1, source_target_pairs={{0,64},{64,128},{128,192},{192,0},{1,65},{65,129},{129,193},{193,1... | collective-permute-start | bytes 86024 | tf_op jit(solution)/shard_map/ppermute | solution.py:242
  53.6 0.0 collective-permute-start.5
  53.6 0.2 fusion.1
  53.7 1.8 %collective-permute-done.3 = f32[16,448]{1,0:T(8,128)S(1)} collective-permute-done((f32[16,448]{1,0:T(8,128)S(1)}, f32[16,448]{1,0:T(8,128)S(1)}, u32[]{:S(2)}, u32[]{:S(2)}) %collective-permute-start.3) | collective-permute-done | bytes 28704 | tf_op jit(solution)/shard_map/ppermute | solution.py:242
  55.5 0.0 collective-permute-done.4
  55.5 3.2 %collective-permute-done.5 = f32[16,448]{1,0:T(8,128)S(1)} collective-permute-done((f32[16,448]{1,0:T(8,128)S(1)}, f32[16,448]{1,0:T(8,128)S(1)}, u32[]{:S(2)}, u32[]{:S(2)}) %collective-permute-start.5) | collective-permute-done | bytes 28704 | tf_op jit(solution)/shard_map/ppermute | solution.py:242
  58.7 0.6 %fusion.8 = (f32[8,448]{1,0:T(8,128)}, f32[8,448]{1,0:T(8,128)}) fusion(f32[16,448]{1,0:T(8,128)S(1)} %fusion.1, f32[16,448]{1,0:T(8,128)S(1)} %add_multiply_fusion, bf16[16,448]{1,0:T(8,128)(2,1)S(1)} %get-tuple-element.11.stacked), kind=kLoop, calls=%fused_computation.14 | loop fusion | flops 46592 | bytes 100352 | tf_op jit(solution)/shard_map/add | solution.py:262
  (4 shorter events, 0.0 us)
Async XLA Ops:
  3.4 2.4 %collective-permute-start = (f32[33,16,128]{2,1,0:T(8,128)S(1)}, f32[33,16,128]{2,1,0:T(8,128)S(1)}, u32[]{:S(2)}, u32[]{:S(2)}) collective-permute-start(f32[33,16,128]{2,1,0:T(8,128)S(1)} %get-tuple-element.13), channel_id=1, source_target_pairs={{0,1},{1,0},{2,3},{3,2},{4,5},{5,4},{6,7},{7,6},{8,9},{9,8},{10,11... | collective-permute-start | bytes 811016 | tf_op jit(solution)/shard_map/ppermute | solution.py:184
  6.5 22.4 %all-to-all-start = ((bf16[32,16,128]{2,1,0:T(8,128)(2,1)}), bf16[32,16,128]{2,1,0:T(8,128)(2,1)S(1)}, u32[]{:S(2)}, u32[]{:S(2)}) async-start(bf16[32,16,128]{2,1,0:T(8,128)(2,1)} %fusion), calls=%async_computation | async-start | bytes 262144 | tf_op jit(solution)/shard_map/all_to_all | solution.py:202
  18.0 5.1 %collective-permute-start.1 = (f32[16,64]{1,0:T(8,128)S(1)}, f32[16,64]{1,0:T(8,128)S(1)}, u32[]{:S(2)}, u32[]{:S(2)}) collective-permute-start(f32[16,64]{1,0:T(8,128)S(1)} %fusion.9), channel_id=1, source_target_pairs={{0,2},{2,4},{4,6},{6,8},{8,10},{10,12},{12,14},{14,16},{16,18},{18... | collective-permute-start | bytes 12296 | tf_op jit(solution)/shard_map/ppermute | solution.py:201
  29.6 16.0 %all-to-all-start.1 = ((bf16[32,16,128]{2,1,0:T(8,128)(2,1)}), bf16[32,16,128]{2,1,0:T(8,128)(2,1)S(1)}, u32[]{:S(2)}, u32[]{:S(2)}) async-start(bf16[32,16,128]{2,1,0:T(8,128)(2,1)} %weighted.1), calls=%async_computation.1 | async-start | bytes 262144 | tf_op jit(solution)/shard_map/all_to_all | solution.py:212
  35.3 1.3 %collective-permute-start.6 = (f32[16,64]{1,0:T(8,128)S(1)}, f32[16,64]{1,0:T(8,128)S(1)}, u32[]{:S(2)}, u32[]{:S(2)}) collective-permute-start(f32[16,64]{1,0:T(8,128)S(1)} %collective-permute-done.1), channel_id=1, source_target_pairs={{0,1},{1,0},{2,3},{3,2},{4,5},{5,4},{6,7},{7,6},{8,9},{9,8},{10,11... | collective-permute-start | bytes 12296 | tf_op jit(solution)/shard_map/ppermute | solution.py:248
  45.6 3.4 %collective-permute-start.2 = (bf16[32,16,128]{2,1,0:T(8,128)(2,1)S(1)}, bf16[32,16,128]{2,1,0:T(8,128)(2,1)S(1)}, u32[]{:S(2)}, u32[]{:S(2)}) collective-permute-start(bf16[32,16,128]{2,1,0:T(8,128)(2,1)S(1)} %all-to-all-done.1.weighted), channel_id=1, source_target_pairs={{0,1},{1,0},{2,3},{3,2},{4,5},{5,4},{6,7},{7,6},{8,9},{9,8},{10,11... | collective-permute-start | bytes 393224 | tf_op jit(solution)/shard_map/ppermute | solution.py:213
  50.1 5.4 %collective-permute-start.3 = (f32[16,448]{1,0:T(8,128)S(1)}, f32[16,448]{1,0:T(8,128)S(1)}, u32[]{:S(2)}, u32[]{:S(2)}) collective-permute-start(f32[16,448]{1,0:T(8,128)S(1)} %fit_theirs.1), channel_id=1, source_target_pairs={{0,128},{64,192},{128,0},{192,64},{1,129},{65,193},{129,1},{193,65... | collective-permute-start | bytes 86024 | tf_op jit(solution)/shard_map/ppermute | solution.py:242
  51.5 4.0 %collective-permute-start.4 = (f32[16,448]{1,0:T(8,128)S(1)}, f32[16,448]{1,0:T(8,128)S(1)}, u32[]{:S(2)}, u32[]{:S(2)}) collective-permute-start(f32[16,448]{1,0:T(8,128)S(1)} %fit_theirs.1), channel_id=1, source_target_pairs={{0,64},{64,128},{128,192},{192,0},{1,65},{65,129},{129,193},{193,1... | collective-permute-start | bytes 86024 | tf_op jit(solution)/shard_map/ppermute | solution.py:242
  53.6 5.1 %collective-permute-start.5 = (f32[16,448]{1,0:T(8,128)S(1)}, f32[16,448]{1,0:T(8,128)S(1)}, u32[]{:S(2)}, u32[]{:S(2)}) collective-permute-start(f32[16,448]{1,0:T(8,128)S(1)} %fit_theirs.1), channel_id=1, source_target_pairs={{0,192},{64,0},{128,64},{192,128},{1,193},{65,1},{129,65},{193,129... | collective-permute-start | bytes 86024 | tf_op jit(solution)/shard_map/ppermute | solution.py:242

commit v5 on v4

--- a/solution.py
+++ b/solution.py
@@ -55,17 +55,30 @@
             out[i * per_piece + k] = product[:, k * LANES : (k + 1) * LANES]
 
 
-def margins_theirs_kernel(
-    w_ref, d_ref, g_ref, a_ref, theirs, stacked_out, ids_out, w, d, held, small_sems, a_sems
+def margins_kernel(
+    w_ref, d_ref, g_ref, labels_ref, a_ref,
+    theirs, mine, stacked_out, ids_out, targets,
+    w, d, their_half, my_half, small_sems, their_sems, my_sems,
 ):
-    core = lax.rem(lax.axis_index("feat"), 2)
+    me = lax.axis_index("feat")
+    core, chip = lax.rem(me, 2), lax.div(me, 2)
+    share = targets.shape[1]
+    spot = pl.multiple_of(core * my_half.shape[1] + chip * share, LANES)
     small = [
         pltpu.make_async_copy(source, target, small_sems.at[i])
-        for i, (source, target) in enumerate(((w_ref, w), (d_ref, d), (g_ref, ids_out)))
+        for i, (source, target) in enumerate(
+            (
+                (w_ref, w),
+                (d_ref, d),
+                (g_ref, ids_out),
+                (labels_ref.at[:, pl.ds(spot, share)], targets),
+            )
+        )
     ]
     for copy in small:
         copy.start()
-    copies = start_half(a_ref, 1 - core, held, a_sems)
+    their_copies = start_half(a_ref, 1 - core, their_half, their_sems)
+    my_copies = start_half(a_ref, core, my_half, my_sems)
     for copy in small:
         copy.wait()
     stacked = jnp.concatenate([w[...], d[...]], 0)
@@ -84,19 +97,8 @@
         rows = stacked.shape[0]
         theirs[theirs.shape[0] - 1] = sums[:rows] + sums[rows:]
 
-    multiply_half(stacked, copies, held, theirs, sum_groups)
-
-
-def margins_mine_kernel(stacked, labels_ref, a_ref, mine, targets, held, labels_sem, a_sems):
-    me = lax.axis_index("feat")
-    core, chip = lax.rem(me, 2), lax.div(me, 2)
-    copies = start_half(a_ref, core, held, a_sems)
-    share = targets.shape[1]
-    spot = pl.multiple_of(core * held.shape[1] + chip * share, LANES)
-    labels_copy = pltpu.make_async_copy(labels_ref.at[:, pl.ds(spot, share)], targets, labels_sem)
-    labels_copy.start()
-    multiply_half(stacked[...], copies, held, mine)
-    labels_copy.wait()
+    multiply_half(stacked, their_copies, their_half, theirs, sum_groups)
+    multiply_half(stacked, my_copies, my_half, mine)
 
 
 def weighted_kernel(arrived, targets, copies):
@@ -151,51 +153,41 @@
     along += [(2 * i + 3, 2 * i + 1) for i in range(chips - 1)]
     f32, bf16 = jnp.float32, jnp.bfloat16
     vmem, hbm = pl.BlockSpec(memory_space=pltpu.VMEM), pl.BlockSpec(memory_space=pltpu.HBM)
-    held = [pltpu.VMEM((width, half), bf16)]
-    limit = pltpu.CompilerParams(vmem_limit_bytes=16 << 20)
-    half_cost = pl.CostEstimate(
-        flops=2 * rows * width * half, bytes_accessed=2 * width * half, transcendentals=0
-    )
 
     def stay(value):
         return pltpu.with_memory_space_constraint(value, pltpu.HBM)
 
     by_neuron = stay(activations.T)
-    theirs, stacked, ids = pl.pallas_call(
-        margins_theirs_kernel,
+    theirs, mine, stacked, ids, targets = pl.pallas_call(
+        margins_kernel,
         out_shape=[
             jax.ShapeDtypeStruct((chips + 1, rows, share), f32),
+            jax.ShapeDtypeStruct((chips, rows, share), f32),
             jax.ShapeDtypeStruct((rows, width), bf16),
             jax.ShapeDtypeStruct((1, width), jnp.int32),
+            jax.ShapeDtypeStruct((probes, share), jnp.int32),
         ],
-        in_specs=[hbm] * 4,
-        out_specs=[vmem] * 3,
+        in_specs=[hbm] * 5,
+        out_specs=[vmem] * 5,
         scratch_shapes=[
             pltpu.VMEM((probes, width), bf16),
             pltpu.VMEM((probes, width), bf16),
-            *held,
-            pltpu.SemaphoreType.DMA((3,)),
+            pltpu.VMEM((width, half), bf16),
+            pltpu.VMEM((width, half), bf16),
+            pltpu.SemaphoreType.DMA((4,)),
+            pltpu.SemaphoreType.DMA((PIECES,)),
             pltpu.SemaphoreType.DMA((PIECES,)),
         ],
-        compiler_params=limit,
-        cost_estimate=half_cost,
-        name="margins_theirs",
-    )(stay(probe_weights), stay(direction), stay(group_ids[None, :]), by_neuron)
+        compiler_params=pltpu.CompilerParams(vmem_limit_bytes=16 << 20),
+        name="margins",
+    )(
+        stay(probe_weights),
+        stay(direction),
+        stay(group_ids[None, :]),
+        stay(labels),
+        by_neuron,
+    )
     from_pair = lax.ppermute(theirs, "feat", swap)
-    mine, targets = pl.pallas_call(
-        margins_mine_kernel,
-        out_shape=[
-            jax.ShapeDtypeStruct((chips, rows, share), f32),
-            jax.ShapeDtypeStruct((probes, share), jnp.int32),
-        ],
-        in_specs=[vmem, hbm, hbm],
-        out_specs=[vmem] * 2,
-        scratch_shapes=[*held, pltpu.SemaphoreType.DMA, pltpu.SemaphoreType.DMA((PIECES,))],
-        compiler_params=limit,
-        cost_estimate=half_cost,
-        name="margins_mine",
-    )(stacked, stay(labels), by_neuron)
-
     stats = theirs[chips, :, :GROUPS] + from_pair[chips, :, :GROUPS]
     outgoing = (mine + from_pair[:chips]).astype(bf16)
     beside = lax.ppermute(stats, "feat", along)
@@ -212,7 +204,11 @@
     weighted_mine = lax.all_to_all(copies, "feat", 0, 0, axis_index_groups=by_core)
     weighted_theirs = lax.ppermute(weighted_mine, "feat", swap)
 
-    flat = pltpu.VMEM((rows, half), bf16)
+    flat, held = pltpu.VMEM((rows, half), bf16), [pltpu.VMEM((width, half), bf16)]
+    limit = pltpu.CompilerParams(vmem_limit_bytes=16 << 20)
+    half_cost = pl.CostEstimate(
+        flops=2 * rows * width * half, bytes_accessed=4 * width * half, transcendentals=0
+    )
     fit_mine, a_theirs = pl.pallas_call(
         fit_mine_kernel,
         out_shape=[jax.ShapeDtypeStruct((rows, width), f32), *held],
@@ -228,6 +224,7 @@
         cost_estimate=half_cost,
         name="fit_mine",
     )(weighted_mine, by_neuron)
+    weighted_theirs, beside = lax.optimization_barrier((weighted_theirs, beside))
     local_fit = pl.pallas_call(
         fit_theirs_kernel,
         out_shape=jax.ShapeDtypeStruct((rows, width), f32),

time: 59.7 us -> 60.3 us (1.010)
  blocking collectives: 0 us -> 16.1 us
  waiting for transfers between devices: 22.4 us -> 13.4 us
  starting transfers between devices: 24.5 us -> 19.4 us
  Pallas kernels: 10.2 us -> 9.03 us
    all_to_all x0 -> x1, blocking collectives: none -> 16.1 us  [local(): lax.all_to_all(copies, 'feat', 0, 0, axis_index_groups=by_core)]
    all_to_all x1 -> x0, waiting for transfers between devices: 9.09 us -> none  [local(): lax.all_to_all(copies, 'feat', 0, 0, axis_index_groups=by_core)]
    all_to_all x1 -> x0, starting transfers between devices: 5.63 us -> none  [local(): lax.all_to_all(copies, 'feat', 0, 0, axis_index_groups=by_core)]
    ppermute x1, waiting for transfers between devices: 0.01 us -> 1.53 us  [local(): from_pair = lax.ppermute(theirs, 'feat', swap)]
    ppermute x1, waiting for transfers between devices: 1.16 us -> 0.01 us  [local(): totals = stats + (beside + lax.ppermute(beside, 'feat', swap))]
    pallas_call x1, Pallas kernels: 0.72 us -> 0.06 us  [local(): pl.pallas_call(weighted_kernel, out_shape=jax.ShapeDtypeStruct((chips, ro...]
    pallas_call x2 -> x1, Pallas kernels: 5.04 us -> 4.57 us  [local(): pl.pallas_call(margins_kernel, out_shape=[jax.ShapeDtypeStruct((chips + 1...]
  transfers between devices with their start and end apart: 9 -> 8, of which waited for: 6 -> 5; matrix products, arithmetic and copies ran while one was open for 0% -> 0% of each run, Pallas kernels for 10% -> 7%
where the time goes in v5:
time: 60.3 us; the launch traced here: 60.1 us
  starting transfers between devices  19.4 us (32%)
  blocking collectives  16.1 us (27%)
  waiting for transfers between devices  13.4 us (22%)
  Pallas kernels  9.03 us (15%)
  other arithmetic  1.34 us (2%)
  between operations  0.71 us (1%)
    all_to_all x1, blocking collectives, local(): lax.all_to_all(copies, 'feat', 0, 0, axis_index_groups=by_core)  16.1 us
    all_to_all x1, starting transfers between devices, local(): arrived = lax.all_to_all(outgoing, 'feat', 0, 0, axis_index_groups=by_core)  11.5 us
    all_to_all x1, waiting for transfers between devices, local(): arrived = lax.all_to_all(outgoing, 'feat', 0, 0, axis_index_groups=by_core)  5.54 us
    ppermute x3, waiting for transfers between devices, local(): lax.ppermute(local_fit, 'tok', [(i, (i + hop) % planes) for i in range(pl...  4.94 us
    pallas_call x1, Pallas kernels, local(): pl.pallas_call(margins_kernel, out_shape=[jax.ShapeDtypeStruct((chips + 1...  4.57 us
    ppermute x1, starting transfers between devices, local(): beside = lax.ppermute(stats, 'feat', along)  3.69 us
    ppermute x3, starting transfers between devices, local(): lax.ppermute(local_fit, 'tok', [(i, (i + hop) % planes) for i in range(pl...  3.52 us
    pallas_call x1, Pallas kernels, local(): pl.pallas_call(fit_mine_kernel, out_shape=[jax.ShapeDtypeStruct((rows, wi...  3.34 us
  transfers between devices with their start and end apart: 8, of which 5 were waited for; matrix products, arithmetic and copies ran while one was open for 0% of the time, Pallas kernels for 7%

profile of v5, /device:TPU:6, one launch (start us, length us, event | category | flops | bytes accessed | tf_op | source)
XLA Modules:
  0.0 60.1 jit_solution(14172082199619448851)
XLA Ops:
  0.6 4.6 %margins.1 = (f32[33,16,128]{2,1,0:T(8,128)S(1)}, f32[32,16,128]{2,1,0:T(8,128)S(1)}, bf16[16,448]{1,0:T(8,128)(2,1)S(1)}, s32[1,448]{1,0:T(1,128)S(1)}, s32[8,128]{1,0:T(8,128)S(1)}) custom-call(bf16[8,448]{1,0:T(8,128)(2,1)} %w_ref.1, bf16[8,448]{1,0:T(8,128)(2,1)} %d_ref.1, s32[1,448]{1,0:T(1,128)} %bitcast.8, s32[8,8192]{1,0:T(8,128)} %labels_ref.1, ...), custom_call_target="tpu_custom_call" | custom-call | tf_op jit(solution)/shard_map/margins/pallas_call | solution.py:161
  5.2 0.1 collective-permute-start
  5.3 1.5 %collective-permute-done = f32[33,16,128]{2,1,0:T(8,128)S(1)} collective-permute-done((f32[33,16,128]{2,1,0:T(8,128)S(1)}, f32[33,16,128]{2,1,0:T(8,128)S(1)}, u32[]{:S(2)}, u32[]{:S(2)}) %collective-permute-start) | collective-permute-done | bytes 270368 | tf_op jit(solution)/shard_map/ppermute | solution.py:190
  6.8 0.7 %fusion = bf16[32,16,128]{2,1,0:T(8,128)(2,1)} fusion(f32[32,16,128]{2,1,0:T(8,128)S(1)} %get-tuple-element.13, f32[33,16,128]{2,1,0:T(8,128)S(1)} %collective-permute-done), kind=kLoop, calls=%fused_computation.1 | loop fusion | flops 131072 | bytes 655360 | tf_op jit(solution)/shard_map/convert_element_type | solution.py:192
  7.5 11.5 %all-to-all-start = ((bf16[32,16,128]{2,1,0:T(8,128)(2,1)}), bf16[32,16,128]{2,1,0:T(8,128)(2,1)S(1)}, u32[]{:S(2)}, u32[]{:S(2)}) async-start(bf16[32,16,128]{2,1,0:T(8,128)(2,1)} %fusion), calls=%async_computation | async-start | bytes 262144 | tf_op jit(solution)/shard_map/all_to_all | solution.py:194
  19.0 3.7 %collective-permute-start.1 = (f32[16,64]{1,0:T(8,128)S(1)}, f32[16,64]{1,0:T(8,128)S(1)}, u32[]{:S(2)}, u32[]{:S(2)}) collective-permute-start(f32[16,64]{1,0:T(8,128)S(1)} %fusion.9), channel_id=1, source_target_pairs={{0,2},{2,4},{4,6},{6,8},{8,10},{10,12},{12,14},{14,16},{16,18},{18... | collective-permute-start | bytes 12296 | tf_op jit(solution)/shard_map/ppermute | solution.py:193
  22.7 1.3 %collective-permute-done.1 = f32[16,64]{1,0:T(8,128)S(1)} collective-permute-done((f32[16,64]{1,0:T(8,128)S(1)}, f32[16,64]{1,0:T(8,128)S(1)}, u32[]{:S(2)}, u32[]{:S(2)}) %collective-permute-start.1) | collective-permute-done | bytes 4128 | tf_op jit(solution)/shard_map/ppermute | solution.py:193
  24.1 5.5 %all-to-all-done.arrived = bf16[32,16,128]{2,1,0:T(8,128)(2,1)S(1)} async-done(((bf16[32,16,128]{2,1,0:T(8,128)(2,1)}), bf16[32,16,128]{2,1,0:T(8,128)(2,1)S(1)}, u32[]{:S(2)}, u32[]{:S(2)}) %all-to-all-start) | async-done | bytes 131104 | tf_op jit(solution)/shard_map/all_to_all | solution.py:194
  29.6 0.1 weighted.1
  29.7 16.1 %all_to_all.10.weighted = bf16[32,16,128]{2,1,0:T(8,128)(2,1)S(1)} all-to-all(bf16[32,16,128]{2,1,0:T(8,128)(2,1)S(1)} %weighted.1), channel_id=1, replica_groups={{0,2,4,6,8,10,12,14,16,18,20,22,24,26,28,30,32,34,36,38,40,42,44,46,48,..., dimensions={0} | all-to-all | bytes 262144 | tf_op jit(solution)/shard_map/all_to_all | solution.py:204
  45.8 0.0 collective-permute-start.2
  45.8 3.3 %fit_mine.1 = (f32[16,448]{1,0:T(8,128)S(1)}, bf16[448,4096]{1,0:T(8,128)(2,1)S(1)}) custom-call(bf16[32,16,128]{2,1,0:T(8,128)(2,1)S(1)} %all_to_all.10.weighted, bf16[448,8192]{1,0:T(8,128)(2,1)} %bitcast.7), custom_call_target="tpu_custom_call" | custom-call | flops 58720256 | bytes 7340032 | tf_op jit(solution)/shard_map/fit_mine/pallas_call | solution.py:212
  49.1 0.0 collective-permute-done.2.weighted
  49.1 0.6 collective-permute-start.6
  49.7 1.1 %fit_theirs.1 = f32[16,448]{1,0:T(8,128)S(1)} custom-call(bf16[32,16,128]{2,1,0:T(8,128)(2,1)S(1)} %collective-permute-done.2.weighted, bf16[448,4096]{1,0:T(8,128)(2,1)S(1)} %get-tuple-element.19.theirs, f32[16,448]{1,0:T(8,128)S(1)} %get-tuple-element.20.base), custom_call_target="tpu_custom_call" | custom-call | flops 58720256 | bytes 7340032 | tf_op jit(solution)/shard_map/fit_theirs/pallas_call | solution.py:228
  50.8 1.4 %collective-permute-start.3 = (f32[16,448]{1,0:T(8,128)S(1)}, f32[16,448]{1,0:T(8,128)S(1)}, u32[]{:S(2)}, u32[]{:S(2)}) collective-permute-start(f32[16,448]{1,0:T(8,128)S(1)} %fit_theirs.1), channel_id=1, source_target_pairs={{0,128},{64,192},{128,0},{192,64},{1,129},{65,193},{129,1},{193,65... | collective-permute-start | bytes 86024 | tf_op jit(solution)/shard_map/ppermute | solution.py:239
  52.2 2.1 %collective-permute-start.4 = (f32[16,448]{1,0:T(8,128)S(1)}, f32[16,448]{1,0:T(8,128)S(1)}, u32[]{:S(2)}, u32[]{:S(2)}) collective-permute-start(f32[16,448]{1,0:T(8,128)S(1)} %fit_theirs.1), channel_id=1, source_target_pairs={{0,64},{64,128},{128,192},{192,0},{1,65},{65,129},{129,193},{193,1... | collective-permute-start | bytes 86024 | tf_op jit(solution)/shard_map/ppermute | solution.py:239
  54.3 0.0 collective-permute-start.5
  54.3 0.0 collective-permute-done.6
  54.3 0.2 fusion.1
  54.5 1.7 %collective-permute-done.3 = f32[16,448]{1,0:T(8,128)S(1)} collective-permute-done((f32[16,448]{1,0:T(8,128)S(1)}, f32[16,448]{1,0:T(8,128)S(1)}, u32[]{:S(2)}, u32[]{:S(2)}) %collective-permute-start.3) | collective-permute-done | bytes 28704 | tf_op jit(solution)/shard_map/ppermute | solution.py:239
  56.2 0.0 collective-permute-done.4
  56.2 3.2 %collective-permute-done.5 = f32[16,448]{1,0:T(8,128)S(1)} collective-permute-done((f32[16,448]{1,0:T(8,128)S(1)}, f32[16,448]{1,0:T(8,128)S(1)}, u32[]{:S(2)}, u32[]{:S(2)}) %collective-permute-start.5) | collective-permute-done | bytes 28704 | tf_op jit(solution)/shard_map/ppermute | solution.py:239
  59.4 0.6 %fusion.8 = (f32[8,448]{1,0:T(8,128)}, f32[8,448]{1,0:T(8,128)}) fusion(f32[16,448]{1,0:T(8,128)S(1)} %fusion.1, f32[16,448]{1,0:T(8,128)S(1)} %add_multiply_fusion, bf16[16,448]{1,0:T(8,128)(2,1)S(1)} %get-tuple-element.21), kind=kLoop, calls=%fused_computation.14 | loop fusion | flops 46592 | bytes 100352 | tf_op jit(solution)/shard_map/add | solution.py:259
  (4 shorter events, 0.0 us)
Async XLA Ops:
  5.2 1.6 %collective-permute-start = (f32[33,16,128]{2,1,0:T(8,128)S(1)}, f32[33,16,128]{2,1,0:T(8,128)S(1)}, u32[]{:S(2)}, u32[]{:S(2)}) collective-permute-start(f32[33,16,128]{2,1,0:T(8,128)S(1)} %get-tuple-element.14), channel_id=1, source_target_pairs={{0,1},{1,0},{2,3},{3,2},{4,5},{5,4},{6,7},{7,6},{8,9},{9,8},{10,11... | collective-permute-start | bytes 811016 | tf_op jit(solution)/shard_map/ppermute | solution.py:190
  7.5 22.1 %all-to-all-start = ((bf16[32,16,128]{2,1,0:T(8,128)(2,1)}), bf16[32,16,128]{2,1,0:T(8,128)(2,1)S(1)}, u32[]{:S(2)}, u32[]{:S(2)}) async-start(bf16[32,16,128]{2,1,0:T(8,128)(2,1)} %fusion), calls=%async_computation | async-start | bytes 262144 | tf_op jit(solution)/shard_map/all_to_all | solution.py:194
  19.0 5.1 %collective-permute-start.1 = (f32[16,64]{1,0:T(8,128)S(1)}, f32[16,64]{1,0:T(8,128)S(1)}, u32[]{:S(2)}, u32[]{:S(2)}) collective-permute-start(f32[16,64]{1,0:T(8,128)S(1)} %fusion.9), channel_id=1, source_target_pairs={{0,2},{2,4},{4,6},{6,8},{8,10},{10,12},{12,14},{14,16},{16,18},{18... | collective-permute-start | bytes 12296 | tf_op jit(solution)/shard_map/ppermute | solution.py:193
  45.8 3.4 %collective-permute-start.2 = (bf16[32,16,128]{2,1,0:T(8,128)(2,1)S(1)}, bf16[32,16,128]{2,1,0:T(8,128)(2,1)S(1)}, u32[]{:S(2)}, u32[]{:S(2)}) collective-permute-start(bf16[32,16,128]{2,1,0:T(8,128)(2,1)S(1)} %all_to_all.10.weighted), channel_id=1, source_target_pairs={{0,1},{1,0},{2,3},{3,2},{4,5},{5,4},{6,7},{7,6},{8,9},{9,8},{10,11... | collective-permute-start | bytes 393224 | tf_op jit(solution)/shard_map/ppermute | solution.py:205
  49.1 5.2 %collective-permute-start.6 = (f32[16,64]{1,0:T(8,128)S(1)}, f32[16,64]{1,0:T(8,128)S(1)}, u32[]{:S(2)}, u32[]{:S(2)}) collective-permute-start(f32[16,64]{1,0:T(8,128)S(1)} %collective-permute-done.1), channel_id=1, source_target_pairs={{0,1},{1,0},{2,3},{3,2},{4,5},{5,4},{6,7},{7,6},{8,9},{9,8},{10,11... | collective-permute-start | bytes 12296 | tf_op jit(solution)/shard_map/ppermute | solution.py:245
  50.8 5.4 %collective-permute-start.3 = (f32[16,448]{1,0:T(8,128)S(1)}, f32[16,448]{1,0:T(8,128)S(1)}, u32[]{:S(2)}, u32[]{:S(2)}) collective-permute-start(f32[16,448]{1,0:T(8,128)S(1)} %fit_theirs.1), channel_id=1, source_target_pairs={{0,128},{64,192},{128,0},{192,64},{1,129},{65,193},{129,1},{193,65... | collective-permute-start | bytes 86024 | tf_op jit(solution)/shard_map/ppermute | solution.py:239
  52.2 4.0 %collective-permute-start.4 = (f32[16,448]{1,0:T(8,128)S(1)}, f32[16,448]{1,0:T(8,128)S(1)}, u32[]{:S(2)}, u32[]{:S(2)}) collective-permute-start(f32[16,448]{1,0:T(8,128)S(1)} %fit_theirs.1), channel_id=1, source_target_pairs={{0,64},{64,128},{128,192},{192,0},{1,65},{65,129},{129,193},{193,1... | collective-permute-start | bytes 86024 | tf_op jit(solution)/shard_map/ppermute | solution.py:239
  54.3 5.1 %collective-permute-start.5 = (f32[16,448]{1,0:T(8,128)S(1)}, f32[16,448]{1,0:T(8,128)S(1)}, u32[]{:S(2)}, u32[]{:S(2)}) collective-permute-start(f32[16,448]{1,0:T(8,128)S(1)} %fit_theirs.1), channel_id=1, source_target_pairs={{0,192},{64,0},{128,64},{192,128},{1,193},{65,1},{129,65},{193,129... | collective-permute-start | bytes 86024 | tf_op jit(solution)/shard_map/ppermute | solution.py:239

commit v6 on v4

--- a/solution.py
+++ b/solution.py
@@ -36,7 +36,7 @@
         copy = pltpu.make_async_copy(
             a_ref.at[:, pl.ds(start, piece)], held.at[:, pl.ds(i * piece, piece)], sems.at[i]
         )
-        copy.start()
+        copy.start(priority=1)
         copies.append(copy)
     return copies
 
@@ -56,7 +56,9 @@
 
 
 def margins_theirs_kernel(
-    w_ref, d_ref, g_ref, a_ref, theirs, stacked_out, ids_out, w, d, held, small_sems, a_sems
+    w_ref, d_ref, g_ref, a_ref,
+    theirs, stats, stacked_out, ids_out,
+    w, d, held, small_sems, a_sems,
 ):
     core = lax.rem(lax.axis_index("feat"), 2)
     small = [
@@ -82,7 +84,7 @@
         member = (number == ids_out[...]).astype(jnp.float32).astype(jnp.bfloat16)
         sums = transposed_dot(jnp.concatenate([high, low], 0), member)
         rows = stacked.shape[0]
-        theirs[theirs.shape[0] - 1] = sums[:rows] + sums[rows:]
+        stats[...] = sums[:rows] + sums[rows:]
 
     multiply_half(stacked, copies, held, theirs, sum_groups)
 
@@ -161,15 +163,16 @@
         return pltpu.with_memory_space_constraint(value, pltpu.HBM)
 
     by_neuron = stay(activations.T)
-    theirs, stacked, ids = pl.pallas_call(
+    theirs, stats, stacked, ids = pl.pallas_call(
         margins_theirs_kernel,
         out_shape=[
-            jax.ShapeDtypeStruct((chips + 1, rows, share), f32),
+            jax.ShapeDtypeStruct((chips, rows, share), f32),
+            jax.ShapeDtypeStruct((rows, LANES), f32),
             jax.ShapeDtypeStruct((rows, width), bf16),
             jax.ShapeDtypeStruct((1, width), jnp.int32),
         ],
         in_specs=[hbm] * 4,
-        out_specs=[vmem] * 3,
+        out_specs=[vmem] * 4,
         scratch_shapes=[
             pltpu.VMEM((probes, width), bf16),
             pltpu.VMEM((probes, width), bf16),
@@ -181,6 +184,9 @@
         cost_estimate=half_cost,
         name="margins_theirs",
     )(stay(probe_weights), stay(direction), stay(group_ids[None, :]), by_neuron)
+    stats = stats + lax.ppermute(stats, "feat", swap)
+    stacked, theirs, stats = lax.optimization_barrier((stacked, theirs, stats))
+    beside = lax.ppermute(stats, "feat", along)
     from_pair = lax.ppermute(theirs, "feat", swap)
     mine, targets = pl.pallas_call(
         margins_mine_kernel,
@@ -196,11 +202,8 @@
         name="margins_mine",
     )(stacked, stay(labels), by_neuron)
 
-    stats = theirs[chips, :, :GROUPS] + from_pair[chips, :, :GROUPS]
-    outgoing = (mine + from_pair[:chips]).astype(bf16)
-    beside = lax.ppermute(stats, "feat", along)
+    outgoing, beside = lax.optimization_barrier(((mine + from_pair).astype(bf16), beside))
     arrived = lax.all_to_all(outgoing, "feat", 0, 0, axis_index_groups=by_core)
-    arrived, beside = lax.optimization_barrier((arrived, beside))
     copies = pl.pallas_call(
         weighted_kernel,
         out_shape=jax.ShapeDtypeStruct((chips, rows, share), bf16),
@@ -238,6 +241,7 @@
         cost_estimate=half_cost,
         name="fit_theirs",
     )(weighted_theirs, pltpu.with_memory_space_constraint(a_theirs, pltpu.VMEM), fit_mine)
+    local_fit, beside = lax.optimization_barrier((local_fit, beside))
     one, two, three = (
         lax.ppermute(local_fit, "tok", [(i, (i + hop) % planes) for i in range(planes)])
         for hop in (1, 2, 3)
@@ -245,7 +249,7 @@
     fitted = (local_fit + two) + (one + three)
     fitted = fitted / math.sqrt(tokens * planes)
 
-    totals = stats + (beside + lax.ppermute(beside, "feat", swap))
+    totals = (stats + (beside + lax.ppermute(beside, "feat", swap)))[:, :GROUPS]
     wide_weights = stacked[:probes].astype(f32)
     wide_direction = stacked[probes:].astype(f32)
     member = (ids == jnp.arange(GROUPS, dtype=jnp.int32)[:, None]).astype(f32)

time: 59.7 us -> 61.2 us (1.025)
  blocking collectives: 0 us -> 36 us
  starting transfers between devices: 24.5 us -> 8.03 us
  waiting for transfers between devices: 22.4 us -> 6.22 us
  Pallas kernels: 10.2 us -> 9.18 us
  other arithmetic: 1.35 us -> 0.69 us
    all_to_all x0 -> x2, blocking collectives: none -> 36 us  [the longest x1 22.2 us: local(): arrived = lax.all_to_all(outgoing, 'feat', 0, 0, axis_index_groups=by_core)]
    all_to_all x2 -> x0, starting transfers between devices: 17.1 us -> none  [the longest x1 11.5 us: local(): arrived = lax.all_to_all(outgoing, 'feat', 0, 0, axis_index_groups=by_core)]
    all_to_all x2 -> x0, waiting for transfers between devices: 15 us -> none  [the longest x1 9.09 us: local(): lax.all_to_all(copies, 'feat', 0, 0, axis_index_groups=by_core)]
    ppermute x1, waiting for transfers between devices: 1.35 us -> 0.01 us  [local(): beside = lax.ppermute(stats, 'feat', along)]
    pallas_call x1, Pallas kernels: 0.72 us -> 0.06 us  [local(): pl.pallas_call(weighted_kernel, out_shape=jax.ShapeDtypeStruct((chips, ro...]
    convert_element_type x1, other arithmetic: 0.69 us -> 0.04 us  [local(): (mine + from_pair).astype(bf16)]
  transfers between devices with their start and end apart: 9 -> 8, of which waited for: 6 -> 3; matrix products, arithmetic and copies ran while one was open for 0% -> 0% of each run, Pallas kernels for 10% -> 9%
where the time goes in v6:
time: 61.2 us; the launch traced here: 61 us
  blocking collectives  36 us (59%)
  Pallas kernels  9.18 us (15%)
  starting transfers between devices  8.03 us (13%)
  waiting for transfers between devices  6.22 us (10%)
  between operations  0.72 us (1%)
  other arithmetic  0.69 us (1%)
    all_to_all x1, blocking collectives, local(): arrived = lax.all_to_all(outgoing, 'feat', 0, 0, axis_index_groups=by_core)  22.2 us
    all_to_all x1, blocking collectives, local(): lax.all_to_all(copies, 'feat', 0, 0, axis_index_groups=by_core)  13.8 us
    ppermute x3, waiting for transfers between devices, local(): lax.ppermute(local_fit, 'tok', [(i, (i + hop) % planes) for i in range(pl...  5.05 us
    ppermute x1, starting transfers between devices, local(): beside = lax.ppermute(stats, 'feat', along)  3.81 us
    ppermute x3, starting transfers between devices, local(): lax.ppermute(local_fit, 'tok', [(i, (i + hop) % planes) for i in range(pl...  3.43 us
    pallas_call x1, Pallas kernels, local(): pl.pallas_call(fit_mine_kernel, out_shape=[jax.ShapeDtypeStruct((rows, wi...  3.34 us
    pallas_call x1, Pallas kernels, local(): pl.pallas_call(margins_theirs_kernel, out_shape=[jax.ShapeDtypeStruct((ch...  2.4 us
    pallas_call x1, Pallas kernels, local(): pl.pallas_call(margins_mine_kernel, out_shape=[jax.ShapeDtypeStruct((chip...  2.33 us
  transfers between devices with their start and end apart: 8, of which 3 were waited for; matrix products, arithmetic and copies ran while one was open for 0% of the time, Pallas kernels for 9%

profile of v6, /device:TPU:6, one launch (start us, length us, event | category | flops | bytes accessed | tf_op | source)
XLA Modules:
  0.0 61.0 jit_solution(14171262624055380387)
XLA Ops:
  0.6 2.4 %margins_theirs.1 = (f32[32,16,128]{2,1,0:T(8,128)S(1)}, f32[16,128]{1,0:T(8,128)S(1)}, bf16[16,448]{1,0:T(8,128)(2,1)S(1)}, s32[1,448]{1,0:T(1,128)S(1)}) custom-call(bf16[8,448]{1,0:T(8,128)(2,1)} %w_ref.1, bf16[8,448]{1,0:T(8,128)(2,1)} %d_ref.1, s32[1,448]{1,0:T(1,128)} %bitcast.7, bf16[448,8192]{1,0:T(8,128)(2,1)} %bitcast.4), custom_call_target="tpu_custom_call" | custom-call | flops 58720256 | bytes 3670016 | tf_op jit(solution)/shard_map/margins_theirs/pallas_call | solution.py:166
  3.0 0.1 collective-permute-start
  3.1 1.2 %collective-permute-done = f32[16,128]{1,0:T(8,128)S(1)} collective-permute-done((f32[16,128]{1,0:T(8,128)S(1)}, f32[16,128]{1,0:T(8,128)S(1)}, u32[]{:S(2)}, u32[]{:S(2)}) %collective-permute-start) | collective-permute-done | bytes 8224 | tf_op jit(solution)/shard_map/ppermute | solution.py:187
  4.3 0.2 collective-permute-start.1
  4.5 3.8 %collective-permute-start.2 = (f32[16,128]{1,0:T(8,128)S(1)}, f32[16,128]{1,0:T(8,128)S(1)}, u32[]{:S(2)}, u32[]{:S(2)}) collective-permute-start(f32[16,128]{1,0:T(8,128)S(1)} %add.33), channel_id=1, source_target_pairs={{0,2},{2,4},{4,6},{6,8},{8,10},{10,12},{12,14},{14,16},{16,18},{18... | collective-permute-start | bytes 24584 | tf_op jit(solution)/shard_map/ppermute | solution.py:189
  8.3 2.3 %margins_mine.1 = (f32[32,16,128]{2,1,0:T(8,128)S(1)}, s32[8,128]{1,0:T(8,128)S(1)}) custom-call(bf16[16,448]{1,0:T(8,128)(2,1)S(1)} %get-tuple-element.20.stacked, s32[8,8192]{1,0:T(8,128)} %labels_ref.1, bf16[448,8192]{1,0:T(8,128)(2,1)} %bitcast.5), custom_call_target="tpu_custom_call" | custom-call | flops 58720256 | bytes 3670016 | tf_op jit(solution)/shard_map/margins_mine/pallas_call | solution.py:191
  10.6 0.0 collective-permute-done.1
  10.7 0.0 collective-permute-done.2
  10.7 22.2 %all_to_all.10.arrived = bf16[32,16,128]{2,1,0:T(8,128)(2,1)S(1)} all-to-all(bf16[32,16,128]{2,1,0:T(8,128)(2,1)S(1)} %add_convert_fusion), channel_id=1, replica_groups={{0,2,4,6,8,10,12,14,16,18,20,22,24,26,28,30,32,34,36,38,40,42,44,46,48,..., dimensions={0} | all-to-all | bytes 262144 | tf_op jit(solution)/shard_map/all_to_all | solution.py:206
  32.9 0.1 weighted.1
  32.9 13.8 %all_to_all.11.weighted = bf16[32,16,128]{2,1,0:T(8,128)(2,1)S(1)} all-to-all(bf16[32,16,128]{2,1,0:T(8,128)(2,1)S(1)} %weighted.1), channel_id=1, replica_groups={{0,2,4,6,8,10,12,14,16,18,20,22,24,26,28,30,32,34,36,38,40,42,44,46,48,..., dimensions={0} | all-to-all | bytes 262144 | tf_op jit(solution)/shard_map/all_to_all | solution.py:215
  46.7 0.0 collective-permute-start.3
  46.7 3.3 %fit_mine.1 = (f32[16,448]{1,0:T(8,128)S(1)}, bf16[448,4096]{1,0:T(8,128)(2,1)S(1)}) custom-call(bf16[32,16,128]{2,1,0:T(8,128)(2,1)S(1)} %all_to_all.11.weighted, bf16[448,8192]{1,0:T(8,128)(2,1)} %bitcast.6), custom_call_target="tpu_custom_call" | custom-call | flops 58720256 | bytes 3670016 | tf_op jit(solution)/shard_map/fit_mine/pallas_call | solution.py:219
  50.1 0.0 collective-permute-done.3.weighted
  50.1 1.1 %fit_theirs.1 = f32[16,448]{1,0:T(8,128)S(1)} custom-call(bf16[32,16,128]{2,1,0:T(8,128)(2,1)S(1)} %collective-permute-done.3.weighted, bf16[448,4096]{1,0:T(8,128)(2,1)S(1)} %get-tuple-element.26.theirs, f32[16,448]{1,0:T(8,128)S(1)} %get-tuple-element.27.base), custom_call_target="tpu_custom_call" | custom-call | flops 58720256 | bytes 3670016 | tf_op jit(solution)/shard_map/fit_theirs/pallas_call | solution.py:234
  51.1 0.5 collective-permute-start.7
  51.7 0.8 %collective-permute-start.6 = (f32[16,448]{1,0:T(8,128)S(1)}, f32[16,448]{1,0:T(8,128)S(1)}, u32[]{:S(2)}, u32[]{:S(2)}) collective-permute-start(f32[16,448]{1,0:T(8,128)S(1)} %fit_theirs.1), channel_id=1, source_target_pairs={{0,192},{64,0},{128,64},{192,128},{1,193},{65,1},{129,65},{193,129... | collective-permute-start | bytes 86024 | tf_op jit(solution)/shard_map/ppermute | solution.py:246
  52.5 2.4 %collective-permute-start.5 = (f32[16,448]{1,0:T(8,128)S(1)}, f32[16,448]{1,0:T(8,128)S(1)}, u32[]{:S(2)}, u32[]{:S(2)}) collective-permute-start(f32[16,448]{1,0:T(8,128)S(1)} %fit_theirs.1), channel_id=1, source_target_pairs={{0,64},{64,128},{128,192},{192,0},{1,65},{65,129},{129,193},{193,1... | collective-permute-start | bytes 86024 | tf_op jit(solution)/shard_map/ppermute | solution.py:246
  54.9 0.2 collective-permute-start.4
  55.1 0.0 collective-permute-done.7
  55.1 0.2 fusion
  55.3 1.5 %collective-permute-done.6 = f32[16,448]{1,0:T(8,128)S(1)} collective-permute-done((f32[16,448]{1,0:T(8,128)S(1)}, f32[16,448]{1,0:T(8,128)S(1)}, u32[]{:S(2)}, u32[]{:S(2)}) %collective-permute-start.6) | collective-permute-done | bytes 28704 | tf_op jit(solution)/shard_map/ppermute | solution.py:246
  56.8 0.0 collective-permute-done.5
  56.8 3.5 %collective-permute-done.4 = f32[16,448]{1,0:T(8,128)S(1)} collective-permute-done((f32[16,448]{1,0:T(8,128)S(1)}, f32[16,448]{1,0:T(8,128)S(1)}, u32[]{:S(2)}, u32[]{:S(2)}) %collective-permute-start.4) | collective-permute-done | bytes 28704 | tf_op jit(solution)/shard_map/ppermute | solution.py:246
  60.3 0.6 %fusion.7 = (f32[8,448]{1,0:T(8,128)}, f32[8,448]{1,0:T(8,128)}) fusion(f32[16,448]{1,0:T(8,128)S(1)} %fusion, f32[16,448]{1,0:T(8,128)S(1)} %add_multiply_fusion, bf16[16,448]{1,0:T(8,128)(2,1)S(1)} %get-tuple-element.20.stacked), kind=kLoop, calls=%fused_computation.13 | loop fusion | flops 46592 | bytes 100352 | tf_op jit(solution)/shard_map/add | solution.py:266
  (5 shorter events, 0.1 us)
Async XLA Ops:
  3.0 1.3 %collective-permute-start = (f32[16,128]{1,0:T(8,128)S(1)}, f32[16,128]{1,0:T(8,128)S(1)}, u32[]{:S(2)}, u32[]{:S(2)}) collective-permute-start(f32[16,128]{1,0:T(8,128)S(1)} %get-tuple-element.19), channel_id=1, source_target_pairs={{0,1},{1,0},{2,3},{3,2},{4,5},{5,4},{6,7},{7,6},{8,9},{9,8},{10,11... | collective-permute-start | bytes 24584 | tf_op jit(solution)/shard_map/ppermute | solution.py:187
  4.3 6.3 %collective-permute-start.1 = (f32[32,16,128]{2,1,0:T(8,128)S(1)}, f32[32,16,128]{2,1,0:T(8,128)S(1)}, u32[]{:S(2)}, u32[]{:S(2)}) collective-permute-start(f32[32,16,128]{2,1,0:T(8,128)S(1)} %get-tuple-element.22), channel_id=1, source_target_pairs={{0,1},{1,0},{2,3},{3,2},{4,5},{5,4},{6,7},{7,6},{8,9},{9,8},{10,11... | collective-permute-start | bytes 786440 | tf_op jit(solution)/shard_map/ppermute | solution.py:190
  4.5 6.2 %collective-permute-start.2 = (f32[16,128]{1,0:T(8,128)S(1)}, f32[16,128]{1,0:T(8,128)S(1)}, u32[]{:S(2)}, u32[]{:S(2)}) collective-permute-start(f32[16,128]{1,0:T(8,128)S(1)} %add.33), channel_id=1, source_target_pairs={{0,2},{2,4},{4,6},{6,8},{8,10},{10,12},{12,14},{14,16},{16,18},{18... | collective-permute-start | bytes 24584 | tf_op jit(solution)/shard_map/ppermute | solution.py:189
  46.7 3.4 %collective-permute-start.3 = (bf16[32,16,128]{2,1,0:T(8,128)(2,1)S(1)}, bf16[32,16,128]{2,1,0:T(8,128)(2,1)S(1)}, u32[]{:S(2)}, u32[]{:S(2)}) collective-permute-start(bf16[32,16,128]{2,1,0:T(8,128)(2,1)S(1)} %all_to_all.11.weighted), channel_id=1, source_target_pairs={{0,1},{1,0},{2,3},{3,2},{4,5},{5,4},{6,7},{7,6},{8,9},{9,8},{10,11... | collective-permute-start | bytes 393224 | tf_op jit(solution)/shard_map/ppermute | solution.py:216
  51.1 4.0 %collective-permute-start.7 = (f32[16,128]{1,0:T(8,128)S(1)}, f32[16,128]{1,0:T(8,128)S(1)}, u32[]{:S(2)}, u32[]{:S(2)}) collective-permute-start(f32[16,128]{1,0:T(8,128)S(1)} %collective-permute-done.2), channel_id=1, source_target_pairs={{0,1},{1,0},{2,3},{3,2},{4,5},{5,4},{6,7},{7,6},{8,9},{9,8},{10,11... | collective-permute-start | bytes 24584 | tf_op jit(solution)/shard_map/ppermute | solution.py:252
  51.7 5.1 %collective-permute-start.6 = (f32[16,448]{1,0:T(8,128)S(1)}, f32[16,448]{1,0:T(8,128)S(1)}, u32[]{:S(2)}, u32[]{:S(2)}) collective-permute-start(f32[16,448]{1,0:T(8,128)S(1)} %fit_theirs.1), channel_id=1, source_target_pairs={{0,192},{64,0},{128,64},{192,128},{1,193},{65,1},{129,65},{193,129... | collective-permute-start | bytes 86024 | tf_op jit(solution)/shard_map/ppermute | solution.py:246
  52.5 4.3 %collective-permute-start.5 = (f32[16,448]{1,0:T(8,128)S(1)}, f32[16,448]{1,0:T(8,128)S(1)}, u32[]{:S(2)}, u32[]{:S(2)}) collective-permute-start(f32[16,448]{1,0:T(8,128)S(1)} %fit_theirs.1), channel_id=1, source_target_pairs={{0,64},{64,128},{128,192},{192,0},{1,65},{65,129},{129,193},{193,1... | collective-permute-start | bytes 86024 | tf_op jit(solution)/shard_map/ppermute | solution.py:246
  54.9 5.4 %collective-permute-start.4 = (f32[16,448]{1,0:T(8,128)S(1)}, f32[16,448]{1,0:T(8,128)S(1)}, u32[]{:S(2)}, u32[]{:S(2)}) collective-permute-start(f32[16,448]{1,0:T(8,128)S(1)} %fit_theirs.1), channel_id=1, source_target_pairs={{0,128},{64,192},{128,0},{192,64},{1,129},{65,193},{129,1},{193,65... | collective-permute-start | bytes 86024 | tf_op jit(solution)/shard_map/ppermute | solution.py:246

commit v7 on v4

--- a/solution.py
+++ b/solution.py
@@ -36,7 +36,7 @@
         copy = pltpu.make_async_copy(
             a_ref.at[:, pl.ds(start, piece)], held.at[:, pl.ds(i * piece, piece)], sems.at[i]
         )
-        copy.start()
+        copy.start(priority=1)
         copies.append(copy)
     return copies
 
@@ -147,8 +147,8 @@
     share = half // chips
     by_core = [[2 * i + side for i in range(chips)] for side in range(2)]
     swap = [(i, i ^ 1) for i in range(devices)]
-    along = [(2 * i, 2 * i + 2) for i in range(chips - 1)]
-    along += [(2 * i + 3, 2 * i + 1) for i in range(chips - 1)]
+    along = [(2 * i, (2 * i + 2) % devices) for i in range(chips)]
+    along += [((2 * i + 3) % devices, 2 * i + 1) for i in range(chips)]
     f32, bf16 = jnp.float32, jnp.bfloat16
     vmem, hbm = pl.BlockSpec(memory_space=pltpu.VMEM), pl.BlockSpec(memory_space=pltpu.HBM)
     held = [pltpu.VMEM((width, half), bf16)]
@@ -238,6 +238,7 @@
         cost_estimate=half_cost,
         name="fit_theirs",
     )(weighted_theirs, pltpu.with_memory_space_constraint(a_theirs, pltpu.VMEM), fit_mine)
+    local_fit, beside = lax.optimization_barrier((local_fit, beside))
     one, two, three = (
         lax.ppermute(local_fit, "tok", [(i, (i + hop) % planes) for i in range(planes)])
         for hop in (1, 2, 3)

time: 59.7 us -> 57.2 us (0.958)
  blocking collectives: 0 us -> 14 us
  waiting for transfers between devices: 22.4 us -> 14.1 us
  starting transfers between devices: 24.5 us -> 17.4 us
  Pallas kernels: 10.2 us -> 9.18 us
    all_to_all x0 -> x1, blocking collectives: none -> 14 us  [local(): lax.all_to_all(copies, 'feat', 0, 0, axis_index_groups=by_core)]
    all_to_all x1 -> x0, waiting for transfers between devices: 9.09 us -> none  [local(): lax.all_to_all(copies, 'feat', 0, 0, axis_index_groups=by_core)]
    all_to_all x1 -> x0, starting transfers between devices: 5.63 us -> none  [local(): lax.all_to_all(copies, 'feat', 0, 0, axis_index_groups=by_core)]
    ppermute x1, waiting for transfers between devices: 1.35 us -> 6.45 us  [local(): beside = lax.ppermute(stats, 'feat', along)]
    all_to_all x1, waiting for transfers between devices: 5.86 us -> 2.59 us  [local(): arrived = lax.all_to_all(outgoing, 'feat', 0, 0, axis_index_groups=by_core)]
    ppermute x1, starting transfers between devices: 3.69 us -> 1.87 us  [local(): beside = lax.ppermute(stats, 'feat', along)]
    ppermute x1, waiting for transfers between devices: 1.16 us -> 0.01 us  [local(): totals = stats + (beside + lax.ppermute(beside, 'feat', swap))]
    pallas_call x1, Pallas kernels: 0.72 us -> 0.06 us  [local(): pl.pallas_call(weighted_kernel, out_shape=jax.ShapeDtypeStruct((chips, ro...]
  transfers between devices with their start and end apart: 9 -> 8, of which waited for: 6 -> 4; matrix products, arithmetic and copies ran while one was open for 0% -> 0% of each run, Pallas kernels for 10% -> 10%
where the time goes in v7:
time: 57.2 us; the launch traced here: 56.9 us
  starting transfers between devices  17.4 us (30%)
  waiting for transfers between devices  14.1 us (25%)
  blocking collectives  14 us (24%)
  Pallas kernels  9.18 us (16%)
  other arithmetic  1.34 us (2%)
  between operations  0.71 us (1%)
    all_to_all x1, blocking collectives, local(): lax.all_to_all(copies, 'feat', 0, 0, axis_index_groups=by_core)  14 us
    all_to_all x1, starting transfers between devices, local(): arrived = lax.all_to_all(outgoing, 'feat', 0, 0, axis_index_groups=by_core)  11.5 us
    ppermute x1, waiting for transfers between devices, local(): beside = lax.ppermute(stats, 'feat', along)  6.45 us
    ppermute x3, waiting for transfers between devices, local(): lax.ppermute(local_fit, 'tok', [(i, (i + hop) % planes) for i in range(pl...  5.05 us
    ppermute x3, starting transfers between devices, local(): lax.ppermute(local_fit, 'tok', [(i, (i + hop) % planes) for i in range(pl...  3.43 us
    pallas_call x1, Pallas kernels, local(): pl.pallas_call(fit_mine_kernel, out_shape=[jax.ShapeDtypeStruct((rows, wi...  3.34 us
    all_to_all x1, waiting for transfers between devices, local(): arrived = lax.all_to_all(outgoing, 'feat', 0, 0, axis_index_groups=by_core)  2.59 us
    pallas_call x1, Pallas kernels, local(): pl.pallas_call(margins_theirs_kernel, out_shape=[jax.ShapeDtypeStruct((ch...  2.4 us
  transfers between devices with their start and end apart: 8, of which 4 were waited for; matrix products, arithmetic and copies ran while one was open for 0% of the time, Pallas kernels for 10%

profile of v7, /device:TPU:6, one launch (start us, length us, event | category | flops | bytes accessed | tf_op | source)
XLA Modules:
  0.0 56.9 jit_solution(5243003281094736403)
XLA Ops:
  0.6 2.4 %margins_theirs.1 = (f32[33,16,128]{2,1,0:T(8,128)S(1)}, bf16[16,448]{1,0:T(8,128)(2,1)S(1)}, s32[1,448]{1,0:T(1,128)S(1)}) custom-call(bf16[8,448]{1,0:T(8,128)(2,1)} %w_ref.1, bf16[8,448]{1,0:T(8,128)(2,1)} %d_ref.1, s32[1,448]{1,0:T(1,128)} %bitcast.9, bf16[448,8192]{1,0:T(8,128)(2,1)} %bitcast.6), custom_call_target="tpu_custom_call" | custom-call | flops 58720256 | bytes 3670016 | tf_op jit(solution)/shard_map/margins_theirs/pallas_call | solution.py:164
  3.0 0.1 collective-permute-start
  3.1 2.3 %margins_mine.1 = (f32[32,16,128]{2,1,0:T(8,128)S(1)}, s32[8,128]{1,0:T(8,128)S(1)}) custom-call(bf16[16,448]{1,0:T(8,128)(2,1)S(1)} %get-tuple-element.13.stacked, s32[8,8192]{1,0:T(8,128)} %labels_ref.1, bf16[448,8192]{1,0:T(8,128)(2,1)} %bitcast.7), custom_call_target="tpu_custom_call" | custom-call | flops 58720256 | bytes 3670016 | tf_op jit(solution)/shard_map/margins_mine/pallas_call | solution.py:185
  5.5 0.0 collective-permute-done
  5.5 0.7 %fusion = bf16[32,16,128]{2,1,0:T(8,128)(2,1)} fusion(f32[32,16,128]{2,1,0:T(8,128)S(1)} %get-tuple-element.14, f32[33,16,128]{2,1,0:T(8,128)S(1)} %collective-permute-done), kind=kLoop, calls=%fused_computation.1 | loop fusion | flops 131072 | bytes 655360 | tf_op jit(solution)/shard_map/convert_element_type | solution.py:200
  6.2 11.5 %all-to-all-start = ((bf16[32,16,128]{2,1,0:T(8,128)(2,1)}), bf16[32,16,128]{2,1,0:T(8,128)(2,1)S(1)}, u32[]{:S(2)}, u32[]{:S(2)}) async-start(bf16[32,16,128]{2,1,0:T(8,128)(2,1)} %fusion), calls=%async_computation | async-start | bytes 262144 | tf_op jit(solution)/shard_map/all_to_all | solution.py:202
  17.7 1.9 %collective-permute-start.1 = (f32[16,64]{1,0:T(8,128)S(1)}, f32[16,64]{1,0:T(8,128)S(1)}, u32[]{:S(2)}, u32[]{:S(2)}) collective-permute-start(f32[16,64]{1,0:T(8,128)S(1)} %fusion.9), channel_id=1, source_target_pairs={{0,2},{2,4},{4,6},{6,8},{8,10},{10,12},{12,14},{14,16},{16,18},{18... | collective-permute-start | bytes 12296 | tf_op jit(solution)/shard_map/ppermute | solution.py:201
  19.5 6.5 %collective-permute-done.1 = f32[16,64]{1,0:T(8,128)S(1)} collective-permute-done((f32[16,64]{1,0:T(8,128)S(1)}, f32[16,64]{1,0:T(8,128)S(1)}, u32[]{:S(2)}, u32[]{:S(2)}) %collective-permute-start.1) | collective-permute-done | bytes 4128 | tf_op jit(solution)/shard_map/ppermute | solution.py:201
  26.0 2.6 %all-to-all-done.arrived = bf16[32,16,128]{2,1,0:T(8,128)(2,1)S(1)} async-done(((bf16[32,16,128]{2,1,0:T(8,128)(2,1)}), bf16[32,16,128]{2,1,0:T(8,128)(2,1)S(1)}, u32[]{:S(2)}, u32[]{:S(2)}) %all-to-all-start) | async-done | bytes 131104 | tf_op jit(solution)/shard_map/all_to_all | solution.py:202
  28.6 0.1 weighted.1
  28.6 14.0 %all_to_all.10.weighted = bf16[32,16,128]{2,1,0:T(8,128)(2,1)S(1)} all-to-all(bf16[32,16,128]{2,1,0:T(8,128)(2,1)S(1)} %weighted.1), channel_id=1, replica_groups={{0,2,4,6,8,10,12,14,16,18,20,22,24,26,28,30,32,34,36,38,40,42,44,46,48,..., dimensions={0} | all-to-all | bytes 262144 | tf_op jit(solution)/shard_map/all_to_all | solution.py:212
  42.7 0.0 collective-permute-start.2
  42.7 3.3 %fit_mine.1 = (f32[16,448]{1,0:T(8,128)S(1)}, bf16[448,4096]{1,0:T(8,128)(2,1)S(1)}) custom-call(bf16[32,16,128]{2,1,0:T(8,128)(2,1)S(1)} %all_to_all.10.weighted, bf16[448,8192]{1,0:T(8,128)(2,1)} %bitcast.8), custom_call_target="tpu_custom_call" | custom-call | flops 58720256 | bytes 3670016 | tf_op jit(solution)/shard_map/fit_mine/pallas_call | solution.py:216
  46.0 0.0 collective-permute-done.2.weighted
  46.0 1.1 %fit_theirs.1 = f32[16,448]{1,0:T(8,128)S(1)} custom-call(bf16[32,16,128]{2,1,0:T(8,128)(2,1)S(1)} %collective-permute-done.2.weighted, bf16[448,4096]{1,0:T(8,128)(2,1)S(1)} %get-tuple-element.18.theirs, f32[16,448]{1,0:T(8,128)S(1)} %get-tuple-element.19.base), custom_call_target="tpu_custom_call" | custom-call | flops 58720256 | bytes 3670016 | tf_op jit(solution)/shard_map/fit_theirs/pallas_call | solution.py:231
  47.1 0.5 collective-permute-start.6
  47.6 0.8 %collective-permute-start.5 = (f32[16,448]{1,0:T(8,128)S(1)}, f32[16,448]{1,0:T(8,128)S(1)}, u32[]{:S(2)}, u32[]{:S(2)}) collective-permute-start(f32[16,448]{1,0:T(8,128)S(1)} %fit_theirs.1), channel_id=1, source_target_pairs={{0,192},{64,0},{128,64},{192,128},{1,193},{65,1},{129,65},{193,129... | collective-permute-start | bytes 86024 | tf_op jit(solution)/shard_map/ppermute | solution.py:243
  48.4 2.4 %collective-permute-start.4 = (f32[16,448]{1,0:T(8,128)S(1)}, f32[16,448]{1,0:T(8,128)S(1)}, u32[]{:S(2)}, u32[]{:S(2)}) collective-permute-start(f32[16,448]{1,0:T(8,128)S(1)} %fit_theirs.1), channel_id=1, source_target_pairs={{0,64},{64,128},{128,192},{192,0},{1,65},{65,129},{129,193},{193,1... | collective-permute-start | bytes 86024 | tf_op jit(solution)/shard_map/ppermute | solution.py:243
  50.9 0.2 collective-permute-start.3
  51.0 0.0 collective-permute-done.6
  51.1 0.2 fusion.1
  51.2 1.5 %collective-permute-done.5 = f32[16,448]{1,0:T(8,128)S(1)} collective-permute-done((f32[16,448]{1,0:T(8,128)S(1)}, f32[16,448]{1,0:T(8,128)S(1)}, u32[]{:S(2)}, u32[]{:S(2)}) %collective-permute-start.5) | collective-permute-done | bytes 28704 | tf_op jit(solution)/shard_map/ppermute | solution.py:243
  52.7 0.0 collective-permute-done.4
  52.7 3.5 %collective-permute-done.3 = f32[16,448]{1,0:T(8,128)S(1)} collective-permute-done((f32[16,448]{1,0:T(8,128)S(1)}, f32[16,448]{1,0:T(8,128)S(1)}, u32[]{:S(2)}, u32[]{:S(2)}) %collective-permute-start.3) | collective-permute-done | bytes 28704 | tf_op jit(solution)/shard_map/ppermute | solution.py:243
  56.3 0.6 %fusion.8 = (f32[8,448]{1,0:T(8,128)}, f32[8,448]{1,0:T(8,128)}) fusion(f32[16,448]{1,0:T(8,128)S(1)} %fusion.1, f32[16,448]{1,0:T(8,128)S(1)} %add_multiply_fusion, bf16[16,448]{1,0:T(8,128)(2,1)S(1)} %get-tuple-element.13.stacked), kind=kLoop, calls=%fused_computation.14 | loop fusion | flops 46592 | bytes 100352 | tf_op jit(solution)/shard_map/add | solution.py:263
  (4 shorter events, 0.0 us)
Async XLA Ops:
  3.0 2.4 %collective-permute-start = (f32[33,16,128]{2,1,0:T(8,128)S(1)}, f32[33,16,128]{2,1,0:T(8,128)S(1)}, u32[]{:S(2)}, u32[]{:S(2)}) collective-permute-start(f32[33,16,128]{2,1,0:T(8,128)S(1)} %get-tuple-element.15), channel_id=1, source_target_pairs={{0,1},{1,0},{2,3},{3,2},{4,5},{5,4},{6,7},{7,6},{8,9},{9,8},{10,11... | collective-permute-start | bytes 811016 | tf_op jit(solution)/shard_map/ppermute | solution.py:184
  6.2 22.4 %all-to-all-start = ((bf16[32,16,128]{2,1,0:T(8,128)(2,1)}), bf16[32,16,128]{2,1,0:T(8,128)(2,1)S(1)}, u32[]{:S(2)}, u32[]{:S(2)}) async-start(bf16[32,16,128]{2,1,0:T(8,128)(2,1)} %fusion), calls=%async_computation | async-start | bytes 262144 | tf_op jit(solution)/shard_map/all_to_all | solution.py:202
  17.7 8.3 %collective-permute-start.1 = (f32[16,64]{1,0:T(8,128)S(1)}, f32[16,64]{1,0:T(8,128)S(1)}, u32[]{:S(2)}, u32[]{:S(2)}) collective-permute-start(f32[16,64]{1,0:T(8,128)S(1)} %fusion.9), channel_id=1, source_target_pairs={{0,2},{2,4},{4,6},{6,8},{8,10},{10,12},{12,14},{14,16},{16,18},{18... | collective-permute-start | bytes 12296 | tf_op jit(solution)/shard_map/ppermute | solution.py:201
  42.7 3.4 %collective-permute-start.2 = (bf16[32,16,128]{2,1,0:T(8,128)(2,1)S(1)}, bf16[32,16,128]{2,1,0:T(8,128)(2,1)S(1)}, u32[]{:S(2)}, u32[]{:S(2)}) collective-permute-start(bf16[32,16,128]{2,1,0:T(8,128)(2,1)S(1)} %all_to_all.10.weighted), channel_id=1, source_target_pairs={{0,1},{1,0},{2,3},{3,2},{4,5},{5,4},{6,7},{7,6},{8,9},{9,8},{10,11... | collective-permute-start | bytes 393224 | tf_op jit(solution)/shard_map/ppermute | solution.py:213
  47.1 4.0 %collective-permute-start.6 = (f32[16,64]{1,0:T(8,128)S(1)}, f32[16,64]{1,0:T(8,128)S(1)}, u32[]{:S(2)}, u32[]{:S(2)}) collective-permute-start(f32[16,64]{1,0:T(8,128)S(1)} %collective-permute-done.1), channel_id=1, source_target_pairs={{0,1},{1,0},{2,3},{3,2},{4,5},{5,4},{6,7},{7,6},{8,9},{9,8},{10,11... | collective-permute-start | bytes 12296 | tf_op jit(solution)/shard_map/ppermute | solution.py:249
  47.6 5.1 %collective-permute-start.5 = (f32[16,448]{1,0:T(8,128)S(1)}, f32[16,448]{1,0:T(8,128)S(1)}, u32[]{:S(2)}, u32[]{:S(2)}) collective-permute-start(f32[16,448]{1,0:T(8,128)S(1)} %fit_theirs.1), channel_id=1, source_target_pairs={{0,192},{64,0},{128,64},{192,128},{1,193},{65,1},{129,65},{193,129... | collective-permute-start | bytes 86024 | tf_op jit(solution)/shard_map/ppermute | solution.py:243
  48.4 4.3 %collective-permute-start.4 = (f32[16,448]{1,0:T(8,128)S(1)}, f32[16,448]{1,0:T(8,128)S(1)}, u32[]{:S(2)}, u32[]{:S(2)}) collective-permute-start(f32[16,448]{1,0:T(8,128)S(1)} %fit_theirs.1), channel_id=1, source_target_pairs={{0,64},{64,128},{128,192},{192,0},{1,65},{65,129},{129,193},{193,1... | collective-permute-start | bytes 86024 | tf_op jit(solution)/shard_map/ppermute | solution.py:243
  50.9 5.4 %collective-permute-start.3 = (f32[16,448]{1,0:T(8,128)S(1)}, f32[16,448]{1,0:T(8,128)S(1)}, u32[]{:S(2)}, u32[]{:S(2)}) collective-permute-start(f32[16,448]{1,0:T(8,128)S(1)} %fit_theirs.1), channel_id=1, source_target_pairs={{0,128},{64,192},{128,0},{192,64},{1,129},{65,193},{129,1},{193,65... | collective-permute-start | bytes 86024 | tf_op jit(solution)/shard_map/ppermute | solution.py:243

commit v8 on v5

v8 whole, which is shorter than its diff:
```python
import math

import jax
import jax.numpy as jnp
from jax import lax
from jax.experimental import pallas as pl
from jax.experimental.pallas import tpu as pltpu
from jax.sharding import PartitionSpec as P

GROUPS = 64


DELTA = 0.05
LAMBDA_WEIGHT = 8.0

LANES = 128
PIECES = 4


def transposed_dot(left, right, precision=None):
    return lax.dot_general(
        left,
        right,
        (((1,), (1,)), ((), ())),
        precision=precision,
        preferred_element_type=jnp.float32,
    )


def start_half(a_ref, side, held, sems):
    half = held.shape[1]
    piece = half // PIECES
    copies = []
    for i in range(PIECES):
        start = pl.multiple_of(side * half + i * piece, LANES)
        copy = pltpu.make_async_copy(
            a_ref.at[:, pl.ds(start, piece)], held.at[:, pl.ds(i * piece, piece)], sems.at[i]
        )
        copy.start(priority=1)
        copies.append(copy)
    return copies


def multiply_half(stacked, copies, held, out, meanwhile=None):
    piece = held.shape[1] // PIECES
    per_piece = piece // LANES
    for i, copy in enumerate(copies):
        if i == 1 and meanwhile is not None:
            meanwhile()
        copy.wait()
        product = jnp.dot(
            stacked, held[:, i * piece : (i + 1) * piece], preferred_element_type=jnp.float32
        )
        for k in range(per_piece):
            out[i * per_piece + k] = product[:, k * LANES : (k + 1) * LANES]


def margins_kernel(
    w_ref, d_ref, g_ref, labels_ref, a_ref,
    theirs, mine, stats_mine, stacked_out, ids_out, targets, their_half, my_half,
    w, d, small_sems, their_sems, my_sems,
):
    me = lax.axis_index("feat")
    core, chip = lax.rem(me, 2), lax.div(me, 2)
    share = targets.shape[1]
    spot = pl.multiple_of(core * my_half.shape[1] + chip * share, LANES)
    small = [
        pltpu.make_async_copy(source, target, small_sems.at[i])
        for i, (source, target) in enumerate(
            (
                (w_ref, w),
                (d_ref, d),
                (g_ref, ids_out),
                (labels_ref.at[:, pl.ds(spot, share)], targets),
            )
        )
    ]
    for copy in small:
        copy.start()
    their_copies = start_half(a_ref, 1 - core, their_half, their_sems)
    my_copies = start_half(a_ref, core, my_half, my_sems)
    for copy in small:
        copy.wait()
    stacked = jnp.concatenate([w[...], d[...]], 0)
    stacked_out[...] = stacked

    def sum_groups():
        wide_weights = w[...].astype(jnp.float32)
        products = jnp.concatenate(
            [wide_weights * wide_weights, wide_weights * d[...].astype(jnp.float32)], 0
        )
        high = products.astype(jnp.bfloat16)
        low = (products - high.astype(jnp.float32)).astype(jnp.bfloat16)
        number = lax.broadcasted_iota(jnp.int32, (LANES, ids_out.shape[1]), 0)
        member = (number == ids_out[...]).astype(jnp.float32).astype(jnp.bfloat16)
        sums = transposed_dot(jnp.concatenate([high, low], 0), member)
        rows = stacked.shape[0]
        sums = sums[:rows] + sums[rows:]
        squares, crosses = sums[: rows // 2], sums[rows // 2 :]
        stats_mine[...] = jnp.where(core == 0, squares, crosses)
        theirs[theirs.shape[0] - 1] = jnp.concatenate([jnp.where(core == 0, crosses, squares)] * 2, 0)

    multiply_half(stacked, their_copies, their_half, theirs, sum_groups)
    multiply_half(stacked, my_copies, my_half, mine)


def weighted_kernel(arrived, targets, copies, totals):
    rows = copies.shape[1]
    probes = rows // 2
    summed = jnp.sum(arrived[...].astype(jnp.float32), 0)
    margins, split_stats = summed[:rows], summed[rows:]
    totals[...] = split_stats[:, :GROUPS] + split_stats[:, GROUPS:]
    likely = 1.0 / (1.0 + jnp.exp(-margins[:probes]))
    weighted = jnp.concatenate(
        [likely - targets[...].astype(jnp.float32), likely * (1.0 - likely) * margins[probes:]], 0
    ).astype(jnp.bfloat16)
    copies[...] = jnp.broadcast_to(weighted[None], copies.shape)


def penalty_kernel(totals_mine, totals_theirs, stacked, ids, out):
    core = lax.rem(lax.axis_index("feat"), 2)
    squares = jnp.where(core == 0, totals_mine[...], totals_theirs[...])
    crosses = jnp.where(core == 0, totals_theirs[...], totals_mine[...])
    probes = squares.shape[0]
    number = lax.broadcasted_iota(jnp.int32, (GROUPS, ids.shape[1]), 0)
    member = (number == ids[...]).astype(jnp.float32)
    group_norm = jnp.sqrt(squares + DELTA * DELTA)
    spread = jnp.dot(
        jnp.concatenate([group_norm, crosses], 0),
        member,
        precision=lax.Precision.HIGHEST,
        preferred_element_type=jnp.float32,
    )
    scale, cross = spread[:probes], spread[probes:]
    wide = stacked[...].astype(jnp.float32)
    weights, direction = wide[:probes], wide[probes:]
    out[:probes] = LAMBDA_WEIGHT * weights / scale
    out[probes:] = LAMBDA_WEIGHT * (
        direction / scale - weights * cross / (scale * scale * scale)
    )


def flatten(weighted, flat):
    for k in range(weighted.shape[0]):
        flat[:, k * LANES : (k + 1) * LANES] = weighted[k]


def fit_kernel(weighted, activations, base, out, flat):
    flatten(weighted, flat)
    out[...] = base[...] + transposed_dot(flat[...], activations[...])


def local(activations, labels, probe_weights, direction, group_ids):
    probes, width = probe_weights.shape
    rows = 2 * probes
    tokens = activations.shape[0]
    half = tokens // 2
    planes = lax.axis_size("tok")
    devices = lax.axis_size("feat")
    chips = devices // 2
    share = half // chips
    by_core = [[2 * i + side for i in range(chips)] for side in range(2)]
    swap = [(i, i ^ 1) for i in range(devices)]
    f32, bf16 = jnp.float32, jnp.bfloat16
    vmem, hbm = pl.BlockSpec(memory_space=pltpu.VMEM), pl.BlockSpec(memory_space=pltpu.HBM)
    held = pltpu.VMEM((width, half), bf16)
    half_cost = pl.CostEstimate(
        flops=2 * rows * width * half, bytes_accessed=2 * width * half, transcendentals=0
    )

    def stay(value):
        return pltpu.with_memory_space_constraint(value, pltpu.HBM)

    theirs, mine, stats_mine, stacked, ids, targets, a_theirs, a_mine = pl.pallas_call(
        margins_kernel,
        out_shape=[
            jax.ShapeDtypeStruct((chips + 1, rows, share), f32),
            jax.ShapeDtypeStruct((chips, rows, share), f32),
            jax.ShapeDtypeStruct((probes, LANES), f32),
            jax.ShapeDtypeStruct((rows, width), bf16),
            jax.ShapeDtypeStruct((1, width), jnp.int32),
            jax.ShapeDtypeStruct((probes, share), jnp.int32),
            held,
            held,
        ],
        in_specs=[hbm] * 5,
        out_specs=[vmem] * 8,
        scratch_shapes=[
            pltpu.VMEM((probes, width), bf16),
            pltpu.VMEM((probes, width), bf16),
            pltpu.SemaphoreType.DMA((4,)),
            pltpu.SemaphoreType.DMA((PIECES,)),
            pltpu.SemaphoreType.DMA((PIECES,)),
        ],
        compiler_params=pltpu.CompilerParams(vmem_limit_bytes=16 << 20),
        name="margins",
    )(
        stay(probe_weights),
        stay(direction),
        stay(group_ids[None, :]),
        stay(labels),
        stay(activations.T),
    )
    from_pair = lax.ppermute(theirs, "feat", swap)
    stats = (stats_mine + from_pair[chips, :probes])[:, :GROUPS]
    high = lax.reduce_precision(stats, 8, 7)
    split_stats = jnp.concatenate([high, stats - high], 1).astype(bf16)
    pair_sum = (mine + from_pair[:chips]).astype(bf16)
    outgoing = jnp.concatenate(
        [pair_sum, jnp.broadcast_to(split_stats[None], (chips, probes, 2 * GROUPS))], 1
    )
    arrived = lax.all_to_all(outgoing, "feat", 0, 0, axis_index_groups=by_core)
    copies, totals_mine = pl.pallas_call(
        weighted_kernel,
        out_shape=[
            jax.ShapeDtypeStruct((chips, rows, share), bf16),
            jax.ShapeDtypeStruct((probes, GROUPS), f32),
        ],
        in_specs=[vmem] * 2,
        out_specs=[vmem] * 2,
        compiler_params=pltpu.CompilerParams(vmem_limit_bytes=4 << 20),
        name="weighted",
    )(arrived, targets)
    weighted_mine = lax.all_to_all(copies, "feat", 0, 0, axis_index_groups=by_core)
    weighted_theirs = lax.ppermute(weighted_mine, "feat", swap)


    def fit(name, weighted, activations, base):
        return pl.pallas_call(
            fit_kernel,
            out_shape=jax.ShapeDtypeStruct((rows, width), f32),
            in_specs=[vmem] * 3,
            out_specs=vmem,
            scratch_shapes=[pltpu.VMEM((rows, half), bf16)],
            compiler_params=pltpu.CompilerParams(vmem_limit_bytes=8 << 20),
            cost_estimate=half_cost,
            name=name,
        )(weighted, pltpu.with_memory_space_constraint(activations, pltpu.VMEM), base)

    fit_mine = fit("fit_mine", weighted_mine, a_mine, jnp.zeros((rows, width), f32))
    local_fit = fit("fit_theirs", weighted_theirs, a_theirs, fit_mine)
    local_fit, totals_mine = lax.optimization_barrier((local_fit, totals_mine))
    one, two, three = (
        lax.ppermute(local_fit, "tok", [(i, (i + hop) % planes) for i in range(planes)])
        for hop in (1, 2, 3)
    )
    fitted = (one + three) + (local_fit + two)
    fitted = fitted / math.sqrt(tokens * planes)

    totals_theirs = lax.ppermute(totals_mine, "feat", swap)
    penalty = pl.pallas_call(
        penalty_kernel,
        out_shape=jax.ShapeDtypeStruct((rows, width), f32),
        in_specs=[vmem] * 4,
        out_specs=vmem,
        compiler_params=pltpu.CompilerParams(vmem_limit_bytes=4 << 20),
        name="penalty",
    )(totals_mine, totals_theirs, stacked, ids)
    gradient = fitted[:probes] + penalty[:probes]
    hess_vec = fitted[probes:] + penalty[probes:]
    return (gradient, hess_vec)


def solution(mesh):
    return jax.shard_map(
        local,
        mesh=mesh,
        in_specs=(P("tok", "feat"), P(None, "tok"), P(None, "feat"), P(None, "feat"), P("feat")),
        out_specs=(P(None, "feat"), P(None, "feat")),
        check_vma=False,
    )
```

time: 60.3 us -> 55.5 us (0.920); the launches traced: 60.1 us -> 54.5 us
  blocking collectives: 16.1 us -> 37.3 us
  starting transfers between devices: 19.4 us -> 3.55 us
  waiting for transfers between devices: 13.4 us -> 5.61 us
  Pallas kernels: 9.03 us -> 6.61 us
    all_to_all x0 -> x1, blocking collectives: none -> 22.9 us  [local(): arrived = lax.all_to_all(outgoing, 'feat', 0, 0, axis_index_groups=by_core)]
    all_to_all x1 -> x0, starting transfers between devices: 11.5 us -> none  [local(): arrived = lax.all_to_all(outgoing, 'feat', 0, 0, axis_index_groups=by_core)]
    all_to_all x1 -> x0, waiting for transfers between devices: 5.54 us -> none  [local(): arrived = lax.all_to_all(outgoing, 'feat', 0, 0, axis_index_groups=by_core)]
    ppermute x2 -> x1, starting transfers between devices: 4.29 us -> 0.01 us  [local(): totals_theirs = lax.ppermute(totals_mine, 'feat', swap)]
    ppermute x3, waiting for transfers between devices: 4.94 us -> 2.63 us  [local(): lax.ppermute(local_fit, 'tok', [(i, (i + hop) % planes) for i in range(pl...]
    pallas_call x3 -> x4, Pallas kernels: 4.46 us -> 2.42 us  [the longest x2 2.12 us: fit(): pl.pallas_call(fit_kernel, out_shape=jax.ShapeDtypeStruct((rows, width),...]
    all_to_all x1, blocking collectives: 16.1 us -> 14.3 us  [local(): lax.all_to_all(copies, 'feat', 0, 0, axis_index_groups=by_core)]
    convert_element_type x1, other arithmetic: 0.68 us -> 0.04 us  [local(): pair_sum = (mine + from_pair[:chips]).astype(bf16)]
  transfers between devices with their start and end apart: 8 -> 6, of which waited for: 5 -> 5; matrix products, arithmetic and copies ran while one was open for 0% -> 0% of each run, Pallas kernels for 7% -> 2%
where the time goes in v8:
time: 55.5 us; the launch traced here: 54.5 us
  blocking collectives  37.3 us (67%)
  Pallas kernels  6.61 us (12%)
  waiting for transfers between devices  5.61 us (10%)
  starting transfers between devices  3.55 us (6%)
  other arithmetic  0.78 us (1%)
  between operations  0.69 us (1%)
    all_to_all x1, blocking collectives, local(): arrived = lax.all_to_all(outgoing, 'feat', 0, 0, axis_index_groups=by_core)  22.9 us
    all_to_all x1, blocking collectives, local(): lax.all_to_all(copies, 'feat', 0, 0, axis_index_groups=by_core)  14.3 us
    pallas_call x1, Pallas kernels, local(): pl.pallas_call(margins_kernel, out_shape=[jax.ShapeDtypeStruct((chips + 1...  4.19 us
    ppermute x3, starting transfers between devices, local(): lax.ppermute(local_fit, 'tok', [(i, (i + hop) % planes) for i in range(pl...  3.45 us
    ppermute x3, waiting for transfers between devices, local(): lax.ppermute(local_fit, 'tok', [(i, (i + hop) % planes) for i in range(pl...  2.63 us
    pallas_call x2, Pallas kernels, fit(): pl.pallas_call(fit_kernel, out_shape=jax.ShapeDtypeStruct((rows, width),...  2.12 us
    ppermute x1, waiting for transfers between devices, local(): from_pair = lax.ppermute(theirs, 'feat', swap)  1.53 us
    ppermute x1, waiting for transfers between devices, local(): totals_theirs = lax.ppermute(totals_mine, 'feat', swap)  1.16 us
  transfers between devices with their start and end apart: 6, of which 5 were waited for; matrix products, arithmetic and copies ran while one was open for 0% of the time, Pallas kernels for 2%

profile of v8, /device:TPU:6, one launch (start us, length us, event | category | flops | bytes accessed | tf_op | source)
XLA Modules:
  0.0 54.5 jit_solution(9258859925188466837)
XLA Ops:
  0.6 4.2 %margins.1 = (f32[33,16,128]{2,1,0:T(8,128)S(1)}, f32[32,16,128]{2,1,0:T(8,128)S(1)}, f32[8,128]{1,0:T(8,128)S(1)}, bf16[16,448]{1,0:T(8,128)(2,1)S(1)}, s32[1,4...) custom-call(bf16[8,448]{1,0:T(8,128)(2,1)} %w_ref.1, ...), custom_call_target="tpu_custom_call" | custom-call | tf_op jit(solution)/shard_map/margins/pallas_call | solution.py:174
  4.8 0.1 collective-permute-start
  4.9 1.5 %collective-permute-done = f32[33,16,128]{2,1,0:T(8,128)S(1)} collective-permute-done((f32[33,16,128]{2,1,0:T(8,128)S(1)}, f32[33,16,128]{2,1,0:T(8,128)S(1)}, u32[]{:S(2)}, u32[]{:S(2)}) %collective-permute-start) | collective-permute-done | bytes 270368 | tf_op jit(solution)/shard_map/ppermute | solution.py:204
  6.5 0.1 pad_maximum_fusion.1
  6.6 22.9 %all_to_all.10.arrived = bf16[32,24,128]{2,1,0:T(8,128)(2,1)S(1)} all-to-all(bf16[32,24,128]{2,1,0:T(8,128)(2,1)S(1)} %pad_maximum_fusion), channel_id=1, replica_groups={{0,2,4,6,8,10,12,14,16,18,20,22,24,26,28,30,32,34,36,38,40,42,44,46,48,..., dimensions={0} | all-to-all | bytes 393216 | tf_op jit(solution)/shard_map/all_to_all | solution.py:212
  29.6 0.1 weighted.1
  29.7 14.3 %all_to_all.11.weighted = bf16[32,16,128]{2,1,0:T(8,128)(2,1)S(1)} all-to-all(bf16[32,16,128]{2,1,0:T(8,128)(2,1)S(1)} %get-tuple-element.18), channel_id=1, replica_groups={{0,2,4,6,8,10,12,14,16,18,20,22,24,26,28,30,32,34,36,38,40,42,44,46,48,..., dimensions={0} | all-to-all | bytes 262144 | tf_op jit(solution)/shard_map/all_to_all | solution.py:224
  44.0 0.0 collective-permute-start.1
  44.0 1.1 %fit_mine.1.base = f32[16,448]{1,0:T(8,128)S(1)} custom-call(bf16[32,16,128]{2,1,0:T(8,128)(2,1)S(1)} %all_to_all.11.weighted, bf16[448,4096]{1,0:T(8,128)(2,1)S(1)} %get-tuple-element.20.activations, f32[16,448]{1,0:T(8,128)S(1)} %broadcast_in_dim.14.base), custom_call_target="tpu_custom_call" | custom-call | flops 58720256 | bytes 3670016 | tf_op jit(solution)/shard_map/fit_mine/pallas_call | solution.py:229
  45.1 0.3 collective-permute-done.1.weighted
  45.4 1.1 %fit_theirs.1 = f32[16,448]{1,0:T(8,128)S(1)} custom-call(bf16[32,16,128]{2,1,0:T(8,128)(2,1)S(1)} %collective-permute-done.1.weighted, bf16[448,4096]{1,0:T(8,128)(2,1)S(1)} %get-tuple-element.19.activations, f32[16,448]{1,0:T(8,128)S(1)} %fit_mine.1.base), custom_call_target="tpu_custom_call" | custom-call | flops 58720256 | bytes 3670016 | tf_op jit(solution)/shard_map/fit_theirs/pallas_call | solution.py:229
  46.4 0.5 collective-permute-start.2
  46.9 1.5 %collective-permute-start.3 = (f32[16,448]{1,0:T(8,128)S(1)}, f32[16,448]{1,0:T(8,128)S(1)}, u32[]{:S(2)}, u32[]{:S(2)}) collective-permute-start(f32[16,448]{1,0:T(8,128)S(1)} %fit_theirs.1), channel_id=1, source_target_pairs={{0,192},{64,0},{128,64},{192,128},{1,193},{65,1},{129,65},{193,129... | collective-permute-start | bytes 86024 | tf_op jit(solution)/shard_map/ppermute | solution.py:244
  48.5 1.4 %collective-permute-start.4 = (f32[16,448]{1,0:T(8,128)S(1)}, f32[16,448]{1,0:T(8,128)S(1)}, u32[]{:S(2)}, u32[]{:S(2)}) collective-permute-start(f32[16,448]{1,0:T(8,128)S(1)} %fit_theirs.1), channel_id=1, source_target_pairs={{0,128},{64,192},{128,0},{192,64},{1,129},{65,193},{129,1},{193,65... | collective-permute-start | bytes 86024 | tf_op jit(solution)/shard_map/ppermute | solution.py:244
  49.9 0.0 collective-permute-start.5
  49.9 1.2 %collective-permute-done.5.totals_theirs = f32[8,64]{1,0:T(8,128)S(1)} collective-permute-done((f32[8,64]{1,0:T(8,128)S(1)}, f32[8,64]{1,0:T(8,128)S(1)}, u32[]{:S(2)}, u32[]{:S(2)}) %collective-permute-start.5) | collective-permute-done | bytes 2080 | tf_op jit(solution)/shard_map/ppermute | solution.py:250
  51.0 0.2 penalty.1
  51.3 0.0 collective-permute-done.2
  51.3 0.8 %collective-permute-done.3 = f32[16,448]{1,0:T(8,128)S(1)} collective-permute-done((f32[16,448]{1,0:T(8,128)S(1)}, f32[16,448]{1,0:T(8,128)S(1)}, u32[]{:S(2)}, u32[]{:S(2)}) %collective-permute-start.3) | collective-permute-done | bytes 28704 | tf_op jit(solution)/shard_map/ppermute | solution.py:244
  52.1 1.8 %collective-permute-done.4 = f32[16,448]{1,0:T(8,128)S(1)} collective-permute-done((f32[16,448]{1,0:T(8,128)S(1)}, f32[16,448]{1,0:T(8,128)S(1)}, u32[]{:S(2)}, u32[]{:S(2)}) %collective-permute-start.4) | collective-permute-done | bytes 28704 | tf_op jit(solution)/shard_map/ppermute | solution.py:244
  53.9 0.6 %slice_add_fusion.1 = (f32[8,448]{1,0:T(8,128)}, f32[8,448]{1,0:T(8,128)}) fusion(f32[16,448]{1,0:T(8,128)S(1)} %penalty.1, f32[16,448]{1,0:T(8,128)S(1)} %add_multiply_fusion), kind=kLoop, calls=%fused_computation.4 | loop fusion | flops 7168 | bytes 86016 | tf_op jit(solution)/shard_map/add | solution.py:260
  (7 shorter events, 0.1 us)
Async XLA Ops:
  4.8 1.6 %collective-permute-start = (f32[33,16,128]{2,1,0:T(8,128)S(1)}, f32[33,16,128]{2,1,0:T(8,128)S(1)}, u32[]{:S(2)}, u32[]{:S(2)}) collective-permute-start(f32[33,16,128]{2,1,0:T(8,128)S(1)} %get-tuple-element.15), channel_id=1, source_target_pairs={{0,1},{1,0},{2,3},{3,2},{4,5},{5,4},{6,7},{7,6},{8,9},{9,8},{10,11... | collective-permute-start | bytes 811016 | tf_op jit(solution)/shard_map/ppermute | solution.py:204
  44.0 1.3 %collective-permute-start.1 = (bf16[32,16,128]{2,1,0:T(8,128)(2,1)S(1)}, bf16[32,16,128]{2,1,0:T(8,128)(2,1)S(1)}, u32[]{:S(2)}, u32[]{:S(2)}) collective-permute-start(bf16[32,16,128]{2,1,0:T(8,128)(2,1)S(1)} %all_to_all.11.weighted), channel_id=1, source_target_pairs={{0,1},{1,0},{2,3},{3,2},{4,5},{5,4},{6,7},{7,6},{8,9},{9,8},{10,11... | collective-permute-start | bytes 393224 | tf_op jit(solution)/shard_map/ppermute | solution.py:225
  46.4 4.8 %collective-permute-start.2 = (f32[16,448]{1,0:T(8,128)S(1)}, f32[16,448]{1,0:T(8,128)S(1)}, u32[]{:S(2)}, u32[]{:S(2)}) collective-permute-start(f32[16,448]{1,0:T(8,128)S(1)} %fit_theirs.1), channel_id=1, source_target_pairs={{0,64},{64,128},{128,192},{192,0},{1,65},{65,129},{129,193},{193,1... | collective-permute-start | bytes 86024 | tf_op jit(solution)/shard_map/ppermute | solution.py:244
  46.9 5.1 %collective-permute-start.3 = (f32[16,448]{1,0:T(8,128)S(1)}, f32[16,448]{1,0:T(8,128)S(1)}, u32[]{:S(2)}, u32[]{:S(2)}) collective-permute-start(f32[16,448]{1,0:T(8,128)S(1)} %fit_theirs.1), channel_id=1, source_target_pairs={{0,192},{64,0},{128,64},{192,128},{1,193},{65,1},{129,65},{193,129... | collective-permute-start | bytes 86024 | tf_op jit(solution)/shard_map/ppermute | solution.py:244
  48.5 5.4 %collective-permute-start.4 = (f32[16,448]{1,0:T(8,128)S(1)}, f32[16,448]{1,0:T(8,128)S(1)}, u32[]{:S(2)}, u32[]{:S(2)}) collective-permute-start(f32[16,448]{1,0:T(8,128)S(1)} %fit_theirs.1), channel_id=1, source_target_pairs={{0,128},{64,192},{128,0},{192,64},{1,129},{65,193},{129,1},{193,65... | collective-permute-start | bytes 86024 | tf_op jit(solution)/shard_map/ppermute | solution.py:244
  49.9 1.2 %collective-permute-start.5 = (f32[8,64]{1,0:T(8,128)S(1)}, f32[8,64]{1,0:T(8,128)S(1)}, u32[]{:S(2)}, u32[]{:S(2)}) collective-permute-start(f32[8,64]{1,0:T(8,128)S(1)} %get-tuple-element.23.totals_mine), channel_id=1, source_target_pairs={{0,1},{1,0},{2,3},{3,2},{4,5},{5,4},{6,7},{7,6},{8,9},{9,8},{10,11... | collective-permute-start | bytes 6152 | tf_op jit(solution)/shard_map/ppermute | solution.py:250

commit v9 on v8

--- a/solution.py
+++ b/solution.py
@@ -55,30 +55,19 @@
             out[i * per_piece + k] = product[:, k * LANES : (k + 1) * LANES]
 
 
-def margins_kernel(
-    w_ref, d_ref, g_ref, labels_ref, a_ref,
-    theirs, mine, stats_mine, stacked_out, ids_out, targets, their_half, my_half,
-    w, d, small_sems, their_sems, my_sems,
+def margins_theirs_kernel(
+    w_ref, d_ref, g_ref, a_ref,
+    theirs, stats_mine, stacked_out, ids_out, held,
+    w, d, small_sems, a_sems,
 ):
-    me = lax.axis_index("feat")
-    core, chip = lax.rem(me, 2), lax.div(me, 2)
-    share = targets.shape[1]
-    spot = pl.multiple_of(core * my_half.shape[1] + chip * share, LANES)
+    core = lax.rem(lax.axis_index("feat"), 2)
     small = [
         pltpu.make_async_copy(source, target, small_sems.at[i])
-        for i, (source, target) in enumerate(
-            (
-                (w_ref, w),
-                (d_ref, d),
-                (g_ref, ids_out),
-                (labels_ref.at[:, pl.ds(spot, share)], targets),
-            )
-        )
+        for i, (source, target) in enumerate(((w_ref, w), (d_ref, d), (g_ref, ids_out)))
     ]
     for copy in small:
         copy.start()
-    their_copies = start_half(a_ref, 1 - core, their_half, their_sems)
-    my_copies = start_half(a_ref, core, my_half, my_sems)
+    copies = start_half(a_ref, 1 - core, held, a_sems)
     for copy in small:
         copy.wait()
     stacked = jnp.concatenate([w[...], d[...]], 0)
@@ -100,8 +89,19 @@
         stats_mine[...] = jnp.where(core == 0, squares, crosses)
         theirs[theirs.shape[0] - 1] = jnp.concatenate([jnp.where(core == 0, crosses, squares)] * 2, 0)
 
-    multiply_half(stacked, their_copies, their_half, theirs, sum_groups)
-    multiply_half(stacked, my_copies, my_half, mine)
+    multiply_half(stacked, copies, held, theirs, sum_groups)
+
+
+def margins_mine_kernel(stacked, labels_ref, a_ref, mine, targets, held, labels_sem, a_sems):
+    me = lax.axis_index("feat")
+    core, chip = lax.rem(me, 2), lax.div(me, 2)
+    copies = start_half(a_ref, core, held, a_sems)
+    share = targets.shape[1]
+    spot = pl.multiple_of(core * held.shape[1] + chip * share, LANES)
+    labels_copy = pltpu.make_async_copy(labels_ref.at[:, pl.ds(spot, share)], targets, labels_sem)
+    labels_copy.start()
+    multiply_half(stacked[...], copies, held, mine)
+    labels_copy.wait()
 
 
 def weighted_kernel(arrived, targets, copies, totals):
@@ -171,37 +171,43 @@
     def stay(value):
         return pltpu.with_memory_space_constraint(value, pltpu.HBM)
 
-    theirs, mine, stats_mine, stacked, ids, targets, a_theirs, a_mine = pl.pallas_call(
-        margins_kernel,
+    by_neuron = stay(activations.T)
+    theirs, stats_mine, stacked, ids, a_theirs = pl.pallas_call(
+        margins_theirs_kernel,
         out_shape=[
             jax.ShapeDtypeStruct((chips + 1, rows, share), f32),
-            jax.ShapeDtypeStruct((chips, rows, share), f32),
             jax.ShapeDtypeStruct((probes, LANES), f32),
             jax.ShapeDtypeStruct((rows, width), bf16),
             jax.ShapeDtypeStruct((1, width), jnp.int32),
-            jax.ShapeDtypeStruct((probes, share), jnp.int32),
             held,
-            held,
-        ],
-        in_specs=[hbm] * 5,
-        out_specs=[vmem] * 8,
+        ],
+        in_specs=[hbm] * 4,
+        out_specs=[vmem] * 5,
         scratch_shapes=[
             pltpu.VMEM((probes, width), bf16),
             pltpu.VMEM((probes, width), bf16),
-            pltpu.SemaphoreType.DMA((4,)),
+            pltpu.SemaphoreType.DMA((3,)),
             pltpu.SemaphoreType.DMA((PIECES,)),
-            pltpu.SemaphoreType.DMA((PIECES,)),
         ],
         compiler_params=pltpu.CompilerParams(vmem_limit_bytes=16 << 20),
-        name="margins",
-    )(
-        stay(probe_weights),
-        stay(direction),
-        stay(group_ids[None, :]),
-        stay(labels),
-        stay(activations.T),
-    )
+        cost_estimate=half_cost,
+        name="margins_theirs",
+    )(stay(probe_weights), stay(direction), stay(group_ids[None, :]), by_neuron)
     from_pair = lax.ppermute(theirs, "feat", swap)
+    mine, targets, a_mine = pl.pallas_call(
+        margins_mine_kernel,
+        out_shape=[
+            jax.ShapeDtypeStruct((chips, rows, share), f32),
+            jax.ShapeDtypeStruct((probes, share), jnp.int32),
+            held,
+        ],
+        in_specs=[vmem, hbm, hbm],
+        out_specs=[vmem] * 3,
+        scratch_shapes=[pltpu.SemaphoreType.DMA, pltpu.SemaphoreType.DMA((PIECES,))],
+        compiler_params=pltpu.CompilerParams(vmem_limit_bytes=16 << 20),
+        cost_estimate=half_cost,
+        name="margins_mine",
+    )(stacked, stay(labels), by_neuron)
     stats = (stats_mine + from_pair[chips, :probes])[:, :GROUPS]
     high = lax.reduce_precision(stats, 8, 7)
     split_stats = jnp.concatenate([high, stats - high], 1).astype(bf16)

time: 55.5 us -> 54.7 us (0.986)
  waiting for transfers between devices: 5.61 us -> 4.08 us
    ppermute x1, waiting for transfers between devices: 1.53 us -> 0.01 us  [local(): from_pair = lax.ppermute(theirs, 'feat', swap)]
    pallas_call x1 -> x2, Pallas kernels: 4.19 us -> 4.73 us  [the longest x1 2.41 us: local(): pl.pallas_call(margins_theirs_kernel, out_shape=[jax.ShapeDtypeStruct((ch...]
  transfers between devices with their start and end apart: 6 -> 6, of which waited for: 5 -> 4; matrix products, arithmetic and copies ran while one was open for 0% -> 0% of each run, Pallas kernels for 2% -> 7%
where the time goes in v9:
time: 54.7 us; the launch traced here: 53.7 us
  blocking collectives  37.5 us (69%)
  Pallas kernels  7.15 us (13%)
  waiting for transfers between devices  4.08 us (7%)
  starting transfers between devices  3.55 us (6%)
  other arithmetic  0.77 us (1%)
  between operations  0.72 us (1%)
    all_to_all x1, blocking collectives, local(): arrived = lax.all_to_all(outgoing, 'feat', 0, 0, axis_index_groups=by_core)  23.4 us
    all_to_all x1, blocking collectives, local(): lax.all_to_all(copies, 'feat', 0, 0, axis_index_groups=by_core)  14 us
    ppermute x3, starting transfers between devices, local(): lax.ppermute(local_fit, 'tok', [(i, (i + hop) % planes) for i in range(pl...  3.45 us
    ppermute x3, waiting for transfers between devices, local(): lax.ppermute(local_fit, 'tok', [(i, (i + hop) % planes) for i in range(pl...  2.63 us
    pallas_call x1, Pallas kernels, local(): pl.pallas_call(margins_theirs_kernel, out_shape=[jax.ShapeDtypeStruct((ch...  2.41 us
    pallas_call x1, Pallas kernels, local(): pl.pallas_call(margins_mine_kernel, out_shape=[jax.ShapeDtypeStruct((chip...  2.33 us
    pallas_call x2, Pallas kernels, fit(): pl.pallas_call(fit_kernel, out_shape=jax.ShapeDtypeStruct((rows, width),...  2.12 us
    ppermute x1, waiting for transfers between devices, local(): totals_theirs = lax.ppermute(totals_mine, 'feat', swap)  1.16 us
  transfers between devices with their start and end apart: 6, of which 4 were waited for; matrix products, arithmetic and copies ran while one was open for 0% of the time, Pallas kernels for 7%

profile of v9, /device:TPU:6, one launch (start us, length us, event | category | flops | bytes accessed | tf_op | source)
XLA Modules:
  0.0 53.7 jit_solution(1086815022181776688)
XLA Ops:
  0.6 2.4 %margins_theirs.1 = (f32[33,16,128]{2,1,0:T(8,128)S(1)}, f32[8,128]{1,0:T(8,128)S(1)}, bf16[16,448]{1,0:T(8,128)(2,1)S(1)}, s32[1,448]{1,0:T(1,128)S(1)}, bf16[448,4096]{1,0:T(8,128)(2,1)S(1)}) custom-call(bf16[8,448]{1,0:T(8,128)(2,1)} %w_ref.1, bf16[8,448]{1,0:T(8,128)(2,1)} %d_ref.1, s32[1,448]{1,0:T(1,128)} %bitcast.8, bf16[448,8192]{1,0:T(8,128)(2,1)} %bitcast.6), custom_call_target="tpu_custom_call" | custom-call | flops 58720256 | bytes 3670016 | tf_op jit(solution)/shard_map/margins_theirs/pallas_call | solution.py:175
  3.0 0.1 collective-permute-start
  3.1 2.3 %margins_mine.1 = (f32[32,16,128]{2,1,0:T(8,128)S(1)}, s32[8,128]{1,0:T(8,128)S(1)}, bf16[448,4096]{1,0:T(8,128)(2,1)S(1)}) custom-call(bf16[16,448]{1,0:T(8,128)(2,1)S(1)} %get-tuple-element.14.stacked, s32[8,8192]{1,0:T(8,128)} %labels_ref.1, bf16[448,8192]{1,0:T(8,128)(2,1)} %bitcast.7), custom_call_target="tpu_custom_call" | custom-call | flops 58720256 | bytes 3670016 | tf_op jit(solution)/shard_map/margins_mine/pallas_call | solution.py:197
  5.5 0.0 collective-permute-done
  5.5 0.1 pad_maximum_fusion.1
  5.7 23.4 %all_to_all.10.arrived = bf16[32,24,128]{2,1,0:T(8,128)(2,1)S(1)} all-to-all(bf16[32,24,128]{2,1,0:T(8,128)(2,1)S(1)} %pad_maximum_fusion), channel_id=1, replica_groups={{0,2,4,6,8,10,12,14,16,18,20,22,24,26,28,30,32,34,36,38,40,42,44,46,48,..., dimensions={0} | all-to-all | bytes 393216 | tf_op jit(solution)/shard_map/all_to_all | solution.py:218
  29.1 0.1 weighted.1
  29.2 14.0 %all_to_all.11.weighted = bf16[32,16,128]{2,1,0:T(8,128)(2,1)S(1)} all-to-all(bf16[32,16,128]{2,1,0:T(8,128)(2,1)S(1)} %get-tuple-element.19), channel_id=1, replica_groups={{0,2,4,6,8,10,12,14,16,18,20,22,24,26,28,30,32,34,36,38,40,42,44,46,48,..., dimensions={0} | all-to-all | bytes 262144 | tf_op jit(solution)/shard_map/all_to_all | solution.py:230
  43.2 0.0 collective-permute-start.1
  43.2 1.1 %fit_mine.1.base = f32[16,448]{1,0:T(8,128)S(1)} custom-call(bf16[32,16,128]{2,1,0:T(8,128)(2,1)S(1)} %all_to_all.11.weighted, bf16[448,4096]{1,0:T(8,128)(2,1)S(1)} %get-tuple-element.21.activations, f32[16,448]{1,0:T(8,128)S(1)} %broadcast_in_dim.14.base), custom_call_target="tpu_custom_call" | custom-call | flops 58720256 | bytes 3670016 | tf_op jit(solution)/shard_map/fit_mine/pallas_call | solution.py:235
  44.3 0.3 collective-permute-done.1.weighted
  44.6 1.1 %fit_theirs.1 = f32[16,448]{1,0:T(8,128)S(1)} custom-call(bf16[32,16,128]{2,1,0:T(8,128)(2,1)S(1)} %collective-permute-done.1.weighted, bf16[448,4096]{1,0:T(8,128)(2,1)S(1)} %get-tuple-element.20.activations, f32[16,448]{1,0:T(8,128)S(1)} %fit_mine.1.base), custom_call_target="tpu_custom_call" | custom-call | flops 58720256 | bytes 3670016 | tf_op jit(solution)/shard_map/fit_theirs/pallas_call | solution.py:235
  45.6 0.5 collective-permute-start.2
  46.1 1.5 %collective-permute-start.3 = (f32[16,448]{1,0:T(8,128)S(1)}, f32[16,448]{1,0:T(8,128)S(1)}, u32[]{:S(2)}, u32[]{:S(2)}) collective-permute-start(f32[16,448]{1,0:T(8,128)S(1)} %fit_theirs.1), channel_id=1, source_target_pairs={{0,192},{64,0},{128,64},{192,128},{1,193},{65,1},{129,65},{193,129... | collective-permute-start | bytes 86024 | tf_op jit(solution)/shard_map/ppermute | solution.py:250
  47.7 1.4 %collective-permute-start.4 = (f32[16,448]{1,0:T(8,128)S(1)}, f32[16,448]{1,0:T(8,128)S(1)}, u32[]{:S(2)}, u32[]{:S(2)}) collective-permute-start(f32[16,448]{1,0:T(8,128)S(1)} %fit_theirs.1), channel_id=1, source_target_pairs={{0,128},{64,192},{128,0},{192,64},{1,129},{65,193},{129,1},{193,65... | collective-permute-start | bytes 86024 | tf_op jit(solution)/shard_map/ppermute | solution.py:250
  49.1 0.0 collective-permute-start.5
  49.1 1.2 %collective-permute-done.5.totals_theirs = f32[8,64]{1,0:T(8,128)S(1)} collective-permute-done((f32[8,64]{1,0:T(8,128)S(1)}, f32[8,64]{1,0:T(8,128)S(1)}, u32[]{:S(2)}, u32[]{:S(2)}) %collective-permute-start.5) | collective-permute-done | bytes 2080 | tf_op jit(solution)/shard_map/ppermute | solution.py:256
  50.3 0.2 penalty.1
  50.5 0.0 collective-permute-done.2
  50.5 0.8 %collective-permute-done.3 = f32[16,448]{1,0:T(8,128)S(1)} collective-permute-done((f32[16,448]{1,0:T(8,128)S(1)}, f32[16,448]{1,0:T(8,128)S(1)}, u32[]{:S(2)}, u32[]{:S(2)}) %collective-permute-start.3) | collective-permute-done | bytes 28704 | tf_op jit(solution)/shard_map/ppermute | solution.py:250
  51.3 1.8 %collective-permute-done.4 = f32[16,448]{1,0:T(8,128)S(1)} collective-permute-done((f32[16,448]{1,0:T(8,128)S(1)}, f32[16,448]{1,0:T(8,128)S(1)}, u32[]{:S(2)}, u32[]{:S(2)}) %collective-permute-start.4) | collective-permute-done | bytes 28704 | tf_op jit(solution)/shard_map/ppermute | solution.py:250
  53.1 0.6 %slice_add_fusion.1 = (f32[8,448]{1,0:T(8,128)}, f32[8,448]{1,0:T(8,128)}) fusion(f32[16,448]{1,0:T(8,128)S(1)} %penalty.1, f32[16,448]{1,0:T(8,128)S(1)} %add_multiply_fusion), kind=kLoop, calls=%fused_computation.4 | loop fusion | flops 7168 | bytes 86016 | tf_op jit(solution)/shard_map/add | solution.py:266
  (7 shorter events, 0.1 us)
Async XLA Ops:
  3.0 2.4 %collective-permute-start = (f32[33,16,128]{2,1,0:T(8,128)S(1)}, f32[33,16,128]{2,1,0:T(8,128)S(1)}, u32[]{:S(2)}, u32[]{:S(2)}) collective-permute-start(f32[33,16,128]{2,1,0:T(8,128)S(1)} %get-tuple-element.16), channel_id=1, source_target_pairs={{0,1},{1,0},{2,3},{3,2},{4,5},{5,4},{6,7},{7,6},{8,9},{9,8},{10,11... | collective-permute-start | bytes 811016 | tf_op jit(solution)/shard_map/ppermute | solution.py:196
  43.2 1.3 %collective-permute-start.1 = (bf16[32,16,128]{2,1,0:T(8,128)(2,1)S(1)}, bf16[32,16,128]{2,1,0:T(8,128)(2,1)S(1)}, u32[]{:S(2)}, u32[]{:S(2)}) collective-permute-start(bf16[32,16,128]{2,1,0:T(8,128)(2,1)S(1)} %all_to_all.11.weighted), channel_id=1, source_target_pairs={{0,1},{1,0},{2,3},{3,2},{4,5},{5,4},{6,7},{7,6},{8,9},{9,8},{10,11... | collective-permute-start | bytes 393224 | tf_op jit(solution)/shard_map/ppermute | solution.py:231
  45.6 4.8 %collective-permute-start.2 = (f32[16,448]{1,0:T(8,128)S(1)}, f32[16,448]{1,0:T(8,128)S(1)}, u32[]{:S(2)}, u32[]{:S(2)}) collective-permute-start(f32[16,448]{1,0:T(8,128)S(1)} %fit_theirs.1), channel_id=1, source_target_pairs={{0,64},{64,128},{128,192},{192,0},{1,65},{65,129},{129,193},{193,1... | collective-permute-start | bytes 86024 | tf_op jit(solution)/shard_map/ppermute | solution.py:250
  46.1 5.1 %collective-permute-start.3 = (f32[16,448]{1,0:T(8,128)S(1)}, f32[16,448]{1,0:T(8,128)S(1)}, u32[]{:S(2)}, u32[]{:S(2)}) collective-permute-start(f32[16,448]{1,0:T(8,128)S(1)} %fit_theirs.1), channel_id=1, source_target_pairs={{0,192},{64,0},{128,64},{192,128},{1,193},{65,1},{129,65},{193,129... | collective-permute-start | bytes 86024 | tf_op jit(solution)/shard_map/ppermute | solution.py:250
  47.7 5.4 %collective-permute-start.4 = (f32[16,448]{1,0:T(8,128)S(1)}, f32[16,448]{1,0:T(8,128)S(1)}, u32[]{:S(2)}, u32[]{:S(2)}) collective-permute-start(f32[16,448]{1,0:T(8,128)S(1)} %fit_theirs.1), channel_id=1, source_target_pairs={{0,128},{64,192},{128,0},{192,64},{1,129},{65,193},{129,1},{193,65... | collective-permute-start | bytes 86024 | tf_op jit(solution)/shard_map/ppermute | solution.py:250
  49.1 1.2 %collective-permute-start.5 = (f32[8,64]{1,0:T(8,128)S(1)}, f32[8,64]{1,0:T(8,128)S(1)}, u32[]{:S(2)}, u32[]{:S(2)}) collective-permute-start(f32[8,64]{1,0:T(8,128)S(1)} %get-tuple-element.24.totals_mine), channel_id=1, source_target_pairs={{0,1},{1,0},{2,3},{3,2},{4,5},{5,4},{6,7},{7,6},{8,9},{9,8},{10,11... | collective-permute-start | bytes 6152 | tf_op jit(solution)/shard_map/ppermute | solution.py:256

commit v10 on v9

--- a/solution.py
+++ b/solution.py
@@ -15,6 +15,7 @@
 
 LANES = 128
 PIECES = 4
+AHEAD = 2
 
 
 def transposed_dot(left, right, precision=None):
@@ -27,12 +28,12 @@
     )
 
 
-def start_half(a_ref, side, held, sems):
-    half = held.shape[1]
-    piece = half // PIECES
+def start_copies(a_ref, first, held, sems):
+    pieces = sems.shape[0]
+    piece = held.shape[1] // pieces
     copies = []
-    for i in range(PIECES):
-        start = pl.multiple_of(side * half + i * piece, LANES)
+    for i in range(pieces):
+        start = pl.multiple_of(first + i * piece, LANES)
         copy = pltpu.make_async_copy(
             a_ref.at[:, pl.ds(start, piece)], held.at[:, pl.ds(i * piece, piece)], sems.at[i]
         )
@@ -41,24 +42,25 @@
     return copies
 
 
-def multiply_half(stacked, copies, held, out, meanwhile=None):
-    piece = held.shape[1] // PIECES
+def multiply(stacked, copies, held, out, skip=0, meanwhile=None):
+    piece = held.shape[1] // len(copies)
     per_piece = piece // LANES
     for i, copy in enumerate(copies):
         if i == 1 and meanwhile is not None:
             meanwhile()
-        copy.wait()
+        if copy is not None:
+            copy.wait()
         product = jnp.dot(
             stacked, held[:, i * piece : (i + 1) * piece], preferred_element_type=jnp.float32
         )
         for k in range(per_piece):
-            out[i * per_piece + k] = product[:, k * LANES : (k + 1) * LANES]
+            out[skip + i * per_piece + k] = product[:, k * LANES : (k + 1) * LANES]
 
 
 def margins_theirs_kernel(
     w_ref, d_ref, g_ref, a_ref,
-    theirs, stats_mine, stacked_out, ids_out, held,
-    w, d, small_sems, a_sems,
+    theirs, stats_mine, stacked_out, ids_out, held, ahead,
+    w, d, small_sems, a_sems, ahead_sems,
 ):
     core = lax.rem(lax.axis_index("feat"), 2)
     small = [
@@ -67,7 +69,9 @@
     ]
     for copy in small:
         copy.start()
-    copies = start_half(a_ref, 1 - core, held, a_sems)
+    half = held.shape[1]
+    copies = start_copies(a_ref, (1 - core) * half, held, a_sems)
+    ahead_copies = start_copies(a_ref, core * half, ahead, ahead_sems)
     for copy in small:
         copy.wait()
     stacked = jnp.concatenate([w[...], d[...]], 0)
@@ -89,18 +93,24 @@
         stats_mine[...] = jnp.where(core == 0, squares, crosses)
         theirs[theirs.shape[0] - 1] = jnp.concatenate([jnp.where(core == 0, crosses, squares)] * 2, 0)
 
-    multiply_half(stacked, copies, held, theirs, sum_groups)
-
-
-def margins_mine_kernel(stacked, labels_ref, a_ref, mine, targets, held, labels_sem, a_sems):
+    multiply(stacked, copies, held, theirs, meanwhile=sum_groups)
+    for copy in ahead_copies:
+        copy.wait()
+
+
+def margins_mine_kernel(
+    stacked, labels_ref, a_ref, ahead, mine, targets, held, labels_sem, a_sems
+):
     me = lax.axis_index("feat")
     core, chip = lax.rem(me, 2), lax.div(me, 2)
-    copies = start_half(a_ref, core, held, a_sems)
+    done, rest = ahead.shape[1], held.shape[1]
+    copies = start_copies(a_ref, core * (done + rest) + done, held, a_sems)
     share = targets.shape[1]
-    spot = pl.multiple_of(core * held.shape[1] + chip * share, LANES)
+    spot = pl.multiple_of(core * (done + rest) + chip * share, LANES)
     labels_copy = pltpu.make_async_copy(labels_ref.at[:, pl.ds(spot, share)], targets, labels_sem)
     labels_copy.start()
-    multiply_half(stacked[...], copies, held, mine)
+    multiply(stacked[...], [None] * AHEAD, ahead, mine)
+    multiply(stacked[...], copies, held, mine, done // LANES)
     labels_copy.wait()
 
 
@@ -145,9 +155,16 @@
         flat[:, k * LANES : (k + 1) * LANES] = weighted[k]
 
 
-def fit_kernel(weighted, activations, base, out, flat):
+def fit_kernel(weighted, base, *refs):
+    parts, out, flat = refs[:-2], refs[-2], refs[-1]
     flatten(weighted, flat)
-    out[...] = base[...] + transposed_dot(flat[...], activations[...])
+    total = base[...]
+    start = 0
+    for activations in parts:
+        end = start + activations.shape[1]
+        total = total + transposed_dot(flat[:, start:end], activations[...])
+        start = end
+    out[...] = total
 
 
 def local(activations, labels, probe_weights, direction, group_ids):
@@ -163,16 +180,22 @@
     swap = [(i, i ^ 1) for i in range(devices)]
     f32, bf16 = jnp.float32, jnp.bfloat16
     vmem, hbm = pl.BlockSpec(memory_space=pltpu.VMEM), pl.BlockSpec(memory_space=pltpu.HBM)
-    held = pltpu.VMEM((width, half), bf16)
+    piece = half // PIECES
+    held, ahead, rest = (
+        pltpu.VMEM((width, pieces * piece), bf16) for pieces in (PIECES, AHEAD, PIECES - AHEAD)
+    )
     half_cost = pl.CostEstimate(
         flops=2 * rows * width * half, bytes_accessed=2 * width * half, transcendentals=0
     )
 
+    def in_vmem(value):
+        return pltpu.with_memory_space_constraint(value, pltpu.VMEM)
+
     def stay(value):
         return pltpu.with_memory_space_constraint(value, pltpu.HBM)
 
     by_neuron = stay(activations.T)
-    theirs, stats_mine, stacked, ids, a_theirs = pl.pallas_call(
+    theirs, stats_mine, stacked, ids, a_theirs, a_ahead = pl.pallas_call(
         margins_theirs_kernel,
         out_shape=[
             jax.ShapeDtypeStruct((chips + 1, rows, share), f32),
@@ -180,14 +203,16 @@
             jax.ShapeDtypeStruct((rows, width), bf16),
             jax.ShapeDtypeStruct((1, width), jnp.int32),
             held,
+            ahead,
         ],
         in_specs=[hbm] * 4,
-        out_specs=[vmem] * 5,
+        out_specs=[vmem] * 6,
         scratch_shapes=[
             pltpu.VMEM((probes, width), bf16),
             pltpu.VMEM((probes, width), bf16),
             pltpu.SemaphoreType.DMA((3,)),
             pltpu.SemaphoreType.DMA((PIECES,)),
+            pltpu.SemaphoreType.DMA((AHEAD,)),
         ],
         compiler_params=pltpu.CompilerParams(vmem_limit_bytes=16 << 20),
         cost_estimate=half_cost,
@@ -199,15 +224,15 @@
         out_shape=[
             jax.ShapeDtypeStruct((chips, rows, share), f32),
             jax.ShapeDtypeStruct((probes, share), jnp.int32),
-            held,
+            rest,
         ],
-        in_specs=[vmem, hbm, hbm],
+        in_specs=[vmem, hbm, hbm, vmem],
         out_specs=[vmem] * 3,
-        scratch_shapes=[pltpu.SemaphoreType.DMA, pltpu.SemaphoreType.DMA((PIECES,))],
+        scratch_shapes=[pltpu.SemaphoreType.DMA, pltpu.SemaphoreType.DMA((PIECES - AHEAD,))],
         compiler_params=pltpu.CompilerParams(vmem_limit_bytes=16 << 20),
         cost_estimate=half_cost,
         name="margins_mine",
-    )(stacked, stay(labels), by_neuron)
+    )(stacked, stay(labels), by_neuron, in_vmem(a_ahead))
     stats = (stats_mine + from_pair[chips, :probes])[:, :GROUPS]
     high = lax.reduce_precision(stats, 8, 7)
     split_stats = jnp.concatenate([high, stats - high], 1).astype(bf16)
@@ -231,26 +256,26 @@
     weighted_theirs = lax.ppermute(weighted_mine, "feat", swap)
 
 
-    def fit(name, weighted, activations, base):
+    def fit(name, weighted, base, *parts):
         return pl.pallas_call(
             fit_kernel,
             out_shape=jax.ShapeDtypeStruct((rows, width), f32),
-            in_specs=[vmem] * 3,
+            in_specs=[vmem] * (2 + len(parts)),
             out_specs=vmem,
             scratch_shapes=[pltpu.VMEM((rows, half), bf16)],
             compiler_params=pltpu.CompilerParams(vmem_limit_bytes=8 << 20),
             cost_estimate=half_cost,
             name=name,
-        )(weighted, pltpu.with_memory_space_constraint(activations, pltpu.VMEM), base)
-
-    fit_mine = fit("fit_mine", weighted_mine, a_mine, jnp.zeros((rows, width), f32))
-    local_fit = fit("fit_theirs", weighted_theirs, a_theirs, fit_mine)
+        )(weighted, base, *map(in_vmem, parts))
+
+    fit_mine = fit("fit_mine", weighted_mine, jnp.zeros((rows, width), f32), a_ahead, a_mine)
+    local_fit = fit("fit_theirs", weighted_theirs, fit_mine, a_theirs)
     local_fit, totals_mine = lax.optimization_barrier((local_fit, totals_mine))
     one, two, three = (
         lax.ppermute(local_fit, "tok", [(i, (i + hop) % planes) for i in range(planes)])
         for hop in (1, 2, 3)
     )
-    fitted = (one + three) + (local_fit + two)
+    fitted = (local_fit + two) + (one + three)
     fitted = fitted / math.sqrt(tokens * planes)
 
     totals_theirs = lax.ppermute(totals_mine, "feat", swap)

time: 54.7 us -> 55.1 us (level)
  waiting for transfers between devices: 4.08 us -> 5.19 us
    ppermute x3, waiting for transfers between devices: 2.63 us -> 3.74 us  [local(): lax.ppermute(local_fit, 'tok', [(i, (i + hop) % planes) for i in range(pl...]
    pallas_call x1, Pallas kernels: 2.33 us -> 1.77 us  [local(): pl.pallas_call(margins_mine_kernel, out_shape=[jax.ShapeDtypeStruct((chip...]
  transfers between devices with their start and end apart: 6 -> 6, of which waited for: 4 -> 4; matrix products, arithmetic and copies ran while one was open for 0% -> 0% of each run, Pallas kernels for 7% -> 6%
where the time goes in v10:
time: 55.1 us; the launch traced here: 54.7 us
  blocking collectives  37.5 us (68%)
  Pallas kernels  6.91 us (13%)
  waiting for transfers between devices  5.19 us (9%)
  starting transfers between devices  3.62 us (7%)
  other arithmetic  0.78 us (1%)
  between operations  0.71 us (1%)
    all_to_all x1, blocking collectives, local(): arrived = lax.all_to_all(outgoing, 'feat', 0, 0, axis_index_groups=by_core)  23.3 us
    all_to_all x1, blocking collectives, local(): lax.all_to_all(copies, 'feat', 0, 0, axis_index_groups=by_core)  14.2 us
    ppermute x3, waiting for transfers between devices, local(): lax.ppermute(local_fit, 'tok', [(i, (i + hop) % planes) for i in range(pl...  3.74 us
    ppermute x3, starting transfers between devices, local(): lax.ppermute(local_fit, 'tok', [(i, (i + hop) % planes) for i in range(pl...  3.52 us
    pallas_call x1, Pallas kernels, local(): pl.pallas_call(margins_theirs_kernel, out_shape=[jax.ShapeDtypeStruct((ch...  2.71 us
    pallas_call x2, Pallas kernels, fit(): pl.pallas_call(fit_kernel, out_shape=jax.ShapeDtypeStruct((rows, width),...  2.13 us
    pallas_call x1, Pallas kernels, local(): pl.pallas_call(margins_mine_kernel, out_shape=[jax.ShapeDtypeStruct((chip...  1.77 us
    ppermute x1, waiting for transfers between devices, local(): totals_theirs = lax.ppermute(totals_mine, 'feat', swap)  1.16 us
  transfers between devices with their start and end apart: 6, of which 4 were waited for; matrix products, arithmetic and copies ran while one was open for 0% of the time, Pallas kernels for 6%

profile of v10, /device:TPU:6, one launch (start us, length us, event | category | flops | bytes accessed | tf_op | source)
XLA Modules:
  0.0 54.7 jit_solution(16096757716037860871)
XLA Ops:
  0.6 2.7 %margins_theirs.1 = (f32[33,16,128]{2,1,0:T(8,128)S(1)}, f32[8,128]{1,0:T(8,128)S(1)}, bf16[16,448]{1,0:T(8,128)(2,1)S(1)}, s32[1,448]{1,0:T(1,128)S(1)}, bf16[4...) custom-call(bf16[8,448]{1,0:T(8,128)(2,1)} %w_ref.1, bf16[8,448]{1,0:T(8,128)(2,1)} %d_ref.1, s32[1,448]{1,0:T(1,128)} %bitcast.8, ...), custom_call_target="tpu_custom_call" | custom-call | flops 58720256 | bytes 3670016 | tf_op jit(solution)/shard_map/margins_theirs/pallas_call | solution.py:198
  3.4 0.1 collective-permute-start
  3.5 1.8 %margins_mine.1 = (f32[32,16,128]{2,1,0:T(8,128)S(1)}, s32[8,128]{1,0:T(8,128)S(1)}, bf16[448,2048]{1,0:T(8,128)(2,1)S(1)}) custom-call(bf16[16,448]{1,0:T(8,128)(2,1)S(1)} %get-tuple-element.15.stacked, s32[8,8192]{1,0:T(8,128)} %labels_ref.1, bf16[448,8192]{1,0:T(8,128)(2,1)} %bitcast.7, bf16[448,2048]{1,0:T(8,128)(2,1)S(1)} %get-tuple-element.16.ahead.refs_0_), custom_call_target="tpu_custom_call" | custom-call | flops 58720256 | bytes 3670016 | tf_op jit(solution)/shard_map/margins_mine/pallas_call | solution.py:222
  5.2 0.0 collective-permute-done
  5.3 0.1 pad_maximum_fusion.1
  5.4 23.3 %all_to_all.10.arrived = bf16[32,24,128]{2,1,0:T(8,128)(2,1)S(1)} all-to-all(bf16[32,24,128]{2,1,0:T(8,128)(2,1)S(1)} %pad_maximum_fusion), channel_id=1, replica_groups={{0,2,4,6,8,10,12,14,16,18,20,22,24,26,28,30,32,34,36,38,40,42,44,46,48,..., dimensions={0} | all-to-all | bytes 393216 | tf_op jit(solution)/shard_map/all_to_all | solution.py:243
  28.7 0.1 weighted.1
  28.8 14.2 %all_to_all.11.weighted = bf16[32,16,128]{2,1,0:T(8,128)(2,1)S(1)} all-to-all(bf16[32,16,128]{2,1,0:T(8,128)(2,1)S(1)} %get-tuple-element.21), channel_id=1, replica_groups={{0,2,4,6,8,10,12,14,16,18,20,22,24,26,28,30,32,34,36,38,40,42,44,46,48,..., dimensions={0} | all-to-all | bytes 262144 | tf_op jit(solution)/shard_map/all_to_all | solution.py:255
  43.0 0.0 collective-permute-start.1
  43.0 1.1 %fit_mine.1.base = f32[16,448]{1,0:T(8,128)S(1)} custom-call(bf16[32,16,128]{2,1,0:T(8,128)(2,1)S(1)} %all_to_all.11.weighted, f32[16,448]{1,0:T(8,128)S(1)} %broadcast_in_dim.14.base, bf16[448,2048]{1,0:T(8,128)(2,1)S(1)} %get-tuple-element.16.ahead.refs_0_, bf16[448,2048]{1,0:T(8,128)(2,1)S(1)} %get-tuple-element.22.refs_1_), custom_call_target="tpu_custom_call" | custom-call | flops 58720256 | bytes 3670016 | tf_op jit(solution)/shard_map/fit_mine/pallas_call | solution.py:260
  44.1 0.3 collective-permute-done.1.weighted
  44.3 1.1 %fit_theirs.1 = f32[16,448]{1,0:T(8,128)S(1)} custom-call(bf16[32,16,128]{2,1,0:T(8,128)(2,1)S(1)} %collective-permute-done.1.weighted, f32[16,448]{1,0:T(8,128)S(1)} %fit_mine.1.base, bf16[448,4096]{1,0:T(8,128)(2,1)S(1)} %get-tuple-element.23.refs_0_), custom_call_target="tpu_custom_call" | custom-call | flops 58720256 | bytes 3670016 | tf_op jit(solution)/shard_map/fit_theirs/pallas_call | solution.py:260
  45.4 1.4 %collective-permute-start.2 = (f32[16,448]{1,0:T(8,128)S(1)}, f32[16,448]{1,0:T(8,128)S(1)}, u32[]{:S(2)}, u32[]{:S(2)}) collective-permute-start(f32[16,448]{1,0:T(8,128)S(1)} %fit_theirs.1), channel_id=1, source_target_pairs={{0,128},{64,192},{128,0},{192,64},{1,129},{65,193},{129,1},{193,65... | collective-permute-start | bytes 86024 | tf_op jit(solution)/shard_map/ppermute | solution.py:275
  46.8 2.1 %collective-permute-start.3 = (f32[16,448]{1,0:T(8,128)S(1)}, f32[16,448]{1,0:T(8,128)S(1)}, u32[]{:S(2)}, u32[]{:S(2)}) collective-permute-start(f32[16,448]{1,0:T(8,128)S(1)} %fit_theirs.1), channel_id=1, source_target_pairs={{0,64},{64,128},{128,192},{192,0},{1,65},{65,129},{129,193},{193,1... | collective-permute-start | bytes 86024 | tf_op jit(solution)/shard_map/ppermute | solution.py:275
  48.9 0.0 collective-permute-start.4
  48.9 0.0 collective-permute-start.5
  48.9 1.2 %collective-permute-done.5.totals_theirs = f32[8,64]{1,0:T(8,128)S(1)} collective-permute-done((f32[8,64]{1,0:T(8,128)S(1)}, f32[8,64]{1,0:T(8,128)S(1)}, u32[]{:S(2)}, u32[]{:S(2)}) %collective-permute-start.5) | collective-permute-done | bytes 2080 | tf_op jit(solution)/shard_map/ppermute | solution.py:281
  50.1 0.2 penalty.1
  50.3 0.5 collective-permute-done.2
  50.8 0.0 collective-permute-done.3
  50.8 3.2 %collective-permute-done.4 = f32[16,448]{1,0:T(8,128)S(1)} collective-permute-done((f32[16,448]{1,0:T(8,128)S(1)}, f32[16,448]{1,0:T(8,128)S(1)}, u32[]{:S(2)}, u32[]{:S(2)}) %collective-permute-start.4) | collective-permute-done | bytes 28704 | tf_op jit(solution)/shard_map/ppermute | solution.py:275
  54.1 0.6 %slice_add_fusion.1 = (f32[8,448]{1,0:T(8,128)}, f32[8,448]{1,0:T(8,128)}) fusion(f32[16,448]{1,0:T(8,128)S(1)} %penalty.1, f32[16,448]{1,0:T(8,128)S(1)} %add_multiply_fusion), kind=kLoop, calls=%fused_computation.4 | loop fusion | flops 7168 | bytes 86016 | tf_op jit(solution)/shard_map/add | solution.py:291
  (7 shorter events, 0.1 us)
Async XLA Ops:
  3.4 1.9 %collective-permute-start = (f32[33,16,128]{2,1,0:T(8,128)S(1)}, f32[33,16,128]{2,1,0:T(8,128)S(1)}, u32[]{:S(2)}, u32[]{:S(2)}) collective-permute-start(f32[33,16,128]{2,1,0:T(8,128)S(1)} %get-tuple-element.18), channel_id=1, source_target_pairs={{0,1},{1,0},{2,3},{3,2},{4,5},{5,4},{6,7},{7,6},{8,9},{9,8},{10,11... | collective-permute-start | bytes 811016 | tf_op jit(solution)/shard_map/ppermute | solution.py:221
  43.0 1.3 %collective-permute-start.1 = (bf16[32,16,128]{2,1,0:T(8,128)(2,1)S(1)}, bf16[32,16,128]{2,1,0:T(8,128)(2,1)S(1)}, u32[]{:S(2)}, u32[]{:S(2)}) collective-permute-start(bf16[32,16,128]{2,1,0:T(8,128)(2,1)S(1)} %all_to_all.11.weighted), channel_id=1, source_target_pairs={{0,1},{1,0},{2,3},{3,2},{4,5},{5,4},{6,7},{7,6},{8,9},{9,8},{10,11... | collective-permute-start | bytes 393224 | tf_op jit(solution)/shard_map/ppermute | solution.py:256
  45.4 5.4 %collective-permute-start.2 = (f32[16,448]{1,0:T(8,128)S(1)}, f32[16,448]{1,0:T(8,128)S(1)}, u32[]{:S(2)}, u32[]{:S(2)}) collective-permute-start(f32[16,448]{1,0:T(8,128)S(1)} %fit_theirs.1), channel_id=1, source_target_pairs={{0,128},{64,192},{128,0},{192,64},{1,129},{65,193},{129,1},{193,65... | collective-permute-start | bytes 86024 | tf_op jit(solution)/shard_map/ppermute | solution.py:275
  46.8 4.0 %collective-permute-start.3 = (f32[16,448]{1,0:T(8,128)S(1)}, f32[16,448]{1,0:T(8,128)S(1)}, u32[]{:S(2)}, u32[]{:S(2)}) collective-permute-start(f32[16,448]{1,0:T(8,128)S(1)} %fit_theirs.1), channel_id=1, source_target_pairs={{0,64},{64,128},{128,192},{192,0},{1,65},{65,129},{129,193},{193,1... | collective-permute-start | bytes 86024 | tf_op jit(solution)/shard_map/ppermute | solution.py:275
  48.9 5.1 %collective-permute-start.4 = (f32[16,448]{1,0:T(8,128)S(1)}, f32[16,448]{1,0:T(8,128)S(1)}, u32[]{:S(2)}, u32[]{:S(2)}) collective-permute-start(f32[16,448]{1,0:T(8,128)S(1)} %fit_theirs.1), channel_id=1, source_target_pairs={{0,192},{64,0},{128,64},{192,128},{1,193},{65,1},{129,65},{193,129... | collective-permute-start | bytes 86024 | tf_op jit(solution)/shard_map/ppermute | solution.py:275
  48.9 1.2 %collective-permute-start.5 = (f32[8,64]{1,0:T(8,128)S(1)}, f32[8,64]{1,0:T(8,128)S(1)}, u32[]{:S(2)}, u32[]{:S(2)}) collective-permute-start(f32[8,64]{1,0:T(8,128)S(1)} %get-tuple-element.26.totals_mine), channel_id=1, source_target_pairs={{0,1},{1,0},{2,3},{3,2},{4,5},{5,4},{6,7},{7,6},{8,9},{9,8},{10,11... | collective-permute-start | bytes 6152 | tf_op jit(solution)/shard_map/ppermute | solution.py:281

commit v11 on v10

--- a/solution.py
+++ b/solution.py
@@ -275,7 +275,7 @@
         lax.ppermute(local_fit, "tok", [(i, (i + hop) % planes) for i in range(planes)])
         for hop in (1, 2, 3)
     )
-    fitted = (local_fit + two) + (one + three)
+    fitted = (one + three) + (local_fit + two)
     fitted = fitted / math.sqrt(tokens * planes)
 
     totals_theirs = lax.ppermute(totals_mine, "feat", swap)

time: 55.1 us -> 54.5 us (0.989); the launches traced: 54.7 us -> 53.5 us
  waiting for transfers between devices: 5.19 us -> 4.07 us
    ppermute x3, waiting for transfers between devices: 3.74 us -> 2.63 us  [local(): lax.ppermute(local_fit, 'tok', [(i, (i + hop) % planes) for i in range(pl...]
where the time goes in v11:
time: 54.5 us; the launch traced here: 53.5 us
  blocking collectives  37.5 us (69%)
  Pallas kernels  6.91 us (13%)
  waiting for transfers between devices  4.07 us (7%)
  starting transfers between devices  3.55 us (7%)
  other arithmetic  0.78 us (1%)
  between operations  0.72 us (1%)
    all_to_all x1, blocking collectives, local(): arrived = lax.all_to_all(outgoing, 'feat', 0, 0, axis_index_groups=by_core)  23.3 us
    all_to_all x1, blocking collectives, local(): lax.all_to_all(copies, 'feat', 0, 0, axis_index_groups=by_core)  14.2 us
    ppermute x3, starting transfers between devices, local(): lax.ppermute(local_fit, 'tok', [(i, (i + hop) % planes) for i in range(pl...  3.45 us
    pallas_call x1, Pallas kernels, local(): pl.pallas_call(margins_theirs_kernel, out_shape=[jax.ShapeDtypeStruct((ch...  2.71 us
    ppermute x3, waiting for transfers between devices, local(): lax.ppermute(local_fit, 'tok', [(i, (i + hop) % planes) for i in range(pl...  2.63 us
    pallas_call x2, Pallas kernels, fit(): pl.pallas_call(fit_kernel, out_shape=jax.ShapeDtypeStruct((rows, width),...  2.13 us
    pallas_call x1, Pallas kernels, local(): pl.pallas_call(margins_mine_kernel, out_shape=[jax.ShapeDtypeStruct((chip...  1.77 us
    ppermute x1, waiting for transfers between devices, local(): totals_theirs = lax.ppermute(totals_mine, 'feat', swap)  1.16 us
  transfers between devices with their start and end apart: 6, of which 4 were waited for; matrix products, arithmetic and copies ran while one was open for 0% of the time, Pallas kernels for 6%

profile of v11, /device:TPU:6, one launch (start us, length us, event | category | flops | bytes accessed | tf_op | source)
XLA Modules:
  0.0 53.5 jit_solution(8729711215918267894)
XLA Ops:
  0.6 2.7 %margins_theirs.1 = (f32[33,16,128]{2,1,0:T(8,128)S(1)}, f32[8,128]{1,0:T(8,128)S(1)}, bf16[16,448]{1,0:T(8,128)(2,1)S(1)}, s32[1,448]{1,0:T(1,128)S(1)}, bf16[4...) custom-call(bf16[8,448]{1,0:T(8,128)(2,1)} %w_ref.1, bf16[8,448]{1,0:T(8,128)(2,1)} %d_ref.1, s32[1,448]{1,0:T(1,128)} %bitcast.8, ...), custom_call_target="tpu_custom_call" | custom-call | flops 58720256 | bytes 3670016 | tf_op jit(solution)/shard_map/margins_theirs/pallas_call | solution.py:198
  3.4 0.1 collective-permute-start
  3.5 1.8 %margins_mine.1 = (f32[32,16,128]{2,1,0:T(8,128)S(1)}, s32[8,128]{1,0:T(8,128)S(1)}, bf16[448,2048]{1,0:T(8,128)(2,1)S(1)}) custom-call(bf16[16,448]{1,0:T(8,128)(2,1)S(1)} %get-tuple-element.15.stacked, s32[8,8192]{1,0:T(8,128)} %labels_ref.1, bf16[448,8192]{1,0:T(8,128)(2,1)} %bitcast.7, bf16[448,2048]{1,0:T(8,128)(2,1)S(1)} %get-tuple-element.16.ahead.refs_0_), custom_call_target="tpu_custom_call" | custom-call | flops 58720256 | bytes 3670016 | tf_op jit(solution)/shard_map/margins_mine/pallas_call | solution.py:222
  5.2 0.0 collective-permute-done
  5.3 0.1 pad_maximum_fusion.1
  5.4 23.3 %all_to_all.10.arrived = bf16[32,24,128]{2,1,0:T(8,128)(2,1)S(1)} all-to-all(bf16[32,24,128]{2,1,0:T(8,128)(2,1)S(1)} %pad_maximum_fusion), channel_id=1, replica_groups={{0,2,4,6,8,10,12,14,16,18,20,22,24,26,28,30,32,34,36,38,40,42,44,46,48,..., dimensions={0} | all-to-all | bytes 393216 | tf_op jit(solution)/shard_map/all_to_all | solution.py:243
  28.7 0.1 weighted.1
  28.8 14.2 %all_to_all.11.weighted = bf16[32,16,128]{2,1,0:T(8,128)(2,1)S(1)} all-to-all(bf16[32,16,128]{2,1,0:T(8,128)(2,1)S(1)} %get-tuple-element.21), channel_id=1, replica_groups={{0,2,4,6,8,10,12,14,16,18,20,22,24,26,28,30,32,34,36,38,40,42,44,46,48,..., dimensions={0} | all-to-all | bytes 262144 | tf_op jit(solution)/shard_map/all_to_all | solution.py:255
  43.0 0.0 collective-permute-start.1
  43.0 1.1 %fit_mine.1.base = f32[16,448]{1,0:T(8,128)S(1)} custom-call(bf16[32,16,128]{2,1,0:T(8,128)(2,1)S(1)} %all_to_all.11.weighted, f32[16,448]{1,0:T(8,128)S(1)} %broadcast_in_dim.14.base, bf16[448,2048]{1,0:T(8,128)(2,1)S(1)} %get-tuple-element.16.ahead.refs_0_, bf16[448,2048]{1,0:T(8,128)(2,1)S(1)} %get-tuple-element.22.refs_1_), custom_call_target="tpu_custom_call" | custom-call | flops 58720256 | bytes 3670016 | tf_op jit(solution)/shard_map/fit_mine/pallas_call | solution.py:260
  44.1 0.3 collective-permute-done.1.weighted
  44.3 1.1 %fit_theirs.1 = f32[16,448]{1,0:T(8,128)S(1)} custom-call(bf16[32,16,128]{2,1,0:T(8,128)(2,1)S(1)} %collective-permute-done.1.weighted, f32[16,448]{1,0:T(8,128)S(1)} %fit_mine.1.base, bf16[448,4096]{1,0:T(8,128)(2,1)S(1)} %get-tuple-element.23.refs_0_), custom_call_target="tpu_custom_call" | custom-call | flops 58720256 | bytes 3670016 | tf_op jit(solution)/shard_map/fit_theirs/pallas_call | solution.py:260
  45.4 0.5 collective-permute-start.2
  45.9 1.5 %collective-permute-start.3 = (f32[16,448]{1,0:T(8,128)S(1)}, f32[16,448]{1,0:T(8,128)S(1)}, u32[]{:S(2)}, u32[]{:S(2)}) collective-permute-start(f32[16,448]{1,0:T(8,128)S(1)} %fit_theirs.1), channel_id=1, source_target_pairs={{0,192},{64,0},{128,64},{192,128},{1,193},{65,1},{129,65},{193,129... | collective-permute-start | bytes 86024 | tf_op jit(solution)/shard_map/ppermute | solution.py:275
  47.5 1.4 %collective-permute-start.4 = (f32[16,448]{1,0:T(8,128)S(1)}, f32[16,448]{1,0:T(8,128)S(1)}, u32[]{:S(2)}, u32[]{:S(2)}) collective-permute-start(f32[16,448]{1,0:T(8,128)S(1)} %fit_theirs.1), channel_id=1, source_target_pairs={{0,128},{64,192},{128,0},{192,64},{1,129},{65,193},{129,1},{193,65... | collective-permute-start | bytes 86024 | tf_op jit(solution)/shard_map/ppermute | solution.py:275
  48.9 0.0 collective-permute-start.5
  48.9 1.2 %collective-permute-done.5.totals_theirs = f32[8,64]{1,0:T(8,128)S(1)} collective-permute-done((f32[8,64]{1,0:T(8,128)S(1)}, f32[8,64]{1,0:T(8,128)S(1)}, u32[]{:S(2)}, u32[]{:S(2)}) %collective-permute-start.5) | collective-permute-done | bytes 2080 | tf_op jit(solution)/shard_map/ppermute | solution.py:281
  50.0 0.2 penalty.1
  50.2 0.0 collective-permute-done.2
  50.2 0.8 %collective-permute-done.3 = f32[16,448]{1,0:T(8,128)S(1)} collective-permute-done((f32[16,448]{1,0:T(8,128)S(1)}, f32[16,448]{1,0:T(8,128)S(1)}, u32[]{:S(2)}, u32[]{:S(2)}) %collective-permute-start.3) | collective-permute-done | bytes 28704 | tf_op jit(solution)/shard_map/ppermute | solution.py:275
  51.0 1.8 %collective-permute-done.4 = f32[16,448]{1,0:T(8,128)S(1)} collective-permute-done((f32[16,448]{1,0:T(8,128)S(1)}, f32[16,448]{1,0:T(8,128)S(1)}, u32[]{:S(2)}, u32[]{:S(2)}) %collective-permute-start.4) | collective-permute-done | bytes 28704 | tf_op jit(solution)/shard_map/ppermute | solution.py:275
  52.9 0.6 %slice_add_fusion.1 = (f32[8,448]{1,0:T(8,128)}, f32[8,448]{1,0:T(8,128)}) fusion(f32[16,448]{1,0:T(8,128)S(1)} %penalty.1, f32[16,448]{1,0:T(8,128)S(1)} %add_multiply_fusion), kind=kLoop, calls=%fused_computation.4 | loop fusion | flops 7168 | bytes 86016 | tf_op jit(solution)/shard_map/add | solution.py:291
  (7 shorter events, 0.1 us)
Async XLA Ops:
  3.4 1.9 %collective-permute-start = (f32[33,16,128]{2,1,0:T(8,128)S(1)}, f32[33,16,128]{2,1,0:T(8,128)S(1)}, u32[]{:S(2)}, u32[]{:S(2)}) collective-permute-start(f32[33,16,128]{2,1,0:T(8,128)S(1)} %get-tuple-element.18), channel_id=1, source_target_pairs={{0,1},{1,0},{2,3},{3,2},{4,5},{5,4},{6,7},{7,6},{8,9},{9,8},{10,11... | collective-permute-start | bytes 811016 | tf_op jit(solution)/shard_map/ppermute | solution.py:221
  43.0 1.3 %collective-permute-start.1 = (bf16[32,16,128]{2,1,0:T(8,128)(2,1)S(1)}, bf16[32,16,128]{2,1,0:T(8,128)(2,1)S(1)}, u32[]{:S(2)}, u32[]{:S(2)}) collective-permute-start(bf16[32,16,128]{2,1,0:T(8,128)(2,1)S(1)} %all_to_all.11.weighted), channel_id=1, source_target_pairs={{0,1},{1,0},{2,3},{3,2},{4,5},{5,4},{6,7},{7,6},{8,9},{9,8},{10,11... | collective-permute-start | bytes 393224 | tf_op jit(solution)/shard_map/ppermute | solution.py:256
  45.4 4.8 %collective-permute-start.2 = (f32[16,448]{1,0:T(8,128)S(1)}, f32[16,448]{1,0:T(8,128)S(1)}, u32[]{:S(2)}, u32[]{:S(2)}) collective-permute-start(f32[16,448]{1,0:T(8,128)S(1)} %fit_theirs.1), channel_id=1, source_target_pairs={{0,64},{64,128},{128,192},{192,0},{1,65},{65,129},{129,193},{193,1... | collective-permute-start | bytes 86024 | tf_op jit(solution)/shard_map/ppermute | solution.py:275
  45.9 5.1 %collective-permute-start.3 = (f32[16,448]{1,0:T(8,128)S(1)}, f32[16,448]{1,0:T(8,128)S(1)}, u32[]{:S(2)}, u32[]{:S(2)}) collective-permute-start(f32[16,448]{1,0:T(8,128)S(1)} %fit_theirs.1), channel_id=1, source_target_pairs={{0,192},{64,0},{128,64},{192,128},{1,193},{65,1},{129,65},{193,129... | collective-permute-start | bytes 86024 | tf_op jit(solution)/shard_map/ppermute | solution.py:275
  47.5 5.4 %collective-permute-start.4 = (f32[16,448]{1,0:T(8,128)S(1)}, f32[16,448]{1,0:T(8,128)S(1)}, u32[]{:S(2)}, u32[]{:S(2)}) collective-permute-start(f32[16,448]{1,0:T(8,128)S(1)} %fit_theirs.1), channel_id=1, source_target_pairs={{0,128},{64,192},{128,0},{192,64},{1,129},{65,193},{129,1},{193,65... | collective-permute-start | bytes 86024 | tf_op jit(solution)/shard_map/ppermute | solution.py:275
  48.9 1.2 %collective-permute-start.5 = (f32[8,64]{1,0:T(8,128)S(1)}, f32[8,64]{1,0:T(8,128)S(1)}, u32[]{:S(2)}, u32[]{:S(2)}) collective-permute-start(f32[8,64]{1,0:T(8,128)S(1)} %get-tuple-element.26.totals_mine), channel_id=1, source_target_pairs={{0,1},{1,0},{2,3},{3,2},{4,5},{5,4},{6,7},{7,6},{8,9},{9,8},{10,11... | collective-permute-start | bytes 6152 | tf_op jit(solution)/shard_map/ppermute | solution.py:281
